TPU v7x, 256 devices: a whole 4x4x8 slice. The times are simulated.
256 devices in a mesh: lat: 2 (over x_lo), lon: 128 (over y, x_hi, z, core).
Axes of the slice: x: 4 (x_hi: 2, x_lo: 2; x = x_hi * 2 + x_lo), y: 4, z: 8, core: 2. Of those that a mesh axis runs over, the one named last changes fastest.
Arguments:
- stream: bfloat16 [2, 48, 384, 768], P(None, 'lat', 'lon'), may hold values from -6 to 6
- land: int32 [48, 384], P('lat', 'lon'), may hold values from 0 to 16
- orography: int32 [48, 384], P('lat', 'lon'), may hold values from 0 to 7
- land_vector: float32 [768], replicated, may hold values from -6 to 6
- orography_table: float32 [8, 768], replicated, may hold values from -6 to 6
- gain_one: float32 [768], replicated, may hold values from 0.1 to 1.9
- qkv_one: bfloat16 [768, 2304], replicated, may hold values from -0.21875 to 0.21875
- proj_one: bfloat16 [768, 768], replicated, may hold values from -0.875 to 0.875
- table_one: bfloat16 [4, 12, 6336], P('lat'), may hold values from -4 to 250
- gain_two: float32 [768], replicated, may hold values from 0.1 to 1.9
- qkv_two: bfloat16 [768, 2304], replicated, may hold values from -0.21875 to 0.21875
- proj_two: bfloat16 [768, 768], replicated, may hold values from -0.875 to 0.875
- table_two: bfloat16 [4, 12, 6336], P('lat'), may hold values from -4 to 250
- cotangent: bfloat16 [2, 48, 384, 768], P(None, 'lat', 'lon'), may hold values from -6 to 6
Outputs:
- output: bfloat16 [2, 48, 384, 768], P(None, 'lat', 'lon')
- grad_stream: bfloat16 [2, 48, 384, 768], P(None, 'lat', 'lon')
All inputs are finite; a program needn't handle non-finite values.
Results may differ from a plain program's by a relative error of at most 0.027.
Values may be sent and summed in bfloat16 or wider, within the bound.
No kernel may reach another device: no remote copies, remote signals or barrier semaphores. Data moves between devices by JAX's collectives and lax.ppermute only.
A program may use at most 192 MiB of HBM per device.

v0:
```python
import jax
import jax.numpy as jnp
from jax import lax
from jax.sharding import PartitionSpec as P

WZ = 2
WLAT = 12
WLON = 6
OROG = 8
LAND = 16


epsilon = 1e-05
highest = lax.Precision.HIGHEST


def shifted_2(value, axis, steps):
    count = lax.axis_size(axis)
    pairs = [(source, (source + steps) % count) for source in range(count)]
    return lax.ppermute(value, axis, pairs)


def from_partner(value, axis, bit):
    return lax.ppermute(value, axis, [(i, i ^ 1 << bit) for i in range(lax.axis_size(axis))])


def layer_norm(stream, gain):
    values = stream.astype(jnp.float32)
    average = jnp.mean(values, axis=-1, keepdims=True)
    centred = values - average
    inverse = lax.rsqrt(jnp.mean(centred * centred, axis=-1, keepdims=True) + epsilon)
    normed = centred * inverse
    return ((normed * gain).astype(jnp.bfloat16), normed, inverse)


def norm_back(grad_normed_in, normed, inverse, gain):
    scaled = grad_normed_in * gain
    first = jnp.mean(scaled, axis=-1, keepdims=True)
    second = jnp.mean(scaled * normed, axis=-1, keepdims=True)
    return (scaled - first - normed * second) * inverse


def window_bias_part(table, first, count):
    heads = table.shape[0]
    shaped = table.astype(jnp.float32).reshape(heads, WZ, WZ, WLAT, WLAT, 2 * WLON - 1)
    query_col = first + jnp.arange(count, dtype=jnp.int32)
    key_col = jnp.arange(WLON, dtype=jnp.int32)
    offset = query_col[:, None] - key_col[None, :] + (WLON - 1)
    picked = jnp.take(shaped, offset, axis=5)
    picked = picked.transpose(0, 1, 3, 5, 2, 4, 6)
    return picked.reshape(heads, WZ, WLAT, count, WZ * WLAT * WLON)


def to_heads(array, heads, groups):
    levels, rows, width, chans = array.shape
    depth = chans // (groups * heads)
    windows = rows // WLAT
    shaped = array.reshape(levels, windows, WLAT, width, groups, heads, depth)
    shaped = shaped.transpose(4, 1, 5, 0, 2, 3, 6)
    return shaped.reshape(groups, windows, heads, levels * WLAT * width, depth)


def from_heads(array, levels, width):
    groups, windows, heads, tokens, depth = array.shape
    shaped = array.reshape(groups, windows, heads, levels, WLAT, width, depth)
    shaped = shaped.transpose(3, 1, 4, 5, 0, 2, 6)
    return shaped.reshape(levels, windows * WLAT, width, groups * heads * depth)


def pair_mask(row_start, rows, total_rows, width):
    line = row_start + jnp.arange(rows, dtype=jnp.int32)
    upper = (line >= total_rows - WLAT // 2).reshape(rows // WLAT, 1, WLAT, 1)
    query_side = jnp.broadcast_to(upper, (rows // WLAT, WZ, WLAT, width)).reshape(rows // WLAT, -1)
    key_side = jnp.broadcast_to(upper, (rows // WLAT, WZ, WLAT, 2 * width)).reshape(
        rows // WLAT, -1
    )
    return query_side[:, :, None] == key_side[:, None, :]


def attend(queries, keys, values, bias, allowed):
    scale = queries.shape[-1] ** (-0.5)
    scores = (
        jnp.einsum("whqe,whke->whqk", queries, keys, preferred_element_type=jnp.float32) * scale
        + bias
    )
    if allowed is not None:
        scores = jnp.where(allowed[:, None], scores, -1000000000.0)
    largest = jnp.max(scores, axis=-1, keepdims=True)
    expo = jnp.exp(scores - largest)
    probs = expo / jnp.sum(expo, axis=-1, keepdims=True)
    rounded = probs.astype(jnp.bfloat16)
    mixed = jnp.einsum("whqk,whke->whqe", rounded, values, preferred_element_type=jnp.float32)
    return (mixed.astype(jnp.bfloat16), probs, rounded)


def attend_back(queries, keys, values, probs, rounded, grad_mixed):
    scale = queries.shape[-1] ** (-0.5)
    grad_probs = jnp.einsum(
        "whqe,whke->whqk", grad_mixed, values, preferred_element_type=jnp.float32
    )
    inner = jnp.sum(probs * grad_probs, axis=-1, keepdims=True)
    grad_scores = (probs * (grad_probs - inner) * scale).astype(jnp.bfloat16)
    grad_q = jnp.einsum("whqk,whke->whqe", grad_scores, keys, preferred_element_type=jnp.float32)
    grad_k = jnp.einsum("whqk,whqe->whke", grad_scores, queries, preferred_element_type=jnp.float32)
    grad_v = jnp.einsum("whqk,whqe->whke", rounded, grad_mixed, preferred_element_type=jnp.float32)
    return (grad_q, grad_k.astype(jnp.bfloat16), grad_v.astype(jnp.bfloat16))


def move_columns(field, offset):
    return shifted_2(field, "lon", offset)


def move_rows(field, offset):
    return shifted_2(field, "lat", offset)


def roll_field(field, sign):
    half = WLAT // 2
    rows = field.shape[1]
    if sign < 0:
        moved = move_columns(field, -1)
        strip = move_rows(moved[:, :half], -1)
        return jnp.concatenate([moved[:, half:], strip], axis=1)
    strip = move_rows(field[:, rows - half :], 1)
    settled = jnp.concatenate([strip, field[:, : rows - half]], axis=1)
    return move_columns(settled, 1)


def block_forward(stream, gain, weight_qkv, weight_proj, table, allowed, parity):
    levels, rows, width, dims = stream.shape
    heads = table.shape[1]
    windows = rows // WLAT
    normed_in, normed, inverse = layer_norm(stream, gain)
    projected = jnp.dot(normed_in.reshape(-1, dims), weight_qkv, preferred_element_type=jnp.float32)
    projected = projected.astype(jnp.bfloat16).reshape(levels, rows, width, 3 * dims)
    near = projected[..., dims:]
    far = from_partner(near, "lon", 0)
    pairs = jnp.where(
        parity == 0, jnp.concatenate([near, far], axis=2), jnp.concatenate([far, near], axis=2)
    )
    queries = to_heads(projected[..., :dims], heads, 1)[0]
    key_values = to_heads(pairs, heads, 2)
    keys = key_values[0]
    values = key_values[1]
    first_col = parity * width

    def bias_of(one_table):
        return window_bias_part(one_table, first_col, width)

    bias = jax.vmap(bias_of)(table)
    bias = bias.reshape(windows, heads, -1, bias.shape[-1])
    mixed, probs, rounded = attend(queries, keys, values, bias, allowed)
    mixed_rows = from_heads(mixed[None], levels, width)
    added = jnp.dot(
        mixed_rows.reshape(-1, dims), weight_proj, preferred_element_type=jnp.float32
    ).reshape(stream.shape)
    result = (stream.astype(jnp.float32) + added).astype(jnp.bfloat16)
    return (result, (normed, inverse, queries, keys, values, probs, rounded))


def block_backward(grad, saved, gain, weight_qkv, weight_proj, parity):
    normed, inverse, queries, keys, values, probs, rounded = saved
    levels, rows, width, dims = grad.shape
    heads = queries.shape[1]
    grad_mixed = jnp.dot(grad.reshape(-1, dims), weight_proj.T, preferred_element_type=jnp.float32)
    grad_mixed = grad_mixed.astype(jnp.bfloat16).reshape(grad.shape)
    grad_windows = to_heads(grad_mixed, heads, 1)[0]
    grad_q, grad_k, grad_v = attend_back(queries, keys, values, probs, rounded, grad_windows)
    key_grads = from_heads(jnp.stack([grad_k, grad_v]), levels, 2 * width)
    lower = key_grads[:, :, :width]
    upper = key_grads[:, :, width:]
    own = jnp.where(parity == 0, lower, upper)
    other = jnp.where(parity == 0, upper, lower)
    received = from_partner(other, "lon", 0)
    summed = (own.astype(jnp.float32) + received.astype(jnp.float32)).astype(jnp.bfloat16)
    query_grads = from_heads(grad_q[None], levels, width).astype(jnp.bfloat16)
    grad_qkv = jnp.concatenate([query_grads, summed], axis=-1)
    grad_normed_in = jnp.dot(
        grad_qkv.reshape(-1, 3 * dims), weight_qkv.T, preferred_element_type=jnp.float32
    ).reshape(grad.shape)
    return (grad.astype(jnp.float32) + norm_back(grad_normed_in, normed, inverse, gain)).astype(
        jnp.bfloat16
    )


def body(
    stream,
    land,
    orography,
    land_vector,
    orography_table,
    gain_one,
    qkv_one,
    proj_one,
    table_one,
    gain_two,
    qkv_two,
    proj_two,
    table_two,
    cotangent,
):
    levels, rows, width, dims = stream.shape
    parity = lax.axis_index("lon") % 2
    first_row = lax.axis_index("lat") * rows
    total_rows = rows * lax.axis_size("lat")
    onehot = (orography[..., None] == jnp.arange(OROG, dtype=jnp.int32)).astype(jnp.float32)
    looked = jnp.dot(onehot.reshape(-1, OROG), orography_table, precision=highest).reshape(
        rows, width, dims
    )
    added = (land.astype(jnp.float32) / LAND)[..., None] * land_vector + looked
    embedded = (stream.astype(jnp.float32) + added[None]).astype(jnp.bfloat16)
    shifted = pair_mask(first_row, rows, total_rows, width)
    middle, saved_one = block_forward(
        embedded, gain_one, qkv_one, proj_one, table_one, None, parity
    )
    turned, saved_two = block_forward(
        roll_field(middle, -1), gain_two, qkv_two, proj_two, table_two, shifted, parity
    )
    output = roll_field(turned, 1)
    grad_turned = block_backward(
        roll_field(cotangent, -1), saved_two, gain_two, qkv_two, proj_two, parity
    )
    grad_stream = block_backward(
        roll_field(grad_turned, 1), saved_one, gain_one, qkv_one, proj_one, parity
    )
    return (output, grad_stream)


def solution(mesh):
    placed = (
        P(None, "lat", "lon", None),
        P("lat", "lon"),
        P("lat", "lon"),
        P(),
        P(),
        P(),
        P(),
        P(),
        P("lat", None, None),
        P(),
        P(),
        P(),
        P("lat", None, None),
        P(None, "lat", "lon", None),
    )
    return jax.shard_map(
        body,
        mesh=mesh,
        in_specs=placed,
        out_specs=(P(None, "lat", "lon", None), P(None, "lat", "lon", None)),
        check_vma=False,
    )
```

profile of v0, /device:TPU:1, one launch (start us, length us, event | category | flops | bytes accessed | tf_op | source)
XLA Modules:
  0.0 534.6 jit_solution(7787000375903102028)
XLA Ops:
  8.6 3.7 convolution_convert_fusion.1
  16.5 3.7 collective-permute-start
  20.4 7.1 %reshape.222 = f32[2,12,2,2,12,12,11]{6,5,4,3,2,0,1:T(8,128)} reshape(bf16[2,12,6336]{2,0,1:T(2,128)(2,1)} %param.28) | data formatting | bytes 912384 | tf_op jit(solution)/shard_map/vmap()/reshape | solution.py:45
  27.5 13.5 %copy.121 = f32[2,12,2,2,12,12,11]{5,4,3,2,1,0,6:T(8,128)} copy(f32[2,12,2,2,12,12,11]{6,5,4,3,2,0,1:T(8,128)} %reshape.222) | data formatting | bytes 1216512 | tf_op jit(solution)/shard_map/vmap()/reshape | solution.py:45
  41.0 11.9 %gather_fusion.1 = f32[18,2,12,2,2,12,12]{6,5,4,3,2,1,0:T(8,128)} fusion(f32[2,12,2,2,12,12,11]{5,4,3,2,1,0,6:T(8,128)} %copy.121, s32[1024]{0:T(1024)S(1)} %pad_clamp_fusion), kind=kCustom, calls=%fused_computation.1.clone | custom fusion | bytes 1990728 | tf_op jit(solution)/shard_map/vmap(jit(_take))/gather | solution.py:49
  52.9 16.3 %copy.122 = f32[18,2,12,2,2,12,12]{6,4,5,3,2,1,0:T(2,128)} copy(f32[18,2,12,2,2,12,12]{6,5,4,3,2,1,0:T(8,128)} %gather_fusion.1) | data formatting | bytes 1990656 | tf_op jit(solution)/shard_map/vmap(jit(_take))/gather | solution.py:49
  69.2 7.1 %reshape.219 = f32[2,12,2,2,12,12,11]{6,5,4,3,2,0,1:T(8,128)} reshape(bf16[2,12,6336]{2,0,1:T(2,128)(2,1)} %param.24) | data formatting | bytes 912384 | tf_op jit(solution)/shard_map/vmap()/reshape | solution.py:45
  76.3 13.5 %copy.103 = f32[2,12,2,2,12,12,11]{5,4,3,2,1,0,6:T(8,128)} copy(f32[2,12,2,2,12,12,11]{6,5,4,3,2,0,1:T(8,128)} %reshape.219) | data formatting | bytes 1216512 | tf_op jit(solution)/shard_map/vmap()/reshape | solution.py:45
  89.8 11.9 %gather_fusion = f32[18,2,12,2,2,12,12]{6,5,4,3,2,1,0:T(8,128)} fusion(f32[2,12,2,2,12,12,11]{5,4,3,2,1,0,6:T(8,128)} %copy.103, s32[1024]{0:T(1024)S(1)} %pad_clamp_fusion), kind=kCustom, calls=%fused_computation.clone | custom fusion | bytes 1990728 | tf_op jit(solution)/shard_map/vmap(jit(_take))/gather | solution.py:49
  101.7 15.2 %copy.104 = f32[18,2,12,2,2,12,12]{6,4,5,3,2,1,0:T(2,128)S(1)} copy(f32[18,2,12,2,2,12,12]{6,5,4,3,2,1,0:T(8,128)} %gather_fusion) | data formatting | bytes 1990656 | tf_op jit(solution)/shard_map/vmap(jit(_take))/gather | solution.py:49
  117.0 26.5 %select_bitcast_fusion = (f32[2,12,2,12,3,2,12,6]{6,5,3,2,1,0,7,4:T(2,128)}, f32[2,12,2,12,3,2,12,6]{6,5,3,2,1,0,7,4:T(2,128)}) fusion(f32[3,6,2,12,2,2,12,12]{7,5,6,4,3,2,1,0:T(2,128)} %bitcast.154, pred[3,6]{1,0:T(4,128)(4,1)S(1)} %compare_and_fusion, f32[3,6,2,12,2,2,12,12]{7,5,6,4,3,2,1,0:T(2,128)S(1)} %bitcast.155), kind=kLoop, calls=%fused_computation.6 | loop fusion | flops 497664 | bytes 3981330 | tf_op jit(solution)/shard_map/vmap()/transpose | solution.py:50
  143.4 2.7 concatenate.44
  147.9 24.1 %copy.105 = f32[2,12,2,12,3,2,12,6]{1,0,7,6,5,4,3,2:T(2,128)} copy(f32[2,12,2,12,3,2,12,6]{6,5,3,2,1,0,7,4:T(2,128)} %get-tuple-element.14) | data formatting | bytes 1990656 | tf_op jit(solution)/shard_map/vmap()/transpose | solution.py:50
  172.0 15.4 %copy.106 = f32[2,12,72,144]{3,2,1,0:T(8,128)} copy(f32[2,12,72,144]{1,0,3,2:T(2,128)} %bitcast.152) | data formatting | bytes 1990656 | tf_op jit(solution)/shard_map/reshape;vmap()/reshape | solution.py:151
  195.4 2.7 concatenate.45
  198.1 3.6 fusion.8
  205.0 3.2 copy.102
  214.4 3.1 copy.108
  217.6 6.1 %convolution_convert_fusion.5 = bf16[2,12,72,64]{2,3,1,0:T(8,128)(2,1)} fusion(bf16[2,12,144,64]{2,3,1,0:T(8,128)(2,1)} %copy.108, f32[2,12,72]{2,1,0:T(8,128)S(1)} %get-tuple-element.15, f32[2,12,72,144]{3,2,1,0:T(8,128)} %copy-done.3), kind=kOutput, calls=%fused_computation.39 | convolution fusion | flops 32709456 | bytes 1665792 | tf_op jit(solution)/shard_map/whqk,whke->whqe/dot_general | solution.py:92
  232.3 9.0 %collective-permute-start.6 = (bf16[2,24,3,768]{3,1,2,0:T(8,128)(2,1)}, bf16[2,24,3,768]{3,1,2,0:T(8,128)(2,1)}, u32[]{:S(2)}, u32[]{:S(2)}) collective-permute-start(bf16[2,24,3,768]{3,1,2,0:T(8,128)(2,1)} %param.29), channel_id=1, source_target_pairs={{0,127},{1,0},{2,1},{3,2},{4,3},{5,4},{6,5},{7,6},{8,7},{9,8},{10,... | collective-permute-start | bytes 663560 | tf_op jit(solution)/shard_map/ppermute | solution.py:20
  266.0 4.7 collective-permute-start.3
  271.5 24.1 %copy.123 = f32[2,12,2,12,3,2,12,6]{1,0,7,6,5,4,3,2:T(2,128)} copy(f32[2,12,2,12,3,2,12,6]{6,5,3,2,1,0,7,4:T(2,128)} %get-tuple-element.13) | data formatting | bytes 1990656 | tf_op jit(solution)/shard_map/vmap()/transpose | solution.py:50
  295.6 15.4 %copy.124 = f32[2,12,72,144]{3,2,1,0:T(8,128)} copy(f32[2,12,72,144]{1,0,3,2:T(2,128)} %bitcast.153) | data formatting | bytes 1990656 | tf_op jit(solution)/shard_map/reshape;vmap()/reshape | solution.py:151
  325.2 2.7 concatenate.49
  336.0 2.7 concatenate.50
  338.7 3.4 fusion.9
  345.4 3.1 copy.120
  354.9 3.3 copy.126
  358.2 2.9 fusion.98
  361.1 6.1 %convolution_convert_fusion.3 = bf16[2,12,144,64]{2,3,1,0:T(8,128)(2,1)} fusion(bf16[2,12,72,64]{2,3,1,0:T(8,128)(2,1)} %copy.131, f32[2,12,72]{2,1,0:T(8,128)} %get-tuple-element.17, f32[2,12,72,144]{3,2,1,0:T(8,128)} %copy-done.4), kind=kOutput, calls=%fused_computation.37 | convolution fusion | flops 32820048 | bytes 1665792 | tf_op jit(solution)/shard_map/whqk,whqe->whke/dot_general | solution.py:105
  367.3 13.6 %fusion.31 = bf16[2,12,144,64]{2,3,1,0:T(8,128)(2,1)} fusion(bf16[2,12,72,64]{2,3,1,0:T(8,128)(2,1)} %copy.119, f32[2,12,72,144]{3,2,1,0:T(8,128)} %fusion.98, f32[2,12,72,144]{3,2,1,0:T(8,128)} %get-tuple-element.18, f32[2,12,72]{2,1,0:T(8,128)} %get-tuple-element.17), kind=kOutput, calls=%fused_computation.35 | convolution fusion | flops 33815376 | bytes 2661120 | tf_op jit(solution)/shard_map/whqk,whqe->whke/dot_general | solution.py:104
  380.8 3.2 copy.137
  384.0 3.2 copy.139
  387.2 4.4 maximum_bitcast_fusion
  393.7 4.3 reshape.215
  400.0 13.5 %fusion.37 = bf16[2,12,72,64]{2,3,1,0:T(8,128)(2,1)} fusion(bf16[2,12,144,64]{2,3,1,0:T(8,128)(2,1)} %copy.120, f32[2,12,72,144]{3,2,1,0:T(8,128)} %fusion.98, f32[2,12,72,144]{3,2,1,0:T(8,128)} %get-tuple-element.18, f32[2,12,72]{2,1,0:T(8,128)} %get-tuple-element.17), kind=kOutput, calls=%fused_computation.41 | convolution fusion | flops 33704784 | bytes 2661120 | tf_op jit(solution)/shard_map/whqk,whke->whqe/dot_general | solution.py:103
  426.5 6.1 %convolution_convert_fusion.4 = bf16[2,12,72,64]{2,3,1,0:T(8,128)(2,1)} fusion(bf16[2,12,144,64]{2,3,1,0:T(8,128)(2,1)} %copy.126, f32[2,12,72]{2,1,0:T(8,128)} %get-tuple-element.17, f32[2,12,72,144]{3,2,1,0:T(8,128)} %copy-done.4), kind=kOutput, calls=%fused_computation.38 | convolution fusion | flops 32709456 | bytes 1665792 | tf_op jit(solution)/shard_map/whqk,whke->whqe/dot_general | solution.py:92
  443.0 3.4 collective-permute-done.4
  459.8 2.9 fusion.99
  462.7 6.2 %convolution_convert_fusion.2 = bf16[2,12,144,64]{2,3,1,0:T(8,128)(2,1)} fusion(bf16[2,12,72,64]{2,3,1,0:T(8,128)(2,1)} %copy.143, f32[2,12,72]{2,1,0:T(8,128)S(1)} %copy-done.21, f32[2,12,72,144]{3,2,1,0:T(8,128)} %copy-done.3), kind=kOutput, calls=%fused_computation.36 | convolution fusion | flops 32820048 | bytes 1665792 | tf_op jit(solution)/shard_map/whqk,whqe->whke/dot_general | solution.py:105
  468.8 13.7 %fusion.28 = bf16[2,12,144,64]{2,3,1,0:T(8,128)(2,1)} fusion(bf16[2,12,72,64]{2,3,1,0:T(8,128)(2,1)} %copy.101, f32[2,12,72,144]{3,2,1,0:T(8,128)} %fusion.99, f32[2,12,72,144]{3,2,1,0:T(8,128)} %get-tuple-element.16, f32[2,12,72]{2,1,0:T(8,128)S(1)} %copy-done.21), kind=kOutput, calls=%fused_computation.34 | convolution fusion | flops 33815376 | bytes 2661120 | tf_op jit(solution)/shard_map/whqk,whqe->whke/dot_general | solution.py:104
  482.6 3.2 copy.149
  485.7 3.2 copy.151
  488.9 4.4 maximum_bitcast_fusion.1
  495.5 4.3 reshape.217
  501.7 5.0 collective-permute-start.11
  506.7 13.8 %fusion.34 = bf16[2,12,72,64]{2,3,1,0:T(8,128)(2,1)} fusion(bf16[2,12,144,64]{2,3,1,0:T(8,128)(2,1)} %copy.102, f32[2,12,72,144]{3,2,1,0:T(8,128)} %fusion.99, f32[2,12,72,144]{3,2,1,0:T(8,128)} %get-tuple-element.16, f32[2,12,72]{2,1,0:T(8,128)S(1)} %copy-done.21), kind=kOutput, calls=%fused_computation.40 | convolution fusion | flops 33704784 | bytes 2661120 | tf_op jit(solution)/shard_map/whqk,whke->whqe/dot_general | solution.py:103
  528.1 3.5 fusion.92
  (177 shorter events, 152.8 us)
Async XLA Ops:
  0.6 258.5 %copy-start = (bf16[768,2304]{1,0:T(8,128)(2,1)S(1)}, bf16[768,2304]{1,0:T(8,128)(2,1)}, u32[]{:S(2)}) copy-start(bf16[768,2304]{1,0:T(8,128)(2,1)} %param.26) | copy-start | bytes 10616836
  3.8 0.7 copy-start.5
  3.8 0.7 copy-start.16
  4.5 0.6 copy-start.18
  16.5 178.9 %collective-permute-start = (bf16[2,24,3,1536]{3,1,2,0:T(8,128)(2,1)}, bf16[2,24,3,1536]{3,1,2,0:T(8,128)(2,1)}, u32[]{:S(2)}, u32[]{:S(2)}) collective-permute-start(bf16[2,24,3,1536]{3,1,2,0:T(8,128)(2,1)} %copy.98), channel_id=1, source_target_pairs={{0,1},{1,0},{2,3},{3,2},{4,5},{5,4},{6,7},{7,6},{8,9},{9,8},{10,11... | collective-permute-start | bytes 1327112 | tf_op jit(solution)/shard_map/ppermute | solution.py:24
  210.4 1.8 copy-start.3
  210.4 2.1 copy-start.8
  212.2 5.4 %copy-start.20 = (f32[2,12,72]{2,1,0:T(8,128)}, f32[2,12,72]{2,1,0:T(8,128)S(1)}, u32[]{:S(2)}) copy-start(f32[2,12,72]{2,1,0:T(8,128)S(1)} %get-tuple-element.15) | copy-start | bytes 20740
  232.2 9.1 %collective-permute-start.1 = (bf16[2,24,3,768]{3,1,2,0:T(8,128)(2,1)}, bf16[2,24,3,768]{3,1,2,0:T(8,128)(2,1)}, u32[]{:S(2)}, u32[]{:S(2)}) collective-permute-start(bf16[2,24,3,768]{3,1,2,0:T(8,128)(2,1)} %fusion.46), channel_id=1, source_target_pairs={{0,127},{1,0},{2,1},{3,2},{4,3},{5,4},{6,5},{7,6},{8,7},{9,8},{10,... | collective-permute-start | bytes 663560 | tf_op jit(solution)/shard_map/ppermute | solution.py:20
  232.3 12.3 %collective-permute-start.6 = (bf16[2,24,3,768]{3,1,2,0:T(8,128)(2,1)}, bf16[2,24,3,768]{3,1,2,0:T(8,128)(2,1)}, u32[]{:S(2)}, u32[]{:S(2)}) collective-permute-start(bf16[2,24,3,768]{3,1,2,0:T(8,128)(2,1)} %param.29), channel_id=1, source_target_pairs={{0,127},{1,0},{2,1},{3,2},{4,3},{5,4},{6,5},{7,6},{8,7},{9,8},{10,... | collective-permute-start | bytes 663560 | tf_op jit(solution)/shard_map/ppermute | solution.py:20
  242.9 5.5 %collective-permute-start.2 = (bf16[2,6,3,768]{3,1,2,0:T(8,128)(2,1)}, bf16[2,6,3,768]{3,1,2,0:T(8,128)(2,1)}, u32[]{:S(2)}, u32[]{:S(2)}) collective-permute-start(bf16[2,6,3,768]{3,1,2,0:T(8,128)(2,1)} %slice.93), channel_id=1, source_target_pairs={{0,128},{128,0},{1,129},{129,1},{2,130},{130,2},{3,131},{131,3},{4... | collective-permute-start | bytes 165896 | tf_op jit(solution)/shard_map/ppermute | solution.py:20
  246.2 65.8 %collective-permute-start.7 = (bf16[2,6,3,768]{3,1,2,0:T(8,128)(2,1)}, bf16[2,6,3,768]{3,1,2,0:T(8,128)(2,1)}, u32[]{:S(2)}, u32[]{:S(2)}) collective-permute-start(bf16[2,6,3,768]{3,1,2,0:T(8,128)(2,1)} %slice.101), channel_id=1, source_target_pairs={{0,128},{128,0},{1,129},{129,1},{2,130},{130,2},{3,131},{131,3},{4... | collective-permute-start | bytes 165896 | tf_op jit(solution)/shard_map/ppermute | solution.py:20
  248.3 0.7 copy-start.1
  248.3 10.8 %copy-start.22 = (f32[768]{0:T(1024)S(1)}, f32[768]{0:T(1024)}, u32[]{:S(2)}) copy-start(f32[768]{0:T(1024)} %param.25) | copy-start | bytes 9220
  261.7 9.0 %copy-start.24 = (pred[2,144]{1,0:T(4,128)(4,1)S(1)}, pred[2,144]{1,0:T(4,128)(4,1)}, u32[]{:S(2)}) copy-start(pred[2,144]{1,0:T(4,128)(4,1)} %eq.52) | copy-start | bytes 868
  263.9 6.8 %copy-start.25 = (pred[2,72]{1,0:T(4,128)(4,1)S(1)}, pred[2,72]{1,0:T(4,128)(4,1)}, u32[]{:S(2)}) copy-start(pred[2,72]{1,0:T(4,128)(4,1)} %eq.50) | copy-start | bytes 436
  266.0 70.0 %collective-permute-start.3 = (bf16[2,24,3,1536]{3,1,2,0:T(8,128)(2,1)}, bf16[2,24,3,1536]{3,1,2,0:T(8,128)(2,1)}, u32[]{:S(2)}, u32[]{:S(2)}) collective-permute-start(bf16[2,24,3,1536]{3,1,2,0:T(8,128)(2,1)} %copy.116), channel_id=1, source_target_pairs={{0,1},{1,0},{2,3},{3,2},{4,5},{5,4},{6,7},{7,6},{8,9},{9,8},{10,11... | collective-permute-start | bytes 1327112 | tf_op jit(solution)/shard_map/ppermute | solution.py:24
  311.9 0.7 copy-start.9
  350.9 2.2 copy-start.4
  350.9 2.2 copy-start.7
  400.0 19.8 %collective-permute-start.8 = (bf16[2,24,3,1536]{3,1,2,0:T(8,128)(2,1)}, bf16[2,24,3,1536]{3,1,2,0:T(8,128)(2,1)}, u32[]{:S(2)}, u32[]{:S(2)}) collective-permute-start(bf16[2,24,3,1536]{3,1,2,0:T(8,128)(2,1)} %broadcast_select_fusion.1), channel_id=1, source_target_pairs={{0,1},{1,0},{2,3},{3,2},{4,5},{5,4},{6,7},{7,6},{8,9},{9,8},{10,11... | collective-permute-start | bytes 1327112 | tf_op jit(solution)/shard_map/ppermute | solution.py:24
  419.8 1.5 copy-start.2
  419.8 1.5 copy-start.15
  421.3 2.4 copy-start.10
  424.9 0.7 copy-start.11
  426.2 12.6 %collective-permute-start.9 = (bf16[2,6,3,768]{3,1,2,0:T(8,128)(2,1)}, bf16[2,6,3,768]{3,1,2,0:T(8,128)(2,1)}, u32[]{:S(2)}, u32[]{:S(2)}) collective-permute-start(bf16[2,6,3,768]{3,1,2,0:T(8,128)(2,1)} %slice.104), channel_id=1, source_target_pairs={{0,128},{128,0},{1,129},{129,1},{2,130},{130,2},{3,131},{131,3},{4... | collective-permute-start | bytes 165896 | tf_op jit(solution)/shard_map/ppermute | solution.py:20
  439.9 7.2 %collective-permute-start.10 = (bf16[2,24,3,768]{3,1,2,0:T(8,128)(2,1)S(1)}, bf16[2,24,3,768]{3,1,2,0:T(8,128)(2,1)S(1)}, u32[]{:S(2)}, u32[]{:S(2)}) collective-permute-start(bf16[2,24,3,768]{3,1,2,0:T(8,128)(2,1)S(1)} %pad_maximum_fusion.3), channel_id=1, source_target_pairs={{0,1},{1,2},{2,3},{3,4},{4,5},{5,6},{6,7},{7,8},{8,9},{9,10},{10,1... | collective-permute-start | bytes 663560 | tf_op jit(solution)/shard_map/ppermute | solution.py:20
  441.7 4.6 collective-permute-start.4
  447.1 59.6 %collective-permute-start.5 = (bf16[2,24,3,768]{3,1,2,0:T(8,128)(2,1)}, bf16[2,24,3,768]{3,1,2,0:T(8,128)(2,1)}, u32[]{:S(2)}, u32[]{:S(2)}) collective-permute-start(bf16[2,24,3,768]{3,1,2,0:T(8,128)(2,1)} %pad_maximum_fusion.1), channel_id=1, source_target_pairs={{0,1},{1,2},{2,3},{3,4},{4,5},{5,6},{6,7},{7,8},{8,9},{9,10},{10,1... | collective-permute-start | bytes 663560 | tf_op jit(solution)/shard_map/ppermute | solution.py:20
  447.1 0.7 copy-start.12
  457.6 5.0 copy-start.21
  501.7 24.8 %collective-permute-start.11 = (bf16[2,24,3,1536]{3,1,2,0:T(8,128)(2,1)}, bf16[2,24,3,1536]{3,1,2,0:T(8,128)(2,1)}, u32[]{:S(2)}, u32[]{:S(2)}) collective-permute-start(bf16[2,24,3,1536]{3,1,2,0:T(8,128)(2,1)} %broadcast_select_fusion), channel_id=1, source_target_pairs={{0,1},{1,0},{2,3},{3,2},{4,5},{5,4},{6,7},{7,6},{8,9},{9,8},{10,11... | collective-permute-start | bytes 1327112 | tf_op jit(solution)/shard_map/ppermute | solution.py:24
  522.4 5.6 %copy-start.17 = (f32[2,24,3]{1,2,0:T(4,128)S(1)}, f32[2,24,3]{1,2,0:T(4,128)}, u32[]{:S(2)}) copy-start(f32[2,24,3]{1,2,0:T(4,128)} %copy-done.16) | copy-start | bytes 1732
  522.4 5.6 %copy-start.19 = (f32[2,24,3]{1,2,0:T(4,128)S(1)}, f32[2,24,3]{1,2,0:T(4,128)}, u32[]{:S(2)}) copy-start(f32[2,24,3]{1,2,0:T(4,128)} %copy-done.18) | copy-start | bytes 1732
  522.4 5.6 %copy-start.23 = (f32[768]{0:T(1024)S(1)}, f32[768]{0:T(1024)}, u32[]{:S(2)}) copy-start(f32[768]{0:T(1024)} %param.21) | copy-start | bytes 9220
  526.5 1.5 copy-start.6
  526.5 1.5 copy-start.14
  528.1 3.5 copy-start.13
where the time goes:
time: 542 us; the launch traced here: 535 us
  local copies, waits for them, and re-layouts  327 us (60%)
  matrix products  112 us (21%)
  other arithmetic  64.8 us (12%)
  starting transfers between devices  25.6 us (5%)
    gather x4, local copies, waits for them, and re-layouts, window_bias_part(): picked = jnp.take(shaped, offset, axis=5)  55.3 us
    transpose x2, local copies, waits for them, and re-layouts, window_bias_part(): picked = picked.transpose(0, 1, 3, 5, 2, 4, 6)  48.3 us
    reshape x4, local copies, waits for them, and re-layouts, window_bias_part(): table.astype(jnp.float32).reshape(heads, WZ, WZ, WLAT, WLAT, 2 * WLON - 1)  41.3 us
    reshape x2, local copies, waits for them, and re-layouts, block_forward(): bias = bias.reshape(windows, heads, -1, bias.shape[-1])  30.8 us
    dot_general x2, matrix products, attend_back(): jnp.einsum('whqk,whqe->whke', grad_scores, queries, preferred_element_typ...  27.3 us
    dot_general x2, matrix products, attend_back(): jnp.einsum('whqk,whke->whqe', grad_scores, keys, preferred_element_type=j...  27.3 us
    transpose x1, other arithmetic, window_bias_part(): picked = picked.transpose(0, 1, 3, 5, 2, 4, 6)  26.5 us
    ppermute x4, starting transfers between devices, from_partner(): lax.ppermute(value, axis, [(i, i ^ 1 << bit) for i in range(lax.axis_size...  13.4 us
  transfers between devices with their start and end apart: 12, of which 1 were waited for; matrix products, arithmetic and copies ran while one was open for 69% of the time, Pallas kernels for 0%

commit v1 on v0

v1 whole, which is shorter than its diff:
```python
import jax
import jax.numpy as jnp
from jax import lax
from jax.experimental import pallas as pl
from jax.experimental.pallas import tpu as pltpu
from jax.sharding import PartitionSpec as P

D = 768
HEADS = 12
DEPTH = 64
TOKENS = 144
HALF = 72
QUAD = 36
CHUNK = 132
OROG = 8
LAND = 16
EPS = 1e-05
LIMIT = 40 * 1024 * 1024

f32 = jnp.float32
bf16 = jnp.bfloat16


def iota(shape, dim):
    return lax.broadcasted_iota(jnp.int32, shape, dim)


def div(a, b):
    return lax.div(a, jnp.int32(b))


def rem(a, b):
    return lax.rem(a, jnp.int32(b))


def dot(a, b):
    return jnp.dot(a, b, preferred_element_type=f32)


def dot_t(a, b):
    return lax.dot_general(a, b, (((1,), (1,)), ((), ())), preferred_element_type=f32)


def t_dot(a, b):
    return lax.dot_general(a, b, (((0,), (0,)), ((), ())), preferred_element_type=f32)


def parity():
    return rem(lax.axis_index("lon").astype(jnp.int32), 2)


def split_token(i):
    level = rem(div(i, 18), 2)
    row = rem(div(i, 36), 2) * 6 + rem(i, 6)
    col = div(i, 72) * 3 + rem(div(i, 6), 3)
    return level, row, col


def natural_place(i, band):
    level = rem(div(i, 18), 2)
    row = band * 12 + div(i, 36) * 6 + rem(i, 6)
    col = rem(div(i, 6), 3)
    return level * 72 + col * 24 + row


def pack_kernel(stream, land, orography, land_vector, orog_table, cotangent, keep, send):
    c = parity()
    kinds = iota((OROG, 24), 0)
    added = []
    for w in range(3):
        onehot = (orography[w : w + 1, :] == kinds).astype(f32)
        looked = lax.dot_general(
            onehot,
            orog_table[...],
            (((0,), (0,)), ((), ())),
            precision=lax.Precision.HIGHEST,
            preferred_element_type=f32,
        )
        share = land[w : w + 1, :].astype(f32) * (1.0 / LAND)
        spread = lax.dot_general(
            jnp.concatenate([share, jnp.zeros((7, 24), f32)], axis=0),
            jnp.concatenate([land_vector[...], jnp.zeros((7, D), f32)], axis=0),
            (((0,), (0,)), ((), ())),
            precision=lax.Precision.HIGHEST,
            preferred_element_type=f32,
        )
        added.append(spread + looked)
    added = jnp.concatenate(added + added, axis=0)
    embedded = (stream[...].astype(f32) + added).astype(bf16)
    out = iota((TOKENS, TOKENS), 0)
    own = out < HALF
    place = natural_place(jnp.where(own, out, out - HALF), jnp.where(own, c, 1 - c))
    move = (iota((TOKENS, TOKENS), 1) == place).astype(f32).astype(bf16)
    e = dot(move, embedded)
    g = dot(move, cotangent[...])
    keep[...] = jnp.concatenate([e[:HALF], g[:HALF]], axis=0).astype(bf16)
    send[...] = jnp.concatenate([e[HALF:], g[HALF:]], axis=0).astype(bf16)


def unpack_kernel(keep, received, output, grad):
    c = parity()
    inp = iota((TOKENS, TOKENS), 1)
    own = inp < HALF
    place = natural_place(jnp.where(own, inp, inp - HALF), jnp.where(own, c, 1 - c))
    move = (iota((TOKENS, TOKENS), 0) == place).astype(f32).astype(bf16)
    k = keep[...].astype(f32)
    r = received[...].astype(f32)
    grads = jnp.concatenate([k[:HALF], r[:HALF]], axis=0).astype(bf16)
    turned = jnp.concatenate([k[HALF:], r[HALF:]], axis=0).astype(bf16)
    grad[...] = dot(move, grads).astype(bf16)
    output[...] = dot(move, turned).astype(bf16)


def bias_kernel(table_one, table_two, bias_one, bias_two, first, second):
    place = iota((TOKENS, TOKENS), 1)
    level, row, col = split_token(iota((TOKENS, TOKENS), 0))
    spread = (place == col * 24 + level * 12 + row).astype(f32).astype(bf16)
    level, row, col = split_token(iota((256, TOKENS), 1))
    lane = iota((256, TOKENS), 0)
    lane = jnp.where(lane < 128, lane, jnp.where(lane < 252, -1000, lane - 124))
    base = lane - row * 11 + col - 5
    picks = []
    for i in range(6):
        hit = base == i
        picks.append(
            [(hit & (level == z)).astype(f32).astype(bf16) for z in range(2)]
        )
    last = (lax.axis_index("lat") == 1) & (parity() == 1)
    half_q = rem(div(iota((TOKENS, TOKENS), 0), QUAD), 2)
    half_k = rem(div(iota((TOKENS, TOKENS), 1), QUAD), 2)
    forbidden = (half_q != half_k) & last
    for table, bias, masked in ((table_one, bias_one, False), (table_two, bias_two, True)):
        for za in range(2):
            for zc in range(2):
                into = second if zc else first
                for ra in range(12):
                    at = ((za * 2 + zc) * 12 + ra) * CHUNK
                    for part, skip in enumerate((0, CHUNK - 128)):
                        into[part, pl.ds(za * 12 + ra, HEADS, stride=24), :] = table[
                            :, at + skip : at + skip + 128
                        ].astype(f32)
        low = jnp.concatenate([first[0], first[1]], axis=1).astype(bf16)
        high = jnp.concatenate([second[0], second[1]], axis=1).astype(bf16)
        parts = [dot(low, picks[i][0]) + dot(high, picks[i][1]) for i in range(6)]
        for n in range(HEADS):
            stacked = jnp.concatenate([part[n * 24 : n * 24 + 24] for part in parts], axis=0)
            one = dot(spread, stacked.astype(bf16))
            if masked:
                one = jnp.where(forbidden, -1e9, one)
            bias[n] = one.astype(bf16)


def norm(u):
    average = jnp.mean(u, axis=-1, keepdims=True)
    centred = u - average
    inverse = lax.rsqrt(jnp.mean(centred * centred, axis=-1, keepdims=True) + EPS)
    return centred * inverse, inverse


def lane_masks(value):
    low = iota((1, 2 * DEPTH), 1) < DEPTH
    return (
        jnp.where(low, value, 0.0).astype(bf16),
        jnp.where(low, 0.0, value).astype(bf16),
    )


def attend(qkv, bias, probs, mixed):
    masks = lane_masks(DEPTH ** (-0.5))
    low = iota((TOKENS, 2 * DEPTH), 1) < DEPTH
    for pair in range(HEADS // 2):
        at = pair * 2 * DEPTH
        q2 = qkv[:, at : at + 128]
        k2 = qkv[:, D + at : D + at + 128]
        v2 = qkv[:, 2 * D + at : 2 * D + at + 128]
        mixes = []
        for side in range(2):
            n = pair * 2 + side
            scores = dot_t(q2 * masks[side], k2) + bias[n].astype(f32)
            expo = jnp.exp(scores - jnp.max(scores, axis=-1, keepdims=True))
            p = (expo * (1.0 / jnp.sum(expo, axis=-1, keepdims=True))).astype(bf16)
            probs[n] = p
            mixes.append(dot(p, v2))
        mixed[:, at : at + 128] = jnp.where(low, mixes[0], mixes[1]).astype(bf16)


def attend_back(qkv, probs, grad_mixed, grad_qkv):
    masks = lane_masks(1.0)
    low = iota((TOKENS, 2 * DEPTH), 1) < DEPTH
    for pair in range(HEADS // 2):
        at = pair * 2 * DEPTH
        q2 = qkv[:, at : at + 128]
        k2 = qkv[:, D + at : D + at + 128]
        v2 = qkv[:, 2 * D + at : 2 * D + at + 128]
        g2 = grad_mixed[:, at : at + 128]
        dq, dk, dv = [], [], []
        for side in range(2):
            n = pair * 2 + side
            p = probs[n]
            pf = p.astype(f32)
            dp = dot_t(g2 * masks[side], v2)
            inner = jnp.sum(pf * dp, axis=-1, keepdims=True)
            ds = (pf * (dp - inner) * (DEPTH ** (-0.5))).astype(bf16)
            dq.append(dot(ds, k2))
            dk.append(t_dot(ds, q2))
            dv.append(t_dot(p, g2))
        for block, part in enumerate((dq, dk, dv)):
            grad_qkv[:, block * D + at : block * D + at + 128] = jnp.where(
                low, part[0], part[1]
            ).astype(bf16)


def norm_back(dh, gain, normed, inverse):
    dn = dh * gain
    first = jnp.mean(dn, axis=-1, keepdims=True)
    second = jnp.mean(dn * normed, axis=-1, keepdims=True)
    return (dn - first - normed * second) * inverse


def piece(array, index):
    return array[index * QUAD : (index + 1) * QUAD]


def one_kernel(
    keep, received, gain, weight_qkv, weight_proj, bias,
    stay, left, up, corner, u_out, qkv, probs, mixed,
):
    c = parity()
    k = keep[...].astype(f32)
    r = received[...].astype(f32)
    mine = c == 0
    lead = jnp.where(mine, k, r)
    trail = jnp.where(mine, r, k)
    u = jnp.concatenate([lead[:HALF], trail[:HALF]], axis=0)
    g = jnp.concatenate([lead[HALF:], trail[HALF:]], axis=0)
    u_out[...] = u.astype(bf16)
    normed, _ = norm(u)
    h = (normed * gain[...]).astype(bf16)
    qkv[...] = dot(h, weight_qkv[...]).astype(bf16)
    attend(qkv, bias, probs, mixed)
    middle = u + dot(mixed[...], weight_proj[...])
    for index, out in ((0, corner), (1, left), (2, up), (3, stay)):
        out[...] = jnp.concatenate([piece(middle, index), piece(g, index)], axis=0).astype(bf16)


def two_kernel(
    stay, right, down, corner, gain, weight_qkv, weight_proj, bias,
    back_stay, back_right, back_down, back_corner,
    qkv, probs, mixed, grad_mixed, grad_qkv,
):
    parts = [ref[...].astype(f32) for ref in (stay, down, right, corner)]
    u = jnp.concatenate([part[:QUAD] for part in parts], axis=0)
    g = jnp.concatenate([part[QUAD:] for part in parts], axis=0)
    normed, inverse = norm(u)
    h = (normed * gain[...]).astype(bf16)
    qkv[...] = dot(h, weight_qkv[...]).astype(bf16)
    attend(qkv, bias, probs, mixed)
    turned = u + dot(mixed[...], weight_proj[...])
    grad_mixed[...] = dot_t(g.astype(bf16), weight_proj[...]).astype(bf16)
    attend_back(qkv, probs, grad_mixed, grad_qkv)
    dh = dot_t(grad_qkv[...], weight_qkv[...])
    du = g + norm_back(dh, gain[...], normed, inverse)
    for index, out in ((0, back_stay), (1, back_down), (2, back_right), (3, back_corner)):
        out[...] = jnp.concatenate([piece(du, index), piece(turned, index)], axis=0).astype(bf16)


def three_kernel(
    stay, left, up, corner, u, qkv, probs, gain, weight_qkv, weight_proj,
    keep, send, grad_mixed, grad_qkv,
):
    c = parity()
    parts = [ref[...].astype(f32) for ref in (corner, left, up, stay)]
    g = jnp.concatenate([part[:QUAD] for part in parts], axis=0)
    turned = jnp.concatenate([part[QUAD:] for part in parts], axis=0)
    normed, inverse = norm(u[...].astype(f32))
    grad_mixed[...] = dot_t(g.astype(bf16), weight_proj[...]).astype(bf16)
    attend_back(qkv, probs, grad_mixed, grad_qkv)
    dh = dot_t(grad_qkv[...], weight_qkv[...])
    du = g + norm_back(dh, gain[...], normed, inverse)
    mine = c == 0
    first = jnp.concatenate([du[:HALF], turned[:HALF]], axis=0)
    second = jnp.concatenate([du[HALF:], turned[HALF:]], axis=0)
    keep[...] = jnp.where(mine, first, second).astype(bf16)
    send[...] = jnp.where(mine, second, first).astype(bf16)


def shape(*dims, dtype=bf16):
    return jax.ShapeDtypeStruct(dims, dtype)


def call(kernel, outs, scratch, *args):
    return pl.pallas_call(
        kernel,
        out_shape=outs,
        scratch_shapes=scratch,
        compiler_params=pltpu.CompilerParams(vmem_limit_bytes=LIMIT),
    )(*args)


def moved(value, lat_size, lon_size, dt, dp):
    bands, columns = 2 * lat_size, lon_size // 2

    def device(t, p):
        return t // 2 * lon_size + 2 * p + t % 2

    pairs = [
        (device(t, p), device((t + dt) % bands, (p + dp) % columns))
        for t in range(bands)
        for p in range(columns)
    ]
    return lax.ppermute(value, ("lat", "lon"), pairs)


def body(
    stream, land, orography, land_vector, orography_table,
    gain_one, qkv_one, proj_one, table_one,
    gain_two, qkv_two, proj_two, table_two, cotangent,
):
    lats = lax.axis_size("lat")
    lons = lax.axis_size("lon")
    swap = [(i, i ^ 1) for i in range(lons)]
    c = lax.axis_index("lon") % 2

    def flat(array):
        return array.transpose(0, 2, 1, 3).reshape(TOKENS, D)

    def field(array):
        return array.reshape(2, 3, 24, D).transpose(0, 2, 1, 3)

    tokens = shape(TOKENS, D)
    quad = shape(2 * QUAD, D)
    keep, send = call(
        pack_kernel, (tokens, tokens), [],
        flat(stream), land.T, orography.T, land_vector[None], orography_table, flat(cotangent),
    )
    received = lax.ppermute(send, "lon", swap)
    bias_shape = shape(HEADS, TOKENS, TOKENS)
    bias_one, bias_two = call(
        bias_kernel, (bias_shape, bias_shape), [pltpu.VMEM((2, HEADS * 24, 128), f32)] * 2,
        lax.dynamic_index_in_dim(table_one, c, 0, False),
        lax.dynamic_index_in_dim(table_two, c, 0, False),
    )
    wide = pltpu.VMEM((TOKENS, 3 * D), bf16)
    narrow = pltpu.VMEM((TOKENS, D), bf16)
    square = pltpu.VMEM((HEADS, TOKENS, TOKENS), bf16)
    stay, left, up, corner, u_one, saved_qkv, saved_probs = call(
        one_kernel,
        (quad, quad, quad, quad, tokens, shape(TOKENS, 3 * D), bias_shape),
        [narrow],
        keep, received, gain_one[None], qkv_one, proj_one, bias_one,
    )
    right = moved(left, lats, lons, 0, -1)
    down = moved(up, lats, lons, -1, 0)
    corner = moved(corner, lats, lons, -1, -1)
    stay, right, down, corner = call(
        two_kernel, (quad, quad, quad, quad), [wide, square, narrow, narrow, wide],
        stay, right, down, corner, gain_two[None], qkv_two, proj_two, bias_two,
    )
    left = moved(right, lats, lons, 0, 1)
    up = moved(down, lats, lons, 1, 0)
    corner = moved(corner, lats, lons, 1, 1)
    keep, send = call(
        three_kernel, (tokens, tokens), [narrow, wide],
        stay, left, up, corner, u_one, saved_qkv, saved_probs, gain_one[None], qkv_one, proj_one,
    )
    received = lax.ppermute(send, "lon", swap)
    output, grad = call(unpack_kernel, (tokens, tokens), [], keep, received)
    return field(output), field(grad)


def solution(mesh):
    tokens = P(None, "lat", "lon", None)
    table = P("lat", None, None)
    placed = (
        tokens, P("lat", "lon"), P("lat", "lon"), P(), P(),
        P(), P(), P(), table, P(), P(), P(), table, tokens,
    )
    return jax.shard_map(
        body, mesh=mesh, in_specs=placed, out_specs=(tokens, tokens), check_vma=False
    )
```

time: 542 us -> 64.5 us (0.12); the launches traced: 535 us -> 64.1 us
  local copies, waits for them, and re-layouts: 327 us -> 9.31 us
  matrix products: 112 us -> 0 us
  other arithmetic: 64.8 us -> 0 us
  Pallas kernels: 0 us -> 21.2 us
  waiting for transfers between devices: 3.41 us -> 18 us
  starting transfers between devices: 25.6 us -> 14.9 us
    dot_general x21 -> x0, matrix products: 112 us -> none  [the longest x2 27.3 us: attend_back(): jnp.einsum('whqk,whqe->whke', grad_scores, queries, preferred_element_typ...]
    reshape x15 -> x0, local copies, waits for them, and re-layouts: 94.8 us -> none  [the longest x4 41.3 us: window_bias_part(): table.astype(jnp.float32).reshape(heads, WZ, WZ, WLAT, WLAT, 2 * WLON - 1)]
    transpose x10 -> x0, local copies, waits for them, and re-layouts: 65.8 us -> none  [the longest x2 48.3 us: window_bias_part(): picked = picked.transpose(0, 1, 3, 5, 2, 4, 6)]
    gather x4 -> x0, local copies, waits for them, and re-layouts: 55.3 us -> none  [window_bias_part(): picked = jnp.take(shaped, offset, axis=5)]
    transpose x5 -> x0, other arithmetic: 42.2 us -> none  [the longest x1 26.5 us: window_bias_part(): picked = picked.transpose(0, 1, 3, 5, 2, 4, 6)]
    convert_element_type x15 -> x0, local copies, waits for them, and re-layouts: 32.8 us -> none  [the longest x4 12.6 us: attend_back(): return (grad_q, grad_k.astype(jnp.bfloat16), grad_v.astype(jnp.bfloat16))]
    slice x20 -> x0, local copies, waits for them, and re-layouts: 25.5 us -> none  [the longest x4 6.62 us: block_forward(): keys = key_values[0]]
    pallas_call x0 -> x6, Pallas kernels: none -> 21.2 us  [call(): pl.pallas_call(kernel, out_shape=outs, scratch_shapes=scratch, compiler_p...]
  transfers between devices with their start and end apart: 12 -> 8, of which waited for: 1 -> 6; matrix products, arithmetic and copies ran while one was open for 69% -> 4% of each run, Pallas kernels for 0% -> 3%
where the time goes in v1:
time: 64.5 us; the launch traced here: 64.1 us
  Pallas kernels  21.2 us (33%)
  waiting for transfers between devices  18 us (28%)
  starting transfers between devices  14.9 us (23%)
  local copies, waits for them, and re-layouts  9.31 us (14%)
  between operations  0.77 us (1%)
    pallas_call x6, Pallas kernels, call(): pl.pallas_call(kernel, out_shape=outs, scratch_shapes=scratch, compiler_p...  21.2 us
    ppermute x6, waiting for transfers between devices, moved(): return lax.ppermute(value, ('lat', 'lon'), pairs)  16.6 us
    ppermute x6, starting transfers between devices, moved(): return lax.ppermute(value, ('lat', 'lon'), pairs)  11.4 us
    unnamed x24, local copies, waits for them, and re-layouts  6.05 us
    ppermute x2, starting transfers between devices, body(): received = lax.ppermute(send, 'lon', swap)  3.42 us
    dynamic_slice x1, local copies, waits for them, and re-layouts, body(): lax.dynamic_index_in_dim(table_two, c, 0, False)  1.7 us
    ppermute x2, waiting for transfers between devices, body(): received = lax.ppermute(send, 'lon', swap)  1.47 us
  transfers between devices with their start and end apart: 8, of which 6 were waited for; matrix products, arithmetic and copies ran while one was open for 4% of the time, Pallas kernels for 3%

profile of v1, /device:TPU:1, one launch (start us, length us, event | category | flops | bytes accessed | tf_op | source)
XLA Modules:
  0.0 64.1 jit_solution(2399685379852023296)
XLA Ops:
  0.6 0.0 copy-start.2
  0.6 0.8 %broadcast_in_dim.10.land_vector = f32[1,768]{1,0:T(1,128)S(1)} reshape(f32[768]{0:T(1024)} %param.17) | data formatting | bytes 6144 | tf_op jit(solution)/shard_map/broadcast_in_dim | solution.py:334
  1.4 0.0 copy-start.5
  1.4 0.9 %copy-done.5 = bf16[2,24,3,768]{3,1,2,0:T(8,128)(2,1)S(1)} copy-done((bf16[2,24,3,768]{3,1,2,0:T(8,128)(2,1)S(1)}, bf16[2,24,3,768]{3,1,2,0:T(8,128)(2,1)}, u32[]{:S(2)}) %copy-start.5) | copy-done | bytes 221208
  2.4 0.0 copy-start.6
  2.4 0.9 %copy-done.6 = bf16[2,24,3,768]{3,1,2,0:T(8,128)(2,1)S(1)} copy-done((bf16[2,24,3,768]{3,1,2,0:T(8,128)(2,1)S(1)}, bf16[2,24,3,768]{3,1,2,0:T(8,128)(2,1)}, u32[]{:S(2)}) %copy-start.6) | copy-done | bytes 221208
  3.3 0.0 copy-start.7
  3.3 0.7 %copy-done.7 = f32[8,768]{1,0:T(8,128)S(1)} copy-done((f32[8,768]{1,0:T(8,128)S(1)}, f32[8,768]{1,0:T(8,128)}, u32[]{:S(2)}) %copy-start.7) | copy-done | bytes 24600
  4.0 0.0 copy-start.8
  4.0 0.7 %copy-done.8 = s32[24,3]{0,1:T(4,128)S(1)} copy-done((s32[24,3]{0,1:T(4,128)S(1)}, s32[24,3]{0,1:T(4,128)}, u32[]{:S(2)}) %copy-start.8) | copy-done | bytes 312
  4.7 0.0 copy-start.9
  4.7 0.7 %copy-done.9 = s32[24,3]{0,1:T(4,128)S(1)} copy-done((s32[24,3]{0,1:T(4,128)S(1)}, s32[24,3]{0,1:T(4,128)}, u32[]{:S(2)}) %copy-start.9) | copy-done | bytes 312
  5.4 0.9 %shard_map.149 = (bf16[144,768]{1,0:T(8,128)(2,1)S(1)}, bf16[144,768]{1,0:T(8,128)(2,1)S(1)}) custom-call(bf16[144,768]{1,0:T(8,128)(2,1)S(1)} %bitcast.22, s32[3,24]{1,0:T(4,128)S(1)} %bitcast.24, s32[3,24]{1,0:T(4,128)S(1)} %bitcast.25, f32[1,768]{1,0:T(1,128)S(1)} %broadcast_in_dim.10.land_vector, f32[8,768]{1,0:T(8,128)S(1)} %copy-done.7, ...), custom_call_target="tpu_custom_call" | custom-call | tf_op jit(solution)/shard_map/pallas_call | solution.py:292
  6.3 3.3 %collective-permute-start = (bf16[144,768]{1,0:T(8,128)(2,1)S(1)}, bf16[144,768]{1,0:T(8,128)(2,1)S(1)}, u32[]{:S(2)}, u32[]{:S(2)}) collective-permute-start(bf16[144,768]{1,0:T(8,128)(2,1)S(1)} %get-tuple-element.22), channel_id=1, source_target_pairs={{0,1},{1,0},{2,3},{3,2},{4,5},{5,4},{6,7},{7,6},{8,9},{9,8},{10,11... | collective-permute-start | bytes 663560 | tf_op jit(solution)/shard_map/ppermute | solution.py:336
  9.7 1.7 %constant_dynamic-slice_fusion = (bf16[1,12,6336]{2,0,1:T(2,128)(2,1)S(1)}, bf16[1,12,6336]{2,0,1:T(2,128)(2,1)S(1)}) fusion(bf16[2,12,6336]{2,0,1:T(2,128)(2,1)} %param.26, s32[]{:T(128)S(6)} %select_n.13, bf16[2,12,6336]{2,0,1:T(2,128)(2,1)} %param.22), kind=kLoop, calls=%fused_computation.2 | loop fusion | bytes 608260 | tf_op jit(solution)/shard_map/jit(dynamic_index_in_dim)/dynamic_slice | solution.py:341
  11.4 0.0 copy-start.4
  11.4 0.0 copy-start.10
  11.5 0.8 %broadcast_in_dim.11.gain = f32[1,768]{1,0:T(1,128)S(1)} reshape(f32[768]{0:T(1024)} %param.19) | data formatting | bytes 6144 | tf_op jit(solution)/shard_map/broadcast_in_dim | solution.py:350
  12.2 2.0 %shard_map.150 = (bf16[12,144,144]{2,1,0:T(8,128)(2,1)S(1)}, bf16[12,144,144]{2,1,0:T(8,128)(2,1)S(1)}) custom-call(bf16[12,6336]{1,0:T(8,128)(2,1)S(1)} %bitcast.21, bf16[12,6336]{1,0:T(8,128)(2,1)S(1)} %bitcast.20), custom_call_target="tpu_custom_call" | custom-call | tf_op jit(solution)/shard_map/pallas_call | solution.py:292
  14.2 0.0 collective-permute-done.received
  14.2 0.0 copy-done.2
  14.2 0.0 copy-start
  14.3 2.0 %copy-done = bf16[768,2304]{1,0:T(8,128)(2,1)S(1)} copy-done((bf16[768,2304]{1,0:T(8,128)(2,1)S(1)}, bf16[768,2304]{1,0:T(8,128)(2,1)}, u32[]{:S(2)}) %copy-start) | copy-done | bytes 3538968
  16.3 0.0 copy-start.3
  16.3 2.5 %shard_map.151 = (bf16[72,768]{1,0:T(8,128)(2,1)S(1)}, bf16[72,768]{1,0:T(8,128)(2,1)S(1)}, bf16[72,768]{1,0:T(8,128)(2,1)S(1)}, bf16[72,768]{1,0:T(8,128)(2,1)S...) custom-call(bf16[144,768]{1,0:T(8,128)(2,1)S(1)} %get-tuple-element.21.keep, ...), custom_call_target="tpu_custom_call" | custom-call | tf_op jit(solution)/shard_map/pallas_call | solution.py:292
  18.8 0.0 copy-start.1
  18.8 8.8 %collective-permute-start.1 = (bf16[72,768]{1,0:T(8,128)(2,1)S(1)}, bf16[72,768]{1,0:T(8,128)(2,1)S(1)}, u32[]{:S(2)}, u32[]{:S(2)}) collective-permute-start(bf16[72,768]{1,0:T(8,128)(2,1)S(1)} %get-tuple-element.25), channel_id=1, source_target_pairs={{0,126},{2,0},{4,2},{6,4},{8,6},{10,8},{12,10},{14,12},{16,14},{18... | collective-permute-start | bytes 331784 | tf_op jit(solution)/shard_map/ppermute | solution.py:311
  27.6 0.3 collective-permute-start.2
  27.9 1.6 %collective-permute-start.3 = (bf16[72,768]{1,0:T(8,128)(2,1)S(1)}, bf16[72,768]{1,0:T(8,128)(2,1)S(1)}, u32[]{:S(2)}, u32[]{:S(2)}) collective-permute-start(bf16[72,768]{1,0:T(8,128)(2,1)S(1)} %get-tuple-element.27), channel_id=1, source_target_pairs={{0,255},{2,129},{4,131},{6,133},{8,135},{10,137},{12,139},{14,141}... | collective-permute-start | bytes 331784 | tf_op jit(solution)/shard_map/ppermute | solution.py:311
  29.5 0.0 copy-done.10
  29.5 0.5 collective-permute-done.1.right
  30.1 2.0 %collective-permute-done.2.down = bf16[72,768]{1,0:T(8,128)(2,1)S(1)} collective-permute-done((bf16[72,768]{1,0:T(8,128)(2,1)S(1)}, bf16[72,768]{1,0:T(8,128)(2,1)S(1)}, u32[]{:S(2)}, u32[]{:S(2)}) %collective-permute-start.2) | collective-permute-done | bytes 110624 | tf_op jit(solution)/shard_map/ppermute | solution.py:311
  32.1 1.8 %collective-permute-done.3.corner = bf16[72,768]{1,0:T(8,128)(2,1)S(1)} collective-permute-done((bf16[72,768]{1,0:T(8,128)(2,1)S(1)}, bf16[72,768]{1,0:T(8,128)(2,1)S(1)}, u32[]{:S(2)}, u32[]{:S(2)}) %collective-permute-start.3) | collective-permute-done | bytes 110624 | tf_op jit(solution)/shard_map/ppermute | solution.py:311
  33.9 0.0 copy-done.4
  33.9 0.0 copy-done.3
  33.9 8.5 %shard_map.152 = (bf16[72,768]{1,0:T(8,128)(2,1)S(1)}, bf16[72,768]{1,0:T(8,128)(2,1)S(1)}, bf16[72,768]{1,0:T(8,128)(2,1)S(1)}, bf16[72,768]{1,0:T(8,128)(2,1)S(1)}) custom-call(bf16[72,768]{1,0:T(8,128)(2,1)S(1)} %get-tuple-element.24.stay, bf16[72,768]{1,0:T(8,128)(2,1)S(1)} %collective-permute-done.1.right, ...), custom_call_target="tpu_custom_call" | custom-call | tf_op jit(solution)/shard_map/pallas_call | solution.py:292
  42.4 0.1 collective-permute-start.4
  42.5 0.6 collective-permute-start.5
  43.1 0.0 collective-permute-start.6
  43.1 9.9 %collective-permute-done.4.left = bf16[72,768]{1,0:T(8,128)(2,1)S(1)} collective-permute-done((bf16[72,768]{1,0:T(8,128)(2,1)S(1)}, bf16[72,768]{1,0:T(8,128)(2,1)S(1)}, u32[]{:S(2)}, u32[]{:S(2)}) %collective-permute-start.4) | collective-permute-done | bytes 110624 | tf_op jit(solution)/shard_map/ppermute | solution.py:311
  53.0 0.0 collective-permute-done.5.up
  53.0 2.3 %collective-permute-done.6.corner = bf16[72,768]{1,0:T(8,128)(2,1)S(1)} collective-permute-done((bf16[72,768]{1,0:T(8,128)(2,1)S(1)}, bf16[72,768]{1,0:T(8,128)(2,1)S(1)}, u32[]{:S(2)}, u32[]{:S(2)}) %collective-permute-start.6) | collective-permute-done | bytes 110624 | tf_op jit(solution)/shard_map/ppermute | solution.py:311
  55.3 0.0 copy-done.1
  55.3 6.3 %shard_map.153 = (bf16[144,768]{1,0:T(8,128)(2,1)S(1)}, bf16[144,768]{1,0:T(8,128)(2,1)S(1)}) custom-call(bf16[72,768]{1,0:T(8,128)(2,1)S(1)} %get-tuple-element.29.stay, bf16[72,768]{1,0:T(8,128)(2,1)S(1)} %collective-permute-done.4.left, bf16[72,768]{1,0:T(8,128)(2,1)S(1)} %collective-permute-done.5.up, bf16[72,768]{1,0:T(8,128)(2,1)S(1)} %collective-permute-done.6.corner, ...), custom_call_target="tpu_custom_call" | custom-call | tf_op jit(solution)/shard_map/pallas_call | solution.py:292
  61.6 0.1 collective-permute-start.7
  61.7 1.5 %collective-permute-done.7.received = bf16[144,768]{1,0:T(8,128)(2,1)S(1)} collective-permute-done((bf16[144,768]{1,0:T(8,128)(2,1)S(1)}, bf16[144,768]{1,0:T(8,128)(2,1)S(1)}, u32[]{:S(2)}, u32[]{:S(2)}) %collective-permute-start.7) | collective-permute-done | bytes 221216 | tf_op jit(solution)/shard_map/ppermute | solution.py:366
  63.2 1.0 %shard_map.154 = (bf16[144,768]{1,0:T(8,128)(2,1)}, bf16[144,768]{1,0:T(8,128)(2,1)}) custom-call(bf16[144,768]{1,0:T(8,128)(2,1)S(1)} %get-tuple-element.36.keep, bf16[144,768]{1,0:T(8,128)(2,1)S(1)} %collective-permute-done.7.received), custom_call_target="tpu_custom_call" | custom-call | tf_op jit(solution)/shard_map/pallas_call | solution.py:292
  (3 shorter events, 0.1 us)
Async XLA Ops:
  0.6 13.6 %copy-start.2 = (bf16[768,768]{1,0:T(8,128)(2,1)S(1)}, bf16[768,768]{1,0:T(8,128)(2,1)}, u32[]{:S(2)}) copy-start(bf16[768,768]{1,0:T(8,128)(2,1)} %weight_proj.5) | copy-start | bytes 3538948
  1.4 0.9 %copy-start.5 = (bf16[2,24,3,768]{3,1,2,0:T(8,128)(2,1)S(1)}, bf16[2,24,3,768]{3,1,2,0:T(8,128)(2,1)}, u32[]{:S(2)}) copy-start(bf16[2,24,3,768]{3,1,2,0:T(8,128)(2,1)} %param.14) | copy-start | bytes 663556
  2.4 0.9 %copy-start.6 = (bf16[2,24,3,768]{3,1,2,0:T(8,128)(2,1)S(1)}, bf16[2,24,3,768]{3,1,2,0:T(8,128)(2,1)}, u32[]{:S(2)}) copy-start(bf16[2,24,3,768]{3,1,2,0:T(8,128)(2,1)} %param.27) | copy-start | bytes 663556
  3.3 0.7 %copy-start.7 = (f32[8,768]{1,0:T(8,128)S(1)}, f32[8,768]{1,0:T(8,128)}, u32[]{:S(2)}) copy-start(f32[8,768]{1,0:T(8,128)} %orog_table.1) | copy-start | bytes 73732
  4.0 0.7 %copy-start.8 = (s32[24,3]{0,1:T(4,128)S(1)}, s32[24,3]{0,1:T(4,128)}, u32[]{:S(2)}) copy-start(s32[24,3]{0,1:T(4,128)} %param.15) | copy-start | bytes 868
  4.7 0.7 %copy-start.9 = (s32[24,3]{0,1:T(4,128)S(1)}, s32[24,3]{0,1:T(4,128)}, u32[]{:S(2)}) copy-start(s32[24,3]{0,1:T(4,128)} %param.16) | copy-start | bytes 868
  6.3 7.9 %collective-permute-start = (bf16[144,768]{1,0:T(8,128)(2,1)S(1)}, bf16[144,768]{1,0:T(8,128)(2,1)S(1)}, u32[]{:S(2)}, u32[]{:S(2)}) collective-permute-start(bf16[144,768]{1,0:T(8,128)(2,1)S(1)} %get-tuple-element.22), channel_id=1, source_target_pairs={{0,1},{1,0},{2,3},{3,2},{4,5},{5,4},{6,7},{7,6},{8,9},{9,8},{10,11... | collective-permute-start | bytes 663560 | tf_op jit(solution)/shard_map/ppermute | solution.py:336
  11.4 22.5 %copy-start.4 = (bf16[768,768]{1,0:T(8,128)(2,1)S(1)}, bf16[768,768]{1,0:T(8,128)(2,1)}, u32[]{:S(2)}) copy-start(bf16[768,768]{1,0:T(8,128)(2,1)} %weight_proj.4) | copy-start | bytes 3538948
  11.4 18.1 %copy-start.10 = (f32[768]{0:T(1024)S(1)}, f32[768]{0:T(1024)}, u32[]{:S(2)}) copy-start(f32[768]{0:T(1024)} %param.23) | copy-start | bytes 9220
  14.2 2.0 %copy-start = (bf16[768,2304]{1,0:T(8,128)(2,1)S(1)}, bf16[768,2304]{1,0:T(8,128)(2,1)}, u32[]{:S(2)}) copy-start(bf16[768,2304]{1,0:T(8,128)(2,1)} %weight_qkv.5) | copy-start | bytes 10616836
  16.3 17.6 %copy-start.3 = (bf16[768,2304]{1,0:T(8,128)(2,1)S(1)}, bf16[768,2304]{1,0:T(8,128)(2,1)}, u32[]{:S(2)}) copy-start(bf16[768,2304]{1,0:T(8,128)(2,1)} %weight_qkv.4) | copy-start | bytes 10616836
  18.8 36.5 %copy-start.1 = (bf16[768,2304]{1,0:T(8,128)(2,1)S(1)}, bf16[768,2304]{1,0:T(8,128)(2,1)}, u32[]{:S(2)}) copy-start(bf16[768,2304]{1,0:T(8,128)(2,1)} %weight_qkv.5) | copy-start | bytes 10616836
  18.8 11.3 %collective-permute-start.1 = (bf16[72,768]{1,0:T(8,128)(2,1)S(1)}, bf16[72,768]{1,0:T(8,128)(2,1)S(1)}, u32[]{:S(2)}, u32[]{:S(2)}) collective-permute-start(bf16[72,768]{1,0:T(8,128)(2,1)S(1)} %get-tuple-element.25), channel_id=1, source_target_pairs={{0,126},{2,0},{4,2},{6,4},{8,6},{10,8},{12,10},{14,12},{16,14},{18... | collective-permute-start | bytes 331784 | tf_op jit(solution)/shard_map/ppermute | solution.py:311
  27.6 4.5 %collective-permute-start.2 = (bf16[72,768]{1,0:T(8,128)(2,1)S(1)}, bf16[72,768]{1,0:T(8,128)(2,1)S(1)}, u32[]{:S(2)}, u32[]{:S(2)}) collective-permute-start(bf16[72,768]{1,0:T(8,128)(2,1)S(1)} %get-tuple-element.26), channel_id=1, source_target_pairs={{0,129},{2,131},{4,133},{6,135},{8,137},{10,139},{12,141},{14,143}... | collective-permute-start | bytes 331784 | tf_op jit(solution)/shard_map/ppermute | solution.py:311
  27.9 5.9 %collective-permute-start.3 = (bf16[72,768]{1,0:T(8,128)(2,1)S(1)}, bf16[72,768]{1,0:T(8,128)(2,1)S(1)}, u32[]{:S(2)}, u32[]{:S(2)}) collective-permute-start(bf16[72,768]{1,0:T(8,128)(2,1)S(1)} %get-tuple-element.27), channel_id=1, source_target_pairs={{0,255},{2,129},{4,131},{6,133},{8,135},{10,137},{12,139},{14,141}... | collective-permute-start | bytes 331784 | tf_op jit(solution)/shard_map/ppermute | solution.py:311
  42.4 10.6 %collective-permute-start.4 = (bf16[72,768]{1,0:T(8,128)(2,1)S(1)}, bf16[72,768]{1,0:T(8,128)(2,1)S(1)}, u32[]{:S(2)}, u32[]{:S(2)}) collective-permute-start(bf16[72,768]{1,0:T(8,128)(2,1)S(1)} %get-tuple-element.30), channel_id=1, source_target_pairs={{0,2},{2,4},{4,6},{6,8},{8,10},{10,12},{12,14},{14,16},{16,18},{18... | collective-permute-start | bytes 331784 | tf_op jit(solution)/shard_map/ppermute | solution.py:311
  42.5 10.5 %collective-permute-start.5 = (bf16[72,768]{1,0:T(8,128)(2,1)S(1)}, bf16[72,768]{1,0:T(8,128)(2,1)S(1)}, u32[]{:S(2)}, u32[]{:S(2)}) collective-permute-start(bf16[72,768]{1,0:T(8,128)(2,1)S(1)} %get-tuple-element.31), channel_id=1, source_target_pairs={{0,1},{2,3},{4,5},{6,7},{8,9},{10,11},{12,13},{14,15},{16,17},{18,... | collective-permute-start | bytes 331784 | tf_op jit(solution)/shard_map/ppermute | solution.py:311
  43.1 12.3 %collective-permute-start.6 = (bf16[72,768]{1,0:T(8,128)(2,1)S(1)}, bf16[72,768]{1,0:T(8,128)(2,1)S(1)}, u32[]{:S(2)}, u32[]{:S(2)}) collective-permute-start(bf16[72,768]{1,0:T(8,128)(2,1)S(1)} %get-tuple-element.32), channel_id=1, source_target_pairs={{0,3},{2,5},{4,7},{6,9},{8,11},{10,13},{12,15},{14,17},{16,19},{18... | collective-permute-start | bytes 331784 | tf_op jit(solution)/shard_map/ppermute | solution.py:311
  61.6 1.6 %collective-permute-start.7 = (bf16[144,768]{1,0:T(8,128)(2,1)S(1)}, bf16[144,768]{1,0:T(8,128)(2,1)S(1)}, u32[]{:S(2)}, u32[]{:S(2)}) collective-permute-start(bf16[144,768]{1,0:T(8,128)(2,1)S(1)} %get-tuple-element.37), channel_id=1, source_target_pairs={{0,1},{1,0},{2,3},{3,2},{4,5},{5,4},{6,7},{7,6},{8,9},{9,8},{10,11... | collective-permute-start | bytes 663560 | tf_op jit(solution)/shard_map/ppermute | solution.py:366

commit v2 on v1

v2 whole, which is shorter than its diff:
```python
import functools

import jax
import jax.numpy as jnp
from jax import lax
from jax.experimental import pallas as pl
from jax.experimental.pallas import tpu as pltpu
from jax.sharding import PartitionSpec as P

D = 768
HEADS = 12
DEPTH = 64
TOKENS = 144
HALF = 72
QUAD = 36
CHUNK = 132
OROG = 8
LAND = 16
EPS = 1e-05

f32 = jnp.float32
bf16 = jnp.bfloat16


def iota(shape, dim):
    return lax.broadcasted_iota(jnp.int32, shape, dim)


def div(a, b):
    return lax.div(a, jnp.int32(b))


def rem(a, b):
    return lax.rem(a, jnp.int32(b))


def dot(a, b):
    return jnp.dot(a, b, preferred_element_type=f32)


def dot_t(a, b):
    return lax.dot_general(a, b, (((1,), (1,)), ((), ())), preferred_element_type=f32)


def t_dot(a, b):
    return lax.dot_general(a, b, (((0,), (0,)), ((), ())), preferred_element_type=f32)


def parity():
    return rem(lax.axis_index("lon").astype(jnp.int32), 2)


def split_token(i):
    level = rem(div(i, 18), 2)
    line = rem(div(i, 36), 2) * 6 + rem(i, 6)
    col = div(i, 72) * 3 + rem(div(i, 6), 3)
    return level, line, col


def natural_place(i, band):
    level = rem(div(i, 18), 2)
    row = band * 12 + div(i, 36) * 6 + rem(i, 6)
    col = rem(div(i, 6), 3)
    return level * 72 + col * 24 + row


def pack_kernel(
    stream_at, land_at, orography_at, vector_at, table_at, cotangent_at, keep, send,
    stream, land, orography, land_vector, orog_table, cotangent, sems,
):
    c = parity()
    copies = [
        pltpu.make_async_copy(source, target, sems.at[index])
        for index, (source, target) in enumerate((
            (stream_at, stream), (cotangent_at, cotangent), (table_at, orog_table),
            (vector_at, land_vector), (land_at, land), (orography_at, orography),
        ))
    ]
    for copy in copies:
        copy.start()
    out = iota((TOKENS, TOKENS), 0)
    own = out < HALF
    place = natural_place(jnp.where(own, out, out - HALF), jnp.where(own, c, 1 - c))
    move = (iota((TOKENS, TOKENS), 1) == place).astype(f32).astype(bf16)
    for copy in copies:
        copy.wait()
    kinds = iota((OROG, 24), 0)
    added = []
    for w in range(3):
        onehot = (orography[w : w + 1, :] == kinds).astype(f32)
        looked = lax.dot_general(
            onehot,
            orog_table[...],
            (((0,), (0,)), ((), ())),
            precision=lax.Precision.HIGHEST,
            preferred_element_type=f32,
        )
        share = land[w : w + 1, :].astype(f32) * (1.0 / LAND)
        spread = lax.dot_general(
            jnp.concatenate([share, jnp.zeros((7, 24), f32)], axis=0),
            jnp.concatenate([row(land_vector), jnp.zeros((7, D), f32)], axis=0),
            (((0,), (0,)), ((), ())),
            precision=lax.Precision.HIGHEST,
            preferred_element_type=f32,
        )
        added.append(spread + looked)
    added = jnp.concatenate(added + added, axis=0)
    embedded = (stream[...].astype(f32) + added).astype(bf16)
    e = dot(move, embedded)
    g = dot(move, cotangent[...])
    keep[...] = jnp.concatenate([e[:HALF], g[:HALF]], axis=0).astype(bf16)
    send[...] = jnp.concatenate([e[HALF:], g[HALF:]], axis=0).astype(bf16)


def unpack_kernel(keep, received, output, grad):
    c = parity()
    inp = iota((TOKENS, TOKENS), 1)
    own = inp < HALF
    place = natural_place(jnp.where(own, inp, inp - HALF), jnp.where(own, c, 1 - c))
    move = (iota((TOKENS, TOKENS), 0) == place).astype(f32).astype(bf16)
    k = keep[...].astype(f32)
    r = received[...].astype(f32)
    grads = jnp.concatenate([k[:HALF], r[:HALF]], axis=0).astype(bf16)
    turned = jnp.concatenate([k[HALF:], r[HALF:]], axis=0).astype(bf16)
    grad[...] = dot(move, grads).astype(bf16)
    output[...] = dot(move, turned).astype(bf16)


def bias_kernel(masked, table, bias, first, second):
    place = iota((TOKENS, TOKENS), 1)
    level, line, col = split_token(iota((TOKENS, TOKENS), 0))
    spread = (place == col * 24 + level * 12 + line).astype(f32).astype(bf16)
    level, line, col = split_token(iota((256, TOKENS), 1))
    lane = iota((256, TOKENS), 0)
    lane = jnp.where(lane < 128, lane, jnp.where(lane < 252, -1000, lane - 124))
    base = lane - line * 11 + col - 5
    for za in range(2):
        for zc in range(2):
            into = second if zc else first
            for ra in range(12):
                at = ((za * 2 + zc) * 12 + ra) * CHUNK
                for part, skip in enumerate((0, CHUNK - 128)):
                    into[part, pl.ds(za * 12 + ra, HEADS, stride=24), :] = table[
                        :, at + skip : at + skip + 128
                    ].astype(f32)
    low = jnp.concatenate([first[0], first[1]], axis=1).astype(bf16)
    high = jnp.concatenate([second[0], second[1]], axis=1).astype(bf16)
    parts = []
    for i in range(6):
        hit = base == i
        pick_low = (hit & (level == 0)).astype(f32).astype(bf16)
        pick_high = (hit & (level == 1)).astype(f32).astype(bf16)
        parts.append(dot(low, pick_low) + dot(high, pick_high))
    if masked:
        last = (lax.axis_index("lat") == lax.axis_size("lat") - 1) & (parity() == 1)
        half_q = rem(div(iota((TOKENS, TOKENS), 0), QUAD), 2)
        half_k = rem(div(iota((TOKENS, TOKENS), 1), QUAD), 2)
        forbidden = (half_q != half_k) & last
    for n in range(HEADS):
        stacked = jnp.concatenate([part[n * 24 : n * 24 + 24] for part in parts], axis=0)
        one = dot(spread, stacked.astype(bf16))
        if masked:
            one = jnp.where(forbidden, -1e9, one)
        bias[n] = one.astype(bf16).T


def norm(u):
    average = jnp.mean(u, axis=-1, keepdims=True)
    centred = u - average
    inverse = lax.rsqrt(jnp.mean(centred * centred, axis=-1, keepdims=True) + EPS)
    return centred * inverse, inverse


def row(vector):
    return vector[...].reshape(1, D)


def lane_masks(value):
    low = iota((1, 2 * DEPTH), 1) < DEPTH
    return (
        jnp.where(low, value, 0.0).astype(bf16),
        jnp.where(low, 0.0, value).astype(bf16),
    )


def attend(qkv, bias, probs, mixed):
    masks = lane_masks(DEPTH ** (-0.5))
    low = iota((TOKENS, 2 * DEPTH), 1) < DEPTH
    for pair in range(HEADS // 2):
        at = pair * 2 * DEPTH
        q2 = qkv[:, at : at + 128]
        k2 = qkv[:, D + at : D + at + 128]
        v2 = qkv[:, 2 * D + at : 2 * D + at + 128]
        both = dot_t(jnp.concatenate([k2 * masks[0], k2 * masks[1]], axis=0), q2)
        turned = []
        for side in range(2):
            n = pair * 2 + side
            scores = both[side * TOKENS : side * TOKENS + TOKENS] + bias[n].astype(f32)
            expo = jnp.exp(scores - jnp.max(scores, axis=0, keepdims=True))
            p = (expo * (1.0 / jnp.sum(expo, axis=0, keepdims=True))).astype(bf16)
            probs[n] = p
            turned.append(p.T)
        both = dot(jnp.concatenate(turned, axis=0), v2)
        mixed[:, at : at + 128] = jnp.where(low, both[:TOKENS], both[TOKENS:]).astype(bf16)


def attend_back(qkv, probs, grad_mixed, grad_qkv):
    masks = lane_masks(1.0)
    low = iota((TOKENS, 2 * DEPTH), 1) < DEPTH
    for pair in range(HEADS // 2):
        at = pair * 2 * DEPTH
        q2 = qkv[:, at : at + 128]
        k2 = qkv[:, D + at : D + at + 128]
        v2 = qkv[:, 2 * D + at : 2 * D + at + 128]
        g2 = grad_mixed[:, at : at + 128]
        both = dot_t(jnp.concatenate([v2 * masks[0], v2 * masks[1]], axis=0), g2)
        ps, ds, ds_t = [], [], []
        for side in range(2):
            p = probs[pair * 2 + side]
            wide = p.astype(f32)
            dp = both[side * TOKENS : side * TOKENS + TOKENS]
            inner = jnp.sum(wide * dp, axis=0, keepdims=True)
            d = (wide * (dp - inner) * (DEPTH ** (-0.5))).astype(bf16)
            ps.append(p)
            ds.append(d)
            ds_t.append(d.T)
        for block, (lhs, rhs) in enumerate(((ds_t, k2), (ds, q2), (ps, g2))):
            both = dot(jnp.concatenate(lhs, axis=0), rhs)
            grad_qkv[:, block * D + at : block * D + at + 128] = jnp.where(
                low, both[:TOKENS], both[TOKENS:]
            ).astype(bf16)


def norm_back(dh, gain, normed, inverse):
    dn = dh * gain
    first = jnp.mean(dn, axis=-1, keepdims=True)
    second = jnp.mean(dn * normed, axis=-1, keepdims=True)
    return (dn - first - normed * second) * inverse


def pieces(array):
    return [array[index * QUAD : (index + 1) * QUAD] for index in range(4)]


QUARTERS_ONE = ((3, 1), (1, 3), (0, 2), (2, 0))
QUARTERS_TWO = ((0, 2), (2, 0), (1, 3), (3, 1))


def deal(quarters, c, refs, above, below):
    tops, bottoms = pieces(above), pieces(below)
    even = c == 0
    for (first, second), out in zip(quarters, refs):
        out[...] = jnp.concatenate(
            [jnp.where(even, part[first], part[second]) for part in (tops, bottoms)], axis=0
        ).astype(bf16)


def gather(quarters, c, refs):
    even = c == 0
    values = [ref[...].astype(f32) for ref in refs]
    chosen = []
    for index in range(4):
        at_even = [first for first, _ in quarters].index(index)
        at_odd = [second for _, second in quarters].index(index)
        chosen.append(jnp.where(even, values[at_even], values[at_odd]))
    return (
        jnp.concatenate([value[:QUAD] for value in chosen], axis=0),
        jnp.concatenate([value[QUAD:] for value in chosen], axis=0),
    )


def one_kernel(
    keep, received, gain, weight_qkv, weight_proj, bias,
    stay, first, second, third, u_out, qkv, probs, mixed,
):
    c = parity()
    k = keep[...].astype(f32)
    r = received[...].astype(f32)
    mine = c == 0
    lead = jnp.where(mine, k, r)
    trail = jnp.where(mine, r, k)
    u = jnp.concatenate([lead[:HALF], trail[:HALF]], axis=0)
    g = jnp.concatenate([lead[HALF:], trail[HALF:]], axis=0)
    u_out[...] = u.astype(bf16)
    normed, _ = norm(u)
    h = (normed * row(gain)).astype(bf16)
    qkv[...] = dot(h, weight_qkv[...]).astype(bf16)
    attend(qkv, bias, probs, mixed)
    middle = u + dot(mixed[...], weight_proj[...])
    deal(QUARTERS_ONE, c, (stay, first, second, third), middle, g)


def two_kernel(
    stay, first, second, third, gain, weight_qkv, weight_proj, bias,
    back_stay, back_first, back_second, back_third,
    qkv, probs, mixed, grad_mixed, grad_qkv,
):
    c = parity()
    u, g = gather(QUARTERS_TWO, c, (stay, first, second, third))
    normed, inverse = norm(u)
    h = (normed * row(gain)).astype(bf16)
    qkv[...] = dot(h, weight_qkv[...]).astype(bf16)
    attend(qkv, bias, probs, mixed)
    turned = u + dot(mixed[...], weight_proj[...])
    grad_mixed[...] = dot_t(g.astype(bf16), weight_proj[...]).astype(bf16)
    attend_back(qkv, probs, grad_mixed, grad_qkv)
    dh = dot_t(grad_qkv[...], weight_qkv[...])
    du = g + norm_back(dh, row(gain), normed, inverse)
    deal(QUARTERS_TWO, c, (back_stay, back_first, back_second, back_third), du, turned)


def three_kernel(
    stay, first, second, third, u, qkv, probs, gain, weight_qkv, weight_proj,
    keep, send, grad_mixed, grad_qkv,
):
    c = parity()
    g, turned = gather(QUARTERS_ONE, c, (stay, first, second, third))
    normed, inverse = norm(u[...].astype(f32))
    grad_mixed[...] = dot_t(g.astype(bf16), weight_proj[...]).astype(bf16)
    attend_back(qkv, probs, grad_mixed, grad_qkv)
    dh = dot_t(grad_qkv[...], weight_qkv[...])
    du = g + norm_back(dh, row(gain), normed, inverse)
    mine = c == 0
    low = jnp.concatenate([du[:HALF], turned[:HALF]], axis=0)
    high = jnp.concatenate([du[HALF:], turned[HALF:]], axis=0)
    keep[...] = jnp.where(mine, low, high).astype(bf16)
    send[...] = jnp.where(mine, high, low).astype(bf16)


def shape(*dims, dtype=bf16):
    return jax.ShapeDtypeStruct(dims, dtype)


def call(kernel, outs, scratch, mib, micros, *args, **options):
    return pl.pallas_call(
        kernel,
        out_shape=outs,
        scratch_shapes=scratch,
        compiler_params=pltpu.CompilerParams(vmem_limit_bytes=mib * 1024 * 1024),
        cost_estimate=pl.CostEstimate(
            flops=int(micros * 1e9), bytes_accessed=int(micros * 3e6), transcendentals=0
        ),
        **options,
    )(*args)


def exchange(number, back):
    lats, lons = lax.axis_size("lat"), lax.axis_size("lon")

    def device(a, p, c):
        return a % lats * lons + 2 * p % lons + c

    pairs = []
    for a in range(lats):
        for p in range(lons // 2):
            even, odd = (
                (device(a, p - 1, 0), device(a, p + 1, 1)),
                (device(a - 1, p, 1), device(a, p, 0)),
                (device(a - 1, p + 1, 1), device(a, p - 1, 0)),
            )[number]
            pairs += [(device(a, p, 0), even), (device(a, p, 1), odd)]
    return [(target, source) for source, target in pairs] if back else pairs


def exchanged(values, back):
    return [
        lax.ppermute(value, ("lat", "lon"), exchange(number, back))
        for number, value in enumerate(values)
    ]


def body(
    stream, land, orography, land_vector, orography_table,
    gain_one, qkv_one, proj_one, table_one,
    gain_two, qkv_two, proj_two, table_two, cotangent,
):
    swap = [(i, i ^ 1) for i in range(lax.axis_size("lon"))]
    c = lax.axis_index("lon") % 2

    def flat(array):
        return array.transpose(0, 2, 1, 3).reshape(TOKENS, D)

    def field(array):
        return array.reshape(2, 3, 24, D).transpose(0, 2, 1, 3)

    tokens = shape(TOKENS, D)
    quad = shape(2 * QUAD, D)
    wide = pltpu.VMEM((TOKENS, 3 * D), bf16)
    narrow = pltpu.VMEM((TOKENS, D), bf16)
    keep, send = call(
        pack_kernel, (tokens, tokens),
        [
            narrow, pltpu.VMEM((3, 24), jnp.int32), pltpu.VMEM((3, 24), jnp.int32),
            pltpu.VMEM((D,), f32), pltpu.VMEM((OROG, D), f32), narrow,
            pltpu.SemaphoreType.DMA((6,)),
        ],
        56, 3.0,
        flat(stream), land.T, orography.T, land_vector, orography_table, flat(cotangent),
        in_specs=[pl.BlockSpec(memory_space=pltpu.HBM)] * 6,
    )
    received = lax.ppermute(send, "lon", swap)
    square = shape(HEADS, TOKENS, TOKENS)

    def bias_of(table, masked):
        return call(
            functools.partial(bias_kernel, masked), square,
            [pltpu.VMEM((2, HEADS * 24, 128), f32)] * 2, 8, 1.5,
            lax.dynamic_index_in_dim(table, c, 0, False),
        )

    stay, *leave, u_one, saved_qkv, saved_probs = call(
        one_kernel,
        (quad, quad, quad, quad, tokens, shape(TOKENS, 3 * D), square),
        [narrow], 16, 3.0,
        keep, received, gain_one, qkv_one, proj_one, bias_of(table_one, False),
    )
    table_two, stay = lax.optimization_barrier((table_two, stay))
    arrived = exchanged(leave, False)
    stay, *leave = call(
        two_kernel, (quad, quad, quad, quad),
        [wide, pltpu.VMEM((HEADS, TOKENS, TOKENS), bf16), narrow, narrow, wide], 16, 8.0,
        stay, *arrived, gain_two, qkv_two, proj_two, bias_of(table_two, True),
    )
    arrived = exchanged(leave, True)
    keep, send = call(
        three_kernel, (tokens, tokens), [narrow, wide], 16, 6.0,
        stay, *arrived, u_one, saved_qkv, saved_probs, gain_one, qkv_one, proj_one,
    )
    received = lax.ppermute(send, "lon", swap)
    output, grad = call(unpack_kernel, (tokens, tokens), [], 8, 1.0, keep, received)
    return field(output), field(grad)


def solution(mesh):
    tokens = P(None, "lat", "lon", None)
    table = P("lat", None, None)
    placed = (
        tokens, P("lat", "lon"), P("lat", "lon"), P(), P(),
        P(), P(), P(), table, P(), P(), P(), table, tokens,
    )
    return jax.shard_map(
        body, mesh=mesh, in_specs=placed, out_specs=(tokens, tokens), check_vma=False
    )
```

time: 64.5 us -> 53 us (0.82)
  local copies, waits for them, and re-layouts: 9.31 us -> 0.72 us
  Pallas kernels: 21.2 us -> 18.7 us
  waiting for transfers between devices: 18 us -> 17.3 us
    unnamed x24 -> x19, local copies, waits for them, and re-layouts: 6.05 us -> 0.33 us
    pallas_call x6 -> x7, Pallas kernels: 21.2 us -> 18.7 us  [call(): pl.pallas_call(kernel, out_shape=outs, scratch_shapes=scratch, compiler_p...]
    broadcast_in_dim x3 -> x0, local copies, waits for them, and re-layouts: 1.56 us -> none  [the longest x1 0.79 us: body(): land_vector[None]]
    dynamic_slice x1, local copies, waits for them, and re-layouts: 1.7 us -> 0.32 us  [bias_of(): lax.dynamic_index_in_dim(table, c, 0, False)]
    ppermute x6, waiting for transfers between devices: 16.6 us -> 15.8 us  [exchanged(): lax.ppermute(value, ('lat', 'lon'), exchange(number, back))]
  transfers between devices with their start and end apart: 8 -> 8, of which waited for: 6 -> 5; matrix products, arithmetic and copies ran while one was open for 4% -> 1% of each run, Pallas kernels for 3% -> 5%
where the time goes in v2:
time: 53 us; the launch traced here: 52.9 us
  Pallas kernels  18.7 us (35%)
  waiting for transfers between devices  17.3 us (33%)
  starting transfers between devices  15.3 us (29%)
  between operations  0.84 us (2%)
  local copies, waits for them, and re-layouts  0.72 us (1%)
    pallas_call x7, Pallas kernels, call(): pl.pallas_call(kernel, out_shape=outs, scratch_shapes=scratch, compiler_p...  18.7 us
    ppermute x6, waiting for transfers between devices, exchanged(): lax.ppermute(value, ('lat', 'lon'), exchange(number, back))  15.8 us
    ppermute x6, starting transfers between devices, exchanged(): lax.ppermute(value, ('lat', 'lon'), exchange(number, back))  11.9 us
    ppermute x2, starting transfers between devices, body(): received = lax.ppermute(send, 'lon', swap)  3.42 us
    ppermute x2, waiting for transfers between devices, body(): received = lax.ppermute(send, 'lon', swap)  1.47 us
  transfers between devices with their start and end apart: 8, of which 5 were waited for; matrix products, arithmetic and copies ran while one was open for 1% of the time, Pallas kernels for 5%

profile of v2, /device:TPU:1, one launch (start us, length us, event | category | flops | bytes accessed | tf_op | source)
XLA Modules:
  0.0 52.9 jit_solution(11682459025931796496)
XLA Ops:
  0.6 0.0 copy-start
  0.6 2.8 %shard_map.149 = (bf16[144,768]{1,0:T(8,128)(2,1)}, bf16[144,768]{1,0:T(8,128)(2,1)}) custom-call(bf16[144,768]{1,0:T(8,128)(2,1)} %bitcast.20, s32[3,24]{1,0:T(4,128)} %bitcast.22, s32[3,24]{1,0:T(4,128)} %bitcast.23, f32[768]{0:T(1024)} %vector_at.1, f32[8,768]{1,0:T(8,128)} %table_at.1, bf16[144,768]{1,0:T(8,128)(2,1)} %bitcast.21), custom_call_target="tpu_custom_call" | custom-call | flops 3000000000 | bytes 9000000 | tf_op jit(solution)/shard_map/pallas_call | solution.py:335
  3.5 0.0 copy-start.4
  3.5 0.0 copy-start.6
  3.5 0.0 copy-start.7
  3.5 3.3 %collective-permute-start = (bf16[144,768]{1,0:T(8,128)(2,1)}, bf16[144,768]{1,0:T(8,128)(2,1)S(1)}, u32[]{:S(2)}, u32[]{:S(2)}) collective-permute-start(bf16[144,768]{1,0:T(8,128)(2,1)} %get-tuple-element.22), channel_id=1, source_target_pairs={{0,1},{1,0},{2,3},{3,2},{4,5},{5,4},{6,7},{7,6},{8,9},{9,8},{10,11... | collective-permute-start | bytes 663560 | tf_op jit(solution)/shard_map/ppermute | solution.py:401
  6.8 0.0 copy-done
  6.8 0.0 copy-start.2
  6.8 0.3 constant_dynamic-slice_fusion
  7.2 1.3 %shard_map.150.bias = bf16[12,144,144]{2,1,0:T(8,128)(2,1)S(1)} custom-call(bf16[12,6336]{1,0:T(8,128)(2,1)S(1)} %bitcast.19), custom_call_target="tpu_custom_call" | custom-call | flops 1500000000 | bytes 4500000 | tf_op jit(solution)/shard_map/pallas_call | solution.py:335
  8.6 0.0 collective-permute-done.received
  8.6 0.0 copy-done.4
  8.6 0.0 copy-done.6
  8.6 0.0 copy-done.7
  8.6 0.2 copy-done.2
  8.8 0.0 copy-start.8
  8.8 2.2 %shard_map.151 = (bf16[72,768]{1,0:T(8,128)(2,1)S(1)}, bf16[72,768]{1,0:T(8,128)(2,1)S(1)}, bf16[72,768]{1,0:T(8,128)(2,1)S(1)}, bf16[72,768]{1,0:T(8,128)(2,1)S...) custom-call(bf16[144,768]{1,0:T(8,128)(2,1)S(1)} %copy-done.7, ...), custom_call_target="tpu_custom_call" | custom-call | flops 3000000000 | bytes 9000000 | tf_op jit(solution)/shard_map/pallas_call | solution.py:335
  11.0 0.0 copy-start.1
  11.1 0.0 copy-start.3
  11.1 0.0 copy-start.5
  11.1 0.1 collective-permute-start.1
  11.2 9.4 %collective-permute-start.2 = (bf16[72,768]{1,0:T(8,128)(2,1)S(1)}, bf16[72,768]{1,0:T(8,128)(2,1)S(1)}, u32[]{:S(2)}, u32[]{:S(2)}) collective-permute-start(bf16[72,768]{1,0:T(8,128)(2,1)S(1)} %get-tuple-element.26), channel_id=1, source_target_pairs={{0,129},{1,0},{2,131},{3,2},{4,133},{5,4},{6,135},{7,6},{8,137},{9... | collective-permute-start | bytes 331784 | tf_op jit(solution)/shard_map/ppermute | solution.py:367
  20.5 0.8 %collective-permute-start.3 = (bf16[72,768]{1,0:T(8,128)(2,1)S(1)}, bf16[72,768]{1,0:T(8,128)(2,1)S(1)}, u32[]{:S(2)}, u32[]{:S(2)}) collective-permute-start(bf16[72,768]{1,0:T(8,128)(2,1)S(1)} %get-tuple-element.27), channel_id=1, source_target_pairs={{0,131},{1,126},{2,133},{3,0},{4,135},{5,2},{6,137},{7,4},{8,139},... | collective-permute-start | bytes 331784 | tf_op jit(solution)/shard_map/ppermute | solution.py:367
  21.3 0.0 copy-done.8
  21.4 1.3 %shard_map.152.bias = bf16[12,144,144]{2,1,0:T(8,128)(2,1)S(1)} custom-call(bf16[12,6336]{1,0:T(8,128)(2,1)S(1)} %dynamic-slice_bitcast_fusion.table), custom_call_target="tpu_custom_call" | custom-call | flops 1500000000 | bytes 4500000 | tf_op jit(solution)/shard_map/pallas_call | solution.py:335
  22.7 0.0 collective-permute-done.1.first
  22.7 0.7 %collective-permute-done.2.second = bf16[72,768]{1,0:T(8,128)(2,1)S(1)} collective-permute-done((bf16[72,768]{1,0:T(8,128)(2,1)S(1)}, bf16[72,768]{1,0:T(8,128)(2,1)S(1)}, u32[]{:S(2)}, u32[]{:S(2)}) %collective-permute-start.2) | collective-permute-done | bytes 110624 | tf_op jit(solution)/shard_map/ppermute | solution.py:367
  23.4 6.7 %collective-permute-done.3.third = bf16[72,768]{1,0:T(8,128)(2,1)S(1)} collective-permute-done((bf16[72,768]{1,0:T(8,128)(2,1)S(1)}, bf16[72,768]{1,0:T(8,128)(2,1)S(1)}, u32[]{:S(2)}, u32[]{:S(2)}) %collective-permute-start.3) | collective-permute-done | bytes 110624 | tf_op jit(solution)/shard_map/ppermute | solution.py:367
  30.1 0.0 copy-done.1
  30.1 0.0 copy-done.3
  30.1 0.0 copy-done.5
  30.1 6.1 %shard_map.153 = (bf16[72,768]{1,0:T(8,128)(2,1)S(1)}, bf16[72,768]{1,0:T(8,128)(2,1)S(1)}, bf16[72,768]{1,0:T(8,128)(2,1)S(1)}, bf16[72,768]{1,0:T(8,128)(2,1)S(1)}) custom-call(bf16[72,768]{1,0:T(8,128)(2,1)S(1)} %get-tuple-element.24.stay, bf16[72,768]{1,0:T(8,128)(2,1)S(1)} %collective-permute-done.1.first, ...), custom_call_target="tpu_custom_call" | custom-call | flops 8000000000 | bytes 24000000 | tf_op jit(solution)/shard_map/pallas_call | solution.py:335
  36.2 0.1 collective-permute-start.4
  36.3 0.1 collective-permute-start.5
  36.4 1.6 %collective-permute-start.6 = (bf16[72,768]{1,0:T(8,128)(2,1)S(1)}, bf16[72,768]{1,0:T(8,128)(2,1)S(1)}, u32[]{:S(2)}, u32[]{:S(2)}) collective-permute-start(bf16[72,768]{1,0:T(8,128)(2,1)S(1)} %get-tuple-element.32), channel_id=1, source_target_pairs={{131,0},{126,1},{133,2},{0,3},{135,4},{2,5},{137,6},{4,7},{139,8},... | collective-permute-start | bytes 331784 | tf_op jit(solution)/shard_map/ppermute | solution.py:367
  38.0 2.2 %collective-permute-done.4.first = bf16[72,768]{1,0:T(8,128)(2,1)S(1)} collective-permute-done((bf16[72,768]{1,0:T(8,128)(2,1)S(1)}, bf16[72,768]{1,0:T(8,128)(2,1)S(1)}, u32[]{:S(2)}, u32[]{:S(2)}) %collective-permute-start.4) | collective-permute-done | bytes 110624 | tf_op jit(solution)/shard_map/ppermute | solution.py:367
  40.2 0.0 collective-permute-done.5.second
  40.2 6.2 %collective-permute-done.6.third = bf16[72,768]{1,0:T(8,128)(2,1)S(1)} collective-permute-done((bf16[72,768]{1,0:T(8,128)(2,1)S(1)}, bf16[72,768]{1,0:T(8,128)(2,1)S(1)}, u32[]{:S(2)}, u32[]{:S(2)}) %collective-permute-start.6) | collective-permute-done | bytes 110624 | tf_op jit(solution)/shard_map/ppermute | solution.py:367
  46.4 3.9 %shard_map.154 = (bf16[144,768]{1,0:T(8,128)(2,1)S(1)}, bf16[144,768]{1,0:T(8,128)(2,1)S(1)}) custom-call(bf16[72,768]{1,0:T(8,128)(2,1)S(1)} %get-tuple-element.29.stay, bf16[72,768]{1,0:T(8,128)(2,1)S(1)} %collective-permute-done.4.first, bf16[72,768]{1,0:T(8,128)(2,1)S(1)} %collective-permute-done.5.second, ...), custom_call_target="tpu_custom_call" | custom-call | flops 6000000000 | bytes 18000000 | tf_op jit(solution)/shard_map/pallas_call | solution.py:335
  50.3 0.1 collective-permute-start.7
  50.4 1.5 %collective-permute-done.7.received = bf16[144,768]{1,0:T(8,128)(2,1)S(1)} collective-permute-done((bf16[144,768]{1,0:T(8,128)(2,1)S(1)}, bf16[144,768]{1,0:T(8,128)(2,1)S(1)}, u32[]{:S(2)}, u32[]{:S(2)}) %collective-permute-start.7) | collective-permute-done | bytes 221216 | tf_op jit(solution)/shard_map/ppermute | solution.py:429
  51.9 1.0 %shard_map.155 = (bf16[144,768]{1,0:T(8,128)(2,1)}, bf16[144,768]{1,0:T(8,128)(2,1)}) custom-call(bf16[144,768]{1,0:T(8,128)(2,1)S(1)} %get-tuple-element.36.keep, bf16[144,768]{1,0:T(8,128)(2,1)S(1)} %collective-permute-done.7.received), custom_call_target="tpu_custom_call" | custom-call | flops 1000000000 | bytes 3000000 | tf_op jit(solution)/shard_map/pallas_call | solution.py:335
  (3 shorter events, 0.1 us)
Async XLA Ops:
  0.6 6.2 %copy-start = (bf16[2,12,6336]{2,0,1:T(2,128)(2,1)S(1)}, bf16[2,12,6336]{2,0,1:T(2,128)(2,1)}, u32[]{:S(2)}) copy-start(bf16[2,12,6336]{2,0,1:T(2,128)(2,1)} %param.22) | copy-start | bytes 912388
  3.5 5.1 %copy-start.4 = (bf16[768,768]{1,0:T(8,128)(2,1)S(1)}, bf16[768,768]{1,0:T(8,128)(2,1)}, u32[]{:S(2)}) copy-start(bf16[768,768]{1,0:T(8,128)(2,1)} %weight_proj.5) | copy-start | bytes 3538948
  3.5 5.1 %copy-start.6 = (f32[768]{0:T(1024)S(1)}, f32[768]{0:T(1024)}, u32[]{:S(2)}) copy-start(f32[768]{0:T(1024)} %gain.5) | copy-start | bytes 9220
  3.5 5.1 %copy-start.7 = (bf16[144,768]{1,0:T(8,128)(2,1)S(1)}, bf16[144,768]{1,0:T(8,128)(2,1)}, u32[]{:S(2)}) copy-start(bf16[144,768]{1,0:T(8,128)(2,1)} %get-tuple-element.21.keep) | copy-start | bytes 663556
  3.5 5.0 %collective-permute-start = (bf16[144,768]{1,0:T(8,128)(2,1)}, bf16[144,768]{1,0:T(8,128)(2,1)S(1)}, u32[]{:S(2)}, u32[]{:S(2)}) collective-permute-start(bf16[144,768]{1,0:T(8,128)(2,1)} %get-tuple-element.22), channel_id=1, source_target_pairs={{0,1},{1,0},{2,3},{3,2},{4,5},{5,4},{6,7},{7,6},{8,9},{9,8},{10,11... | collective-permute-start | bytes 663560 | tf_op jit(solution)/shard_map/ppermute | solution.py:401
  6.8 2.0 %copy-start.2 = (bf16[768,2304]{1,0:T(8,128)(2,1)S(1)}, bf16[768,2304]{1,0:T(8,128)(2,1)}, u32[]{:S(2)}) copy-start(bf16[768,2304]{1,0:T(8,128)(2,1)} %weight_qkv.5) | copy-start | bytes 10616836
  8.8 12.4 %copy-start.8 = (bf16[2,12,6336]{2,0,1:T(2,128)(2,1)S(1)}, bf16[2,12,6336]{2,0,1:T(2,128)(2,1)}, u32[]{:S(2)}) copy-start(bf16[2,12,6336]{2,0,1:T(2,128)(2,1)} %param.26) | copy-start | bytes 912388
  11.0 19.1 %copy-start.1 = (bf16[768,2304]{1,0:T(8,128)(2,1)S(1)}, bf16[768,2304]{1,0:T(8,128)(2,1)}, u32[]{:S(2)}) copy-start(bf16[768,2304]{1,0:T(8,128)(2,1)} %weight_qkv.4) | copy-start | bytes 10616836
  11.1 19.1 %copy-start.3 = (bf16[768,768]{1,0:T(8,128)(2,1)S(1)}, bf16[768,768]{1,0:T(8,128)(2,1)}, u32[]{:S(2)}) copy-start(bf16[768,768]{1,0:T(8,128)(2,1)} %weight_proj.4) | copy-start | bytes 3538948
  11.1 19.1 %copy-start.5 = (f32[768]{0:T(1024)S(1)}, f32[768]{0:T(1024)}, u32[]{:S(2)}) copy-start(f32[768]{0:T(1024)} %gain.4) | copy-start | bytes 9220
  11.1 11.6 %collective-permute-start.1 = (bf16[72,768]{1,0:T(8,128)(2,1)S(1)}, bf16[72,768]{1,0:T(8,128)(2,1)S(1)}, u32[]{:S(2)}, u32[]{:S(2)}) collective-permute-start(bf16[72,768]{1,0:T(8,128)(2,1)S(1)} %get-tuple-element.25), channel_id=1, source_target_pairs={{0,126},{1,3},{2,0},{3,5},{4,2},{5,7},{6,4},{7,9},{8,6},{9,11},{10... | collective-permute-start | bytes 331784 | tf_op jit(solution)/shard_map/ppermute | solution.py:367
  11.2 12.3 %collective-permute-start.2 = (bf16[72,768]{1,0:T(8,128)(2,1)S(1)}, bf16[72,768]{1,0:T(8,128)(2,1)S(1)}, u32[]{:S(2)}, u32[]{:S(2)}) collective-permute-start(bf16[72,768]{1,0:T(8,128)(2,1)S(1)} %get-tuple-element.26), channel_id=1, source_target_pairs={{0,129},{1,0},{2,131},{3,2},{4,133},{5,4},{6,135},{7,6},{8,137},{9... | collective-permute-start | bytes 331784 | tf_op jit(solution)/shard_map/ppermute | solution.py:367
  20.5 9.6 %collective-permute-start.3 = (bf16[72,768]{1,0:T(8,128)(2,1)S(1)}, bf16[72,768]{1,0:T(8,128)(2,1)S(1)}, u32[]{:S(2)}, u32[]{:S(2)}) collective-permute-start(bf16[72,768]{1,0:T(8,128)(2,1)S(1)} %get-tuple-element.27), channel_id=1, source_target_pairs={{0,131},{1,126},{2,133},{3,0},{4,135},{5,2},{6,137},{7,4},{8,139},... | collective-permute-start | bytes 331784 | tf_op jit(solution)/shard_map/ppermute | solution.py:367
  36.2 4.0 %collective-permute-start.4 = (bf16[72,768]{1,0:T(8,128)(2,1)S(1)}, bf16[72,768]{1,0:T(8,128)(2,1)S(1)}, u32[]{:S(2)}, u32[]{:S(2)}) collective-permute-start(bf16[72,768]{1,0:T(8,128)(2,1)S(1)} %get-tuple-element.30), channel_id=1, source_target_pairs={{126,0},{3,1},{0,2},{5,3},{2,4},{7,5},{4,6},{9,7},{6,8},{11,9},{8,... | collective-permute-start | bytes 331784 | tf_op jit(solution)/shard_map/ppermute | solution.py:367
  36.3 3.9 %collective-permute-start.5 = (bf16[72,768]{1,0:T(8,128)(2,1)S(1)}, bf16[72,768]{1,0:T(8,128)(2,1)S(1)}, u32[]{:S(2)}, u32[]{:S(2)}) collective-permute-start(bf16[72,768]{1,0:T(8,128)(2,1)S(1)} %get-tuple-element.31), channel_id=1, source_target_pairs={{129,0},{0,1},{131,2},{2,3},{133,4},{4,5},{135,6},{6,7},{137,8},{8... | collective-permute-start | bytes 331784 | tf_op jit(solution)/shard_map/ppermute | solution.py:367
  36.4 10.0 %collective-permute-start.6 = (bf16[72,768]{1,0:T(8,128)(2,1)S(1)}, bf16[72,768]{1,0:T(8,128)(2,1)S(1)}, u32[]{:S(2)}, u32[]{:S(2)}) collective-permute-start(bf16[72,768]{1,0:T(8,128)(2,1)S(1)} %get-tuple-element.32), channel_id=1, source_target_pairs={{131,0},{126,1},{133,2},{0,3},{135,4},{2,5},{137,6},{4,7},{139,8},... | collective-permute-start | bytes 331784 | tf_op jit(solution)/shard_map/ppermute | solution.py:367
  50.3 1.6 %collective-permute-start.7 = (bf16[144,768]{1,0:T(8,128)(2,1)S(1)}, bf16[144,768]{1,0:T(8,128)(2,1)S(1)}, u32[]{:S(2)}, u32[]{:S(2)}) collective-permute-start(bf16[144,768]{1,0:T(8,128)(2,1)S(1)} %get-tuple-element.37), channel_id=1, source_target_pairs={{0,1},{1,0},{2,3},{3,2},{4,5},{5,4},{6,7},{7,6},{8,9},{9,8},{10,11... | collective-permute-start | bytes 663560 | tf_op jit(solution)/shard_map/ppermute | solution.py:429

commit v3 on v2

--- a/solution.py
+++ b/solution.py
@@ -242,8 +242,14 @@
     return [array[index * QUAD : (index + 1) * QUAD] for index in range(4)]
 
 
-QUARTERS_ONE = ((3, 1), (1, 3), (0, 2), (2, 0))
-QUARTERS_TWO = ((0, 2), (2, 0), (1, 3), (3, 1))
+QUARTERS_ONE = ((1, 3), (3, 1), (2, 0), (0, 2))
+QUARTERS_TWO = ((2, 0), (0, 2), (3, 1), (1, 3))
+FORTH = (1, 0, 2)
+BACK = (0, 1, 2)
+
+
+def ordered(quarters, order):
+    return quarters[:1] + tuple(quarters[1 + number] for number in order)
 
 
 def deal(quarters, c, refs, above, below):
@@ -287,44 +293,49 @@
     qkv[...] = dot(h, weight_qkv[...]).astype(bf16)
     attend(qkv, bias, probs, mixed)
     middle = u + dot(mixed[...], weight_proj[...])
-    deal(QUARTERS_ONE, c, (stay, first, second, third), middle, g)
+    deal(ordered(QUARTERS_ONE, FORTH), c, (stay, first, second, third), middle, g)
 
 
 def two_kernel(
-    stay, first, second, third, gain, weight_qkv, weight_proj, bias,
+    stay, first, second, third, gain, weight_qkv, weight_proj, weight_qkv_t, weight_proj_t, bias,
     back_stay, back_first, back_second, back_third,
     qkv, probs, mixed, grad_mixed, grad_qkv,
 ):
     c = parity()
-    u, g = gather(QUARTERS_TWO, c, (stay, first, second, third))
+    u, g = gather(ordered(QUARTERS_TWO, FORTH), c, (stay, first, second, third))
     normed, inverse = norm(u)
     h = (normed * row(gain)).astype(bf16)
     qkv[...] = dot(h, weight_qkv[...]).astype(bf16)
     attend(qkv, bias, probs, mixed)
     turned = u + dot(mixed[...], weight_proj[...])
-    grad_mixed[...] = dot_t(g.astype(bf16), weight_proj[...]).astype(bf16)
+    grad_mixed[...] = dot(g.astype(bf16), weight_proj_t[...]).astype(bf16)
     attend_back(qkv, probs, grad_mixed, grad_qkv)
-    dh = dot_t(grad_qkv[...], weight_qkv[...])
+    dh = dot(grad_qkv[...], weight_qkv_t[...])
     du = g + norm_back(dh, row(gain), normed, inverse)
-    deal(QUARTERS_TWO, c, (back_stay, back_first, back_second, back_third), du, turned)
+    deal(ordered(QUARTERS_TWO, BACK), c, (back_stay, back_first, back_second, back_third), du, turned)
 
 
 def three_kernel(
-    stay, first, second, third, u, qkv, probs, gain, weight_qkv, weight_proj,
+    stay, first, second, third, u, qkv, probs, gain, weight_qkv_t, weight_proj_t,
     keep, send, grad_mixed, grad_qkv,
 ):
     c = parity()
-    g, turned = gather(QUARTERS_ONE, c, (stay, first, second, third))
+    g, turned = gather(ordered(QUARTERS_ONE, BACK), c, (stay, first, second, third))
     normed, inverse = norm(u[...].astype(f32))
-    grad_mixed[...] = dot_t(g.astype(bf16), weight_proj[...]).astype(bf16)
+    grad_mixed[...] = dot(g.astype(bf16), weight_proj_t[...]).astype(bf16)
     attend_back(qkv, probs, grad_mixed, grad_qkv)
-    dh = dot_t(grad_qkv[...], weight_qkv[...])
+    dh = dot(grad_qkv[...], weight_qkv_t[...])
     du = g + norm_back(dh, row(gain), normed, inverse)
     mine = c == 0
     low = jnp.concatenate([du[:HALF], turned[:HALF]], axis=0)
     high = jnp.concatenate([du[HALF:], turned[HALF:]], axis=0)
     keep[...] = jnp.where(mine, low, high).astype(bf16)
     send[...] = jnp.where(mine, high, low).astype(bf16)
+
+
+def turn_kernel(weight_qkv, weight_proj, qkv_t, proj_t):
+    qkv_t[...] = weight_qkv[...].T
+    proj_t[...] = weight_proj[...].T
 
 
 def shape(*dims, dtype=bf16):
@@ -354,9 +365,9 @@
     for a in range(lats):
         for p in range(lons // 2):
             even, odd = (
-                (device(a, p - 1, 0), device(a, p + 1, 1)),
+                (device(a, p + 1, 0), device(a, p - 1, 1)),
                 (device(a - 1, p, 1), device(a, p, 0)),
-                (device(a - 1, p + 1, 1), device(a, p - 1, 0)),
+                (device(a - 1, p - 1, 1), device(a, p + 1, 0)),
             )[number]
             pairs += [(device(a, p, 0), even), (device(a, p, 1), odd)]
     return [(target, source) for source, target in pairs] if back else pairs
@@ -365,7 +376,7 @@
 def exchanged(values, back):
     return [
         lax.ppermute(value, ("lat", "lon"), exchange(number, back))
-        for number, value in enumerate(values)
+        for number, value in zip(BACK if back else FORTH, values)
     ]
 
 
@@ -414,17 +425,22 @@
         [narrow], 16, 3.0,
         keep, received, gain_one, qkv_one, proj_one, bias_of(table_one, False),
     )
-    table_two, stay = lax.optimization_barrier((table_two, stay))
+    table_two, qkv_now, stay = lax.optimization_barrier((table_two, qkv_two, stay))
+    turned_shapes = (shape(3 * D, D), shape(D, D))
+    qkv_two_t, proj_two_t = call(turn_kernel, turned_shapes, [], 14, 1.5, qkv_now, proj_two)
     arrived = exchanged(leave, False)
     stay, *leave = call(
         two_kernel, (quad, quad, quad, quad),
         [wide, pltpu.VMEM((HEADS, TOKENS, TOKENS), bf16), narrow, narrow, wide], 16, 8.0,
-        stay, *arrived, gain_two, qkv_two, proj_two, bias_of(table_two, True),
+        stay, *arrived, gain_two, qkv_two, proj_two, qkv_two_t, proj_two_t,
+        bias_of(table_two, True),
     )
     arrived = exchanged(leave, True)
+    qkv_now, stay = lax.optimization_barrier((qkv_one, stay))
+    qkv_one_t, proj_one_t = call(turn_kernel, turned_shapes, [], 14, 1.5, qkv_now, proj_one)
     keep, send = call(
         three_kernel, (tokens, tokens), [narrow, wide], 16, 6.0,
-        stay, *arrived, u_one, saved_qkv, saved_probs, gain_one, qkv_one, proj_one,
+        stay, *arrived, u_one, saved_qkv, saved_probs, gain_one, qkv_one_t, proj_one_t,
     )
     received = lax.ppermute(send, "lon", swap)
     output, grad = call(unpack_kernel, (tokens, tokens), [], 8, 1.0, keep, received)

time: 53 us -> 47.3 us (0.89)
  waiting for transfers between devices: 17.3 us -> 9.2 us
  starting transfers between devices: 15.3 us -> 16.8 us
  Pallas kernels: 18.7 us -> 19.6 us
    ppermute x6, waiting for transfers between devices: 15.8 us -> 8.09 us  [exchanged(): lax.ppermute(value, ('lat', 'lon'), exchange(number, back))]
    ppermute x2, starting transfers between devices: 3.42 us -> 5.34 us  [body(): received = lax.ppermute(send, 'lon', swap)]
    pallas_call x7 -> x9, Pallas kernels: 18.7 us -> 19.6 us  [call(): pl.pallas_call(kernel, out_shape=outs, scratch_shapes=scratch, compiler_p...]
  transfers between devices with their start and end apart: 8 -> 8, of which waited for: 5 -> 3; matrix products, arithmetic and copies ran while one was open for 1% -> 1% of each run, Pallas kernels for 5% -> 11%
where the time goes in v3:
time: 47.3 us; the launch traced here: 47.2 us
  Pallas kernels  19.6 us (41%)
  starting transfers between devices  16.8 us (36%)
  waiting for transfers between devices  9.2 us (19%)
  between operations  0.85 us (2%)
  local copies, waits for them, and re-layouts  0.72 us (2%)
    pallas_call x9, Pallas kernels, call(): pl.pallas_call(kernel, out_shape=outs, scratch_shapes=scratch, compiler_p...  19.6 us
    ppermute x6, starting transfers between devices, exchanged(): lax.ppermute(value, ('lat', 'lon'), exchange(number, back))  11.5 us
    ppermute x6, waiting for transfers between devices, exchanged(): lax.ppermute(value, ('lat', 'lon'), exchange(number, back))  8.09 us
    ppermute x2, starting transfers between devices, body(): received = lax.ppermute(send, 'lon', swap)  5.34 us
    ppermute x2, waiting for transfers between devices, body(): received = lax.ppermute(send, 'lon', swap)  1.11 us
  transfers between devices with their start and end apart: 8, of which 3 were waited for; matrix products, arithmetic and copies ran while one was open for 1% of the time, Pallas kernels for 11%

profile of v3, /device:TPU:1, one launch (start us, length us, event | category | flops | bytes accessed | tf_op | source)
XLA Modules:
  0.0 47.2 jit_solution(13314079939730549316)
XLA Ops:
  0.6 0.0 copy-start
  0.6 2.8 %shard_map.149 = (bf16[144,768]{1,0:T(8,128)(2,1)}, bf16[144,768]{1,0:T(8,128)(2,1)}) custom-call(bf16[144,768]{1,0:T(8,128)(2,1)} %bitcast.20, s32[3,24]{1,0:T(4,128)} %bitcast.22, s32[3,24]{1,0:T(4,128)} %bitcast.23, f32[768]{0:T(1024)} %vector_at.1, f32[8,768]{1,0:T(8,128)} %table_at.1, bf16[144,768]{1,0:T(8,128)(2,1)} %bitcast.21), custom_call_target="tpu_custom_call" | custom-call | flops 3000000000 | bytes 9000000 | tf_op jit(solution)/shard_map/pallas_call | solution.py:346
  3.5 0.0 copy-start.4
  3.5 0.0 copy-start.6
  3.5 0.0 copy-start.7
  3.5 3.3 %collective-permute-start = (bf16[144,768]{1,0:T(8,128)(2,1)}, bf16[144,768]{1,0:T(8,128)(2,1)S(1)}, u32[]{:S(2)}, u32[]{:S(2)}) collective-permute-start(bf16[144,768]{1,0:T(8,128)(2,1)} %get-tuple-element.29), channel_id=1, source_target_pairs={{0,1},{1,0},{2,3},{3,2},{4,5},{5,4},{6,7},{7,6},{8,9},{9,8},{10,11... | collective-permute-start | bytes 663560 | tf_op jit(solution)/shard_map/ppermute | solution.py:412
  6.8 0.0 copy-done
  6.8 0.0 copy-start.2
  6.8 0.3 constant_dynamic-slice_fusion
  7.2 1.3 %shard_map.150.bias = bf16[12,144,144]{2,1,0:T(8,128)(2,1)S(1)} custom-call(bf16[12,6336]{1,0:T(8,128)(2,1)S(1)} %bitcast.19), custom_call_target="tpu_custom_call" | custom-call | flops 1500000000 | bytes 4500000 | tf_op jit(solution)/shard_map/pallas_call | solution.py:346
  8.6 0.0 collective-permute-done.received
  8.6 0.0 copy-done.4
  8.6 0.0 copy-done.6
  8.6 0.0 copy-done.7
  8.6 0.2 copy-done.2
  8.8 0.0 copy-start.8
  8.8 2.2 %shard_map.151 = (bf16[72,768]{1,0:T(8,128)(2,1)S(1)}, bf16[72,768]{1,0:T(8,128)(2,1)S(1)}, bf16[72,768]{1,0:T(8,128)(2,1)S(1)}, bf16[72,768]{1,0:T(8,128)(2,1)S...) custom-call(bf16[144,768]{1,0:T(8,128)(2,1)S(1)} %copy-done.7, ...), custom_call_target="tpu_custom_call" | custom-call | flops 3000000000 | bytes 9000000 | tf_op jit(solution)/shard_map/pallas_call | solution.py:346
  11.0 0.0 copy-start.1
  11.1 0.0 copy-start.3
  11.1 0.4 collective-permute-start.1
  11.5 8.8 %collective-permute-start.2 = (bf16[72,768]{1,0:T(8,128)(2,1)S(1)}, bf16[72,768]{1,0:T(8,128)(2,1)S(1)}, u32[]{:S(2)}, u32[]{:S(2)}) collective-permute-start(bf16[72,768]{1,0:T(8,128)(2,1)S(1)} %get-tuple-element.33), channel_id=1, source_target_pairs={{0,2},{1,127},{2,4},{3,1},{4,6},{5,3},{6,8},{7,5},{8,10},{9,7},{10... | collective-permute-start | bytes 331784 | tf_op jit(solution)/shard_map/ppermute | solution.py:378
  20.2 0.0 collective-permute-start.3
  20.2 0.0 copy-done.8
  20.3 1.3 %shard_map.153.bias = bf16[12,144,144]{2,1,0:T(8,128)(2,1)S(1)} custom-call(bf16[12,6336]{1,0:T(8,128)(2,1)S(1)} %dynamic-slice_bitcast_fusion.table), custom_call_target="tpu_custom_call" | custom-call | flops 1500000000 | bytes 4500000 | tf_op jit(solution)/shard_map/pallas_call | solution.py:346
  21.7 0.0 copy-done.1
  21.7 0.0 copy-done.3
  21.7 0.0 copy-start.5
  21.7 1.3 %shard_map.152 = (bf16[2304,768]{1,0:T(8,128)(2,1)S(1)}, bf16[768,768]{1,0:T(8,128)(2,1)S(1)}) custom-call(bf16[768,2304]{1,0:T(8,128)(2,1)S(1)} %copy-done.1, bf16[768,768]{1,0:T(8,128)(2,1)S(1)} %copy-done.3), custom_call_target="tpu_custom_call" | custom-call | flops 1500000000 | bytes 4500000 | tf_op jit(solution)/shard_map/pallas_call | solution.py:346
  23.0 0.0 collective-permute-done.1.first
  23.0 0.0 collective-permute-done.2.second
  23.0 2.3 %collective-permute-done.3.third = bf16[72,768]{1,0:T(8,128)(2,1)S(1)} collective-permute-done((bf16[72,768]{1,0:T(8,128)(2,1)S(1)}, bf16[72,768]{1,0:T(8,128)(2,1)S(1)}, u32[]{:S(2)}, u32[]{:S(2)}) %collective-permute-start.3) | collective-permute-done | bytes 110624 | tf_op jit(solution)/shard_map/ppermute | solution.py:378
  25.3 0.0 copy-done.5
  25.3 5.2 %shard_map.154 = (bf16[72,768]{1,0:T(8,128)(2,1)S(1)}, bf16[72,768]{1,0:T(8,128)(2,1)S(1)}, bf16[72,768]{1,0:T(8,128)(2,1)S(1)}, bf16[72,768]{1,0:T(8,128)(2,1)S(1)}) custom-call(bf16[72,768]{1,0:T(8,128)(2,1)S(1)} %get-tuple-element.31.stay, bf16[72,768]{1,0:T(8,128)(2,1)S(1)} %collective-permute-done.1.first, ...), custom_call_target="tpu_custom_call" | custom-call | flops 8000000000 | bytes 24000000 | tf_op jit(solution)/shard_map/pallas_call | solution.py:346
  30.5 0.1 collective-permute-start.4
  30.6 1.5 %collective-permute-start.5 = (bf16[72,768]{1,0:T(8,128)(2,1)S(1)}, bf16[72,768]{1,0:T(8,128)(2,1)S(1)}, u32[]{:S(2)}, u32[]{:S(2)}) collective-permute-start(bf16[72,768]{1,0:T(8,128)(2,1)S(1)} %get-tuple-element.42), channel_id=1, source_target_pairs={{129,0},{0,1},{131,2},{2,3},{133,4},{4,5},{135,6},{6,7},{137,8},{8... | collective-permute-start | bytes 331784 | tf_op jit(solution)/shard_map/ppermute | solution.py:378
  32.1 0.7 %collective-permute-start.6 = (bf16[72,768]{1,0:T(8,128)(2,1)S(1)}, bf16[72,768]{1,0:T(8,128)(2,1)S(1)}, u32[]{:S(2)}, u32[]{:S(2)}) collective-permute-start(bf16[72,768]{1,0:T(8,128)(2,1)S(1)} %get-tuple-element.43), channel_id=1, source_target_pairs={{255,0},{2,1},{129,2},{4,3},{131,4},{6,5},{133,6},{8,7},{135,8},{1... | collective-permute-start | bytes 331784 | tf_op jit(solution)/shard_map/ppermute | solution.py:378
  32.8 1.3 %shard_map.155 = (bf16[2304,768]{1,0:T(8,128)(2,1)S(1)}, bf16[768,768]{1,0:T(8,128)(2,1)S(1)}) custom-call(bf16[768,2304]{1,0:T(8,128)(2,1)S(1)} %copy-done.2, bf16[768,768]{1,0:T(8,128)(2,1)S(1)} %copy-done.4), custom_call_target="tpu_custom_call" | custom-call | flops 1500000000 | bytes 4500000 | tf_op jit(solution)/shard_map/pallas_call | solution.py:346
  34.1 5.8 %collective-permute-done.4.first = bf16[72,768]{1,0:T(8,128)(2,1)S(1)} collective-permute-done((bf16[72,768]{1,0:T(8,128)(2,1)S(1)}, bf16[72,768]{1,0:T(8,128)(2,1)S(1)}, u32[]{:S(2)}, u32[]{:S(2)}) %collective-permute-start.4) | collective-permute-done | bytes 110624 | tf_op jit(solution)/shard_map/ppermute | solution.py:378
  39.9 0.0 collective-permute-done.5.second
  39.9 0.0 collective-permute-done.6.third
  39.9 3.2 %shard_map.156 = (bf16[144,768]{1,0:T(8,128)(2,1)S(1)}, bf16[144,768]{1,0:T(8,128)(2,1)S(1)}) custom-call(bf16[72,768]{1,0:T(8,128)(2,1)S(1)} %get-tuple-element.40.stay, bf16[72,768]{1,0:T(8,128)(2,1)S(1)} %collective-permute-done.4.first, bf16[72,768]{1,0:T(8,128)(2,1)S(1)} %collective-permute-done.5.second, ...), custom_call_target="tpu_custom_call" | custom-call | flops 6000000000 | bytes 18000000 | tf_op jit(solution)/shard_map/pallas_call | solution.py:346
  43.1 2.0 %collective-permute-start.7 = (bf16[144,768]{1,0:T(8,128)(2,1)S(1)}, bf16[144,768]{1,0:T(8,128)(2,1)S(1)}, u32[]{:S(2)}, u32[]{:S(2)}) collective-permute-start(bf16[144,768]{1,0:T(8,128)(2,1)S(1)} %get-tuple-element.51), channel_id=1, source_target_pairs={{0,1},{1,0},{2,3},{3,2},{4,5},{5,4},{6,7},{7,6},{8,9},{9,8},{10,11... | collective-permute-start | bytes 663560 | tf_op jit(solution)/shard_map/ppermute | solution.py:445
  45.1 1.1 %collective-permute-done.7.received = bf16[144,768]{1,0:T(8,128)(2,1)S(1)} collective-permute-done((bf16[144,768]{1,0:T(8,128)(2,1)S(1)}, bf16[144,768]{1,0:T(8,128)(2,1)S(1)}, u32[]{:S(2)}, u32[]{:S(2)}) %collective-permute-start.7) | collective-permute-done | bytes 221216 | tf_op jit(solution)/shard_map/ppermute | solution.py:445
  46.2 1.0 %shard_map.157 = (bf16[144,768]{1,0:T(8,128)(2,1)}, bf16[144,768]{1,0:T(8,128)(2,1)}) custom-call(bf16[144,768]{1,0:T(8,128)(2,1)S(1)} %get-tuple-element.50.keep, bf16[144,768]{1,0:T(8,128)(2,1)S(1)} %collective-permute-done.7.received), custom_call_target="tpu_custom_call" | custom-call | flops 1000000000 | bytes 3000000 | tf_op jit(solution)/shard_map/pallas_call | solution.py:346
  (3 shorter events, 0.1 us)
Async XLA Ops:
  0.6 6.2 %copy-start = (bf16[2,12,6336]{2,0,1:T(2,128)(2,1)S(1)}, bf16[2,12,6336]{2,0,1:T(2,128)(2,1)}, u32[]{:S(2)}) copy-start(bf16[2,12,6336]{2,0,1:T(2,128)(2,1)} %param.22) | copy-start | bytes 912388
  3.5 5.1 %copy-start.4 = (bf16[768,768]{1,0:T(8,128)(2,1)S(1)}, bf16[768,768]{1,0:T(8,128)(2,1)}, u32[]{:S(2)}) copy-start(bf16[768,768]{1,0:T(8,128)(2,1)} %weight_proj.7) | copy-start | bytes 3538948
  3.5 5.1 %copy-start.6 = (f32[768]{0:T(1024)S(1)}, f32[768]{0:T(1024)}, u32[]{:S(2)}) copy-start(f32[768]{0:T(1024)} %gain.5) | copy-start | bytes 9220
  3.5 5.1 %copy-start.7 = (bf16[144,768]{1,0:T(8,128)(2,1)S(1)}, bf16[144,768]{1,0:T(8,128)(2,1)}, u32[]{:S(2)}) copy-start(bf16[144,768]{1,0:T(8,128)(2,1)} %get-tuple-element.28.keep) | copy-start | bytes 663556
  3.5 5.0 %collective-permute-start = (bf16[144,768]{1,0:T(8,128)(2,1)}, bf16[144,768]{1,0:T(8,128)(2,1)S(1)}, u32[]{:S(2)}, u32[]{:S(2)}) collective-permute-start(bf16[144,768]{1,0:T(8,128)(2,1)} %get-tuple-element.29), channel_id=1, source_target_pairs={{0,1},{1,0},{2,3},{3,2},{4,5},{5,4},{6,7},{7,6},{8,9},{9,8},{10,11... | collective-permute-start | bytes 663560 | tf_op jit(solution)/shard_map/ppermute | solution.py:412
  6.8 2.0 %copy-start.2 = (bf16[768,2304]{1,0:T(8,128)(2,1)S(1)}, bf16[768,2304]{1,0:T(8,128)(2,1)}, u32[]{:S(2)}) copy-start(bf16[768,2304]{1,0:T(8,128)(2,1)} %weight_qkv.5) | copy-start | bytes 10616836
  8.8 11.4 %copy-start.8 = (bf16[2,12,6336]{2,0,1:T(2,128)(2,1)S(1)}, bf16[2,12,6336]{2,0,1:T(2,128)(2,1)}, u32[]{:S(2)}) copy-start(bf16[2,12,6336]{2,0,1:T(2,128)(2,1)} %param.26) | copy-start | bytes 912388
  11.0 10.6 %copy-start.1 = (bf16[768,2304]{1,0:T(8,128)(2,1)S(1)}, bf16[768,2304]{1,0:T(8,128)(2,1)}, u32[]{:S(2)}) copy-start(bf16[768,2304]{1,0:T(8,128)(2,1)} %weight_qkv.4) | copy-start | bytes 10616836
  11.1 10.6 %copy-start.3 = (bf16[768,768]{1,0:T(8,128)(2,1)S(1)}, bf16[768,768]{1,0:T(8,128)(2,1)}, u32[]{:S(2)}) copy-start(bf16[768,768]{1,0:T(8,128)(2,1)} %weight_proj.6) | copy-start | bytes 3538948
  11.1 11.9 %collective-permute-start.1 = (bf16[72,768]{1,0:T(8,128)(2,1)S(1)}, bf16[72,768]{1,0:T(8,128)(2,1)S(1)}, u32[]{:S(2)}, u32[]{:S(2)}) collective-permute-start(bf16[72,768]{1,0:T(8,128)(2,1)S(1)} %get-tuple-element.32), channel_id=1, source_target_pairs={{0,129},{1,0},{2,131},{3,2},{4,133},{5,4},{6,135},{7,6},{8,137},{9... | collective-permute-start | bytes 331784 | tf_op jit(solution)/shard_map/ppermute | solution.py:378
  11.5 11.5 %collective-permute-start.2 = (bf16[72,768]{1,0:T(8,128)(2,1)S(1)}, bf16[72,768]{1,0:T(8,128)(2,1)S(1)}, u32[]{:S(2)}, u32[]{:S(2)}) collective-permute-start(bf16[72,768]{1,0:T(8,128)(2,1)S(1)} %get-tuple-element.33), channel_id=1, source_target_pairs={{0,2},{1,127},{2,4},{3,1},{4,6},{5,3},{6,8},{7,5},{8,10},{9,7},{10... | collective-permute-start | bytes 331784 | tf_op jit(solution)/shard_map/ppermute | solution.py:378
  20.2 5.1 %collective-permute-start.3 = (bf16[72,768]{1,0:T(8,128)(2,1)S(1)}, bf16[72,768]{1,0:T(8,128)(2,1)S(1)}, u32[]{:S(2)}, u32[]{:S(2)}) collective-permute-start(bf16[72,768]{1,0:T(8,128)(2,1)S(1)} %get-tuple-element.34), channel_id=1, source_target_pairs={{0,255},{1,2},{2,129},{3,4},{4,131},{5,6},{6,133},{7,8},{8,135},{9... | collective-permute-start | bytes 331784 | tf_op jit(solution)/shard_map/ppermute | solution.py:378
  21.7 3.6 %copy-start.5 = (f32[768]{0:T(1024)S(1)}, f32[768]{0:T(1024)}, u32[]{:S(2)}) copy-start(f32[768]{0:T(1024)} %gain.4) | copy-start | bytes 9220
  30.5 9.4 %collective-permute-start.4 = (bf16[72,768]{1,0:T(8,128)(2,1)S(1)}, bf16[72,768]{1,0:T(8,128)(2,1)S(1)}, u32[]{:S(2)}, u32[]{:S(2)}) collective-permute-start(bf16[72,768]{1,0:T(8,128)(2,1)S(1)} %get-tuple-element.41), channel_id=1, source_target_pairs={{2,0},{127,1},{4,2},{1,3},{6,4},{3,5},{8,6},{5,7},{10,8},{7,9},{12... | collective-permute-start | bytes 331784 | tf_op jit(solution)/shard_map/ppermute | solution.py:378
  30.6 9.3 %collective-permute-start.5 = (bf16[72,768]{1,0:T(8,128)(2,1)S(1)}, bf16[72,768]{1,0:T(8,128)(2,1)S(1)}, u32[]{:S(2)}, u32[]{:S(2)}) collective-permute-start(bf16[72,768]{1,0:T(8,128)(2,1)S(1)} %get-tuple-element.42), channel_id=1, source_target_pairs={{129,0},{0,1},{131,2},{2,3},{133,4},{4,5},{135,6},{6,7},{137,8},{8... | collective-permute-start | bytes 331784 | tf_op jit(solution)/shard_map/ppermute | solution.py:378
  32.1 7.8 %collective-permute-start.6 = (bf16[72,768]{1,0:T(8,128)(2,1)S(1)}, bf16[72,768]{1,0:T(8,128)(2,1)S(1)}, u32[]{:S(2)}, u32[]{:S(2)}) collective-permute-start(bf16[72,768]{1,0:T(8,128)(2,1)S(1)} %get-tuple-element.43), channel_id=1, source_target_pairs={{255,0},{2,1},{129,2},{4,3},{131,4},{6,5},{133,6},{8,7},{135,8},{1... | collective-permute-start | bytes 331784 | tf_op jit(solution)/shard_map/ppermute | solution.py:378
  43.1 3.1 %collective-permute-start.7 = (bf16[144,768]{1,0:T(8,128)(2,1)S(1)}, bf16[144,768]{1,0:T(8,128)(2,1)S(1)}, u32[]{:S(2)}, u32[]{:S(2)}) collective-permute-start(bf16[144,768]{1,0:T(8,128)(2,1)S(1)} %get-tuple-element.51), channel_id=1, source_target_pairs={{0,1},{1,0},{2,3},{3,2},{4,5},{5,4},{6,7},{7,6},{8,9},{9,8},{10,11... | collective-permute-start | bytes 663560 | tf_op jit(solution)/shard_map/ppermute | solution.py:445

commit v4 on v3

--- a/solution.py
+++ b/solution.py
@@ -85,25 +85,20 @@
     for copy in copies:
         copy.wait()
     kinds = iota((OROG, 24), 0)
+    spare = jnp.zeros((7, D), f32)
+    rest = jnp.concatenate([orog_table[...], row(land_vector), spare], axis=0)
+    terms = []
+    for _ in range(3):
+        terms.append(rest.astype(bf16))
+        rest = rest - terms[-1].astype(f32)
+    terms = jnp.concatenate(terms, axis=0)
     added = []
     for w in range(3):
         onehot = (orography[w : w + 1, :] == kinds).astype(f32)
-        looked = lax.dot_general(
-            onehot,
-            orog_table[...],
-            (((0,), (0,)), ((), ())),
-            precision=lax.Precision.HIGHEST,
-            preferred_element_type=f32,
-        )
         share = land[w : w + 1, :].astype(f32) * (1.0 / LAND)
-        spread = lax.dot_general(
-            jnp.concatenate([share, jnp.zeros((7, 24), f32)], axis=0),
-            jnp.concatenate([row(land_vector), jnp.zeros((7, D), f32)], axis=0),
-            (((0,), (0,)), ((), ())),
-            precision=lax.Precision.HIGHEST,
-            preferred_element_type=f32,
-        )
-        added.append(spread + looked)
+        coded = jnp.concatenate([onehot, share, jnp.zeros((7, 24), f32)], axis=0)
+        coded = jnp.concatenate([coded, coded, coded], axis=0).astype(bf16)
+        added.append(t_dot(coded, terms))
     added = jnp.concatenate(added + added, axis=0)
     embedded = (stream[...].astype(f32) + added).astype(bf16)
     e = dot(move, embedded)
@@ -183,6 +178,11 @@
     )
 
 
+def four_masks(value):
+    lane = div(iota((1, 4 * DEPTH), 1), DEPTH)
+    return [jnp.where(lane == i, value, 0.0).astype(bf16) for i in range(4)]
+
+
 def attend(qkv, bias, probs, mixed):
     masks = lane_masks(DEPTH ** (-0.5))
     low = iota((TOKENS, 2 * DEPTH), 1) < DEPTH
@@ -205,30 +205,34 @@
 
 
 def attend_back(qkv, probs, grad_mixed, grad_qkv):
-    masks = lane_masks(1.0)
+    masks = four_masks(DEPTH ** (-0.5))
     low = iota((TOKENS, 2 * DEPTH), 1) < DEPTH
-    for pair in range(HEADS // 2):
-        at = pair * 2 * DEPTH
-        q2 = qkv[:, at : at + 128]
-        k2 = qkv[:, D + at : D + at + 128]
-        v2 = qkv[:, 2 * D + at : 2 * D + at + 128]
-        g2 = grad_mixed[:, at : at + 128]
-        both = dot_t(jnp.concatenate([v2 * masks[0], v2 * masks[1]], axis=0), g2)
-        ps, ds, ds_t = [], [], []
-        for side in range(2):
-            p = probs[pair * 2 + side]
-            wide = p.astype(f32)
-            dp = both[side * TOKENS : side * TOKENS + TOKENS]
-            inner = jnp.sum(wide * dp, axis=0, keepdims=True)
-            d = (wide * (dp - inner) * (DEPTH ** (-0.5))).astype(bf16)
-            ps.append(p)
-            ds.append(d)
-            ds_t.append(d.T)
-        for block, (lhs, rhs) in enumerate(((ds_t, k2), (ds, q2), (ps, g2))):
-            both = dot(jnp.concatenate(lhs, axis=0), rhs)
-            grad_qkv[:, block * D + at : block * D + at + 128] = jnp.where(
-                low, both[:TOKENS], both[TOKENS:]
-            ).astype(bf16)
+    for group in range(HEADS // 4):
+        first = group * 4 * DEPTH
+        v4 = qkv[:, 2 * D + first : 2 * D + first + 256]
+        g4 = grad_mixed[:, first : first + 256]
+        all_dp = dot_t(jnp.concatenate([v4 * mask for mask in masks], axis=0), g4)
+        for half in range(2):
+            at = first + 128 * half
+            q2 = qkv[:, at : at + 128]
+            k2 = qkv[:, D + at : D + at + 128]
+            g2 = grad_mixed[:, at : at + 128]
+            ps, ds, ds_t = [], [], []
+            for side in range(2):
+                n = 2 * half + side
+                p = probs[group * 4 + n]
+                wide = p.astype(f32)
+                dp = all_dp[n * TOKENS : n * TOKENS + TOKENS]
+                inner = jnp.sum(wide * dp, axis=0, keepdims=True)
+                d = (wide * (dp - inner)).astype(bf16)
+                ps.append(p)
+                ds.append(d)
+                ds_t.append(d.T)
+            for block, (lhs, rhs) in enumerate(((ds_t, k2), (ds, q2), (ps, g2))):
+                both = dot(jnp.concatenate(lhs, axis=0), rhs)
+                grad_qkv[:, block * D + at : block * D + at + 128] = jnp.where(
+                    low, both[:TOKENS], both[TOKENS:]
+                ).astype(bf16)
 
 
 def norm_back(dh, gain, normed, inverse):
@@ -245,7 +249,7 @@
 QUARTERS_ONE = ((1, 3), (3, 1), (2, 0), (0, 2))
 QUARTERS_TWO = ((2, 0), (0, 2), (3, 1), (1, 3))
 FORTH = (1, 0, 2)
-BACK = (0, 1, 2)
+BACK = (2, 0, 1)
 
 
 def ordered(quarters, order):

time: 47.3 us -> 44.7 us (0.945)
  waiting for transfers between devices: 9.2 us -> 5.89 us
  starting transfers between devices: 16.8 us -> 19.3 us
  Pallas kernels: 19.6 us -> 17.8 us
    ppermute x6, starting transfers between devices: 11.5 us -> 15.5 us  [exchanged(): lax.ppermute(value, ('lat', 'lon'), exchange(number, back))]
    ppermute x6, waiting for transfers between devices: 8.09 us -> 4.78 us  [exchanged(): lax.ppermute(value, ('lat', 'lon'), exchange(number, back))]
    pallas_call x9, Pallas kernels: 19.6 us -> 17.8 us  [call(): pl.pallas_call(kernel, out_shape=outs, scratch_shapes=scratch, compiler_p...]
    ppermute x2, starting transfers between devices: 5.34 us -> 3.86 us  [body(): received = lax.ppermute(send, 'lon', swap)]
  transfers between devices with their start and end apart: 8 -> 8, of which waited for: 3 -> 3; matrix products, arithmetic and copies ran while one was open for 1% -> 1% of each run, Pallas kernels for 11% -> 12%
where the time goes in v4:
time: 44.7 us; the launch traced here: 44.6 us
  starting transfers between devices  19.3 us (43%)
  Pallas kernels  17.8 us (40%)
  waiting for transfers between devices  5.89 us (13%)
  between operations  0.85 us (2%)
  local copies, waits for them, and re-layouts  0.72 us (2%)
    pallas_call x9, Pallas kernels, call(): pl.pallas_call(kernel, out_shape=outs, scratch_shapes=scratch, compiler_p...  17.8 us
    ppermute x6, starting transfers between devices, exchanged(): lax.ppermute(value, ('lat', 'lon'), exchange(number, back))  15.5 us
    ppermute x6, waiting for transfers between devices, exchanged(): lax.ppermute(value, ('lat', 'lon'), exchange(number, back))  4.78 us
    ppermute x2, starting transfers between devices, body(): received = lax.ppermute(send, 'lon', swap)  3.86 us
    ppermute x2, waiting for transfers between devices, body(): received = lax.ppermute(send, 'lon', swap)  1.11 us
  transfers between devices with their start and end apart: 8, of which 3 were waited for; matrix products, arithmetic and copies ran while one was open for 1% of the time, Pallas kernels for 12%

profile of v4, /device:TPU:1, one launch (start us, length us, event | category | flops | bytes accessed | tf_op | source)
XLA Modules:
  0.0 44.6 jit_solution(1235509803700484846)
XLA Ops:
  0.6 0.0 copy-start
  0.6 2.4 %shard_map.149 = (bf16[144,768]{1,0:T(8,128)(2,1)}, bf16[144,768]{1,0:T(8,128)(2,1)}) custom-call(bf16[144,768]{1,0:T(8,128)(2,1)} %bitcast.20, s32[3,24]{1,0:T(4,128)} %bitcast.22, s32[3,24]{1,0:T(4,128)} %bitcast.23, f32[768]{0:T(1024)} %vector_at.1, f32[8,768]{1,0:T(8,128)} %table_at.1, bf16[144,768]{1,0:T(8,128)(2,1)} %bitcast.21), custom_call_target="tpu_custom_call" | custom-call | flops 3000000000 | bytes 9000000 | tf_op jit(solution)/shard_map/pallas_call | solution.py:350
  3.0 0.0 copy-start.4
  3.0 0.0 copy-start.6
  3.0 0.0 copy-start.7
  3.1 3.3 %collective-permute-start = (bf16[144,768]{1,0:T(8,128)(2,1)}, bf16[144,768]{1,0:T(8,128)(2,1)S(1)}, u32[]{:S(2)}, u32[]{:S(2)}) collective-permute-start(bf16[144,768]{1,0:T(8,128)(2,1)} %get-tuple-element.29), channel_id=1, source_target_pairs={{0,1},{1,0},{2,3},{3,2},{4,5},{5,4},{6,7},{7,6},{8,9},{9,8},{10,11... | collective-permute-start | bytes 663560 | tf_op jit(solution)/shard_map/ppermute | solution.py:416
  6.4 0.0 copy-done
  6.4 0.0 copy-start.2
  6.4 0.3 constant_dynamic-slice_fusion
  6.8 1.3 %shard_map.150.bias = bf16[12,144,144]{2,1,0:T(8,128)(2,1)S(1)} custom-call(bf16[12,6336]{1,0:T(8,128)(2,1)S(1)} %bitcast.19), custom_call_target="tpu_custom_call" | custom-call | flops 1500000000 | bytes 4500000 | tf_op jit(solution)/shard_map/pallas_call | solution.py:350
  8.1 0.0 collective-permute-done.received
  8.1 0.0 copy-done.4
  8.1 0.0 copy-done.6
  8.1 0.0 copy-done.7
  8.1 0.2 copy-done.2
  8.4 0.0 copy-start.8
  8.4 2.2 %shard_map.151 = (bf16[72,768]{1,0:T(8,128)(2,1)S(1)}, bf16[72,768]{1,0:T(8,128)(2,1)S(1)}, bf16[72,768]{1,0:T(8,128)(2,1)S(1)}, bf16[72,768]{1,0:T(8,128)(2,1)S...) custom-call(bf16[144,768]{1,0:T(8,128)(2,1)S(1)} %copy-done.7, ...), custom_call_target="tpu_custom_call" | custom-call | flops 3000000000 | bytes 9000000 | tf_op jit(solution)/shard_map/pallas_call | solution.py:350
  10.6 0.0 copy-start.1
  10.6 0.0 copy-start.3
  10.6 0.4 collective-permute-start.1
  11.0 8.7 %collective-permute-start.2 = (bf16[72,768]{1,0:T(8,128)(2,1)S(1)}, bf16[72,768]{1,0:T(8,128)(2,1)S(1)}, u32[]{:S(2)}, u32[]{:S(2)}) collective-permute-start(bf16[72,768]{1,0:T(8,128)(2,1)S(1)} %get-tuple-element.33), channel_id=1, source_target_pairs={{0,2},{1,127},{2,4},{3,1},{4,6},{5,3},{6,8},{7,5},{8,10},{9,7},{10... | collective-permute-start | bytes 331784 | tf_op jit(solution)/shard_map/ppermute | solution.py:382
  19.8 0.0 collective-permute-start.3
  19.8 0.0 copy-done.8
  19.9 1.3 %shard_map.153.bias = bf16[12,144,144]{2,1,0:T(8,128)(2,1)S(1)} custom-call(bf16[12,6336]{1,0:T(8,128)(2,1)S(1)} %dynamic-slice_bitcast_fusion.table), custom_call_target="tpu_custom_call" | custom-call | flops 1500000000 | bytes 4500000 | tf_op jit(solution)/shard_map/pallas_call | solution.py:350
  21.2 0.0 copy-done.1
  21.2 0.0 copy-done.3
  21.2 0.0 copy-start.5
  21.2 1.3 %shard_map.152 = (bf16[2304,768]{1,0:T(8,128)(2,1)S(1)}, bf16[768,768]{1,0:T(8,128)(2,1)S(1)}) custom-call(bf16[768,2304]{1,0:T(8,128)(2,1)S(1)} %copy-done.1, bf16[768,768]{1,0:T(8,128)(2,1)S(1)} %copy-done.3), custom_call_target="tpu_custom_call" | custom-call | flops 1500000000 | bytes 4500000 | tf_op jit(solution)/shard_map/pallas_call | solution.py:350
  22.5 0.0 collective-permute-done.1.first
  22.6 0.0 collective-permute-done.2.second
  22.6 2.3 %collective-permute-done.3.third = bf16[72,768]{1,0:T(8,128)(2,1)S(1)} collective-permute-done((bf16[72,768]{1,0:T(8,128)(2,1)S(1)}, bf16[72,768]{1,0:T(8,128)(2,1)S(1)}, u32[]{:S(2)}, u32[]{:S(2)}) %collective-permute-start.3) | collective-permute-done | bytes 110624 | tf_op jit(solution)/shard_map/ppermute | solution.py:382
  24.9 0.0 copy-done.5
  24.9 4.4 %shard_map.154 = (bf16[72,768]{1,0:T(8,128)(2,1)S(1)}, bf16[72,768]{1,0:T(8,128)(2,1)S(1)}, bf16[72,768]{1,0:T(8,128)(2,1)S(1)}, bf16[72,768]{1,0:T(8,128)(2,1)S(1)}) custom-call(bf16[72,768]{1,0:T(8,128)(2,1)S(1)} %get-tuple-element.31.stay, bf16[72,768]{1,0:T(8,128)(2,1)S(1)} %collective-permute-done.1.first, ...), custom_call_target="tpu_custom_call" | custom-call | flops 8000000000 | bytes 24000000 | tf_op jit(solution)/shard_map/pallas_call | solution.py:350
  29.2 0.5 %collective-permute-start.4 = (bf16[72,768]{1,0:T(8,128)(2,1)S(1)}, bf16[72,768]{1,0:T(8,128)(2,1)S(1)}, u32[]{:S(2)}, u32[]{:S(2)}) collective-permute-start(bf16[72,768]{1,0:T(8,128)(2,1)S(1)} %get-tuple-element.41), channel_id=1, source_target_pairs={{255,0},{2,1},{129,2},{4,3},{131,4},{6,5},{133,6},{8,7},{135,8},{1... | collective-permute-start | bytes 331784 | tf_op jit(solution)/shard_map/ppermute | solution.py:382
  29.7 0.0 collective-permute-start.5
  29.7 5.8 %collective-permute-start.6 = (bf16[72,768]{1,0:T(8,128)(2,1)S(1)}, bf16[72,768]{1,0:T(8,128)(2,1)S(1)}, u32[]{:S(2)}, u32[]{:S(2)}) collective-permute-start(bf16[72,768]{1,0:T(8,128)(2,1)S(1)} %get-tuple-element.43), channel_id=1, source_target_pairs={{129,0},{0,1},{131,2},{2,3},{133,4},{4,5},{135,6},{6,7},{137,8},{8... | collective-permute-start | bytes 331784 | tf_op jit(solution)/shard_map/ppermute | solution.py:382
  35.5 1.3 %shard_map.155 = (bf16[2304,768]{1,0:T(8,128)(2,1)S(1)}, bf16[768,768]{1,0:T(8,128)(2,1)S(1)}) custom-call(bf16[768,2304]{1,0:T(8,128)(2,1)S(1)} %copy-done.2, bf16[768,768]{1,0:T(8,128)(2,1)S(1)} %copy-done.4), custom_call_target="tpu_custom_call" | custom-call | flops 1500000000 | bytes 4500000 | tf_op jit(solution)/shard_map/pallas_call | solution.py:350
  36.8 0.0 collective-permute-done.4.first
  36.8 2.5 %collective-permute-done.5.second = bf16[72,768]{1,0:T(8,128)(2,1)S(1)} collective-permute-done((bf16[72,768]{1,0:T(8,128)(2,1)S(1)}, bf16[72,768]{1,0:T(8,128)(2,1)S(1)}, u32[]{:S(2)}, u32[]{:S(2)}) %collective-permute-start.5) | collective-permute-done | bytes 110624 | tf_op jit(solution)/shard_map/ppermute | solution.py:382
  39.3 0.0 collective-permute-done.6.third
  39.3 2.7 %shard_map.156 = (bf16[144,768]{1,0:T(8,128)(2,1)S(1)}, bf16[144,768]{1,0:T(8,128)(2,1)S(1)}) custom-call(bf16[72,768]{1,0:T(8,128)(2,1)S(1)} %get-tuple-element.40.stay, bf16[72,768]{1,0:T(8,128)(2,1)S(1)} %collective-permute-done.4.first, bf16[72,768]{1,0:T(8,128)(2,1)S(1)} %collective-permute-done.5.second, ...), custom_call_target="tpu_custom_call" | custom-call | flops 6000000000 | bytes 18000000 | tf_op jit(solution)/shard_map/pallas_call | solution.py:350
  42.0 0.5 %collective-permute-start.7 = (bf16[144,768]{1,0:T(8,128)(2,1)S(1)}, bf16[144,768]{1,0:T(8,128)(2,1)S(1)}, u32[]{:S(2)}, u32[]{:S(2)}) collective-permute-start(bf16[144,768]{1,0:T(8,128)(2,1)S(1)} %get-tuple-element.51), channel_id=1, source_target_pairs={{0,1},{1,0},{2,3},{3,2},{4,5},{5,4},{6,7},{7,6},{8,9},{9,8},{10,11... | collective-permute-start | bytes 663560 | tf_op jit(solution)/shard_map/ppermute | solution.py:449
  42.5 1.1 %collective-permute-done.7.received = bf16[144,768]{1,0:T(8,128)(2,1)S(1)} collective-permute-done((bf16[144,768]{1,0:T(8,128)(2,1)S(1)}, bf16[144,768]{1,0:T(8,128)(2,1)S(1)}, u32[]{:S(2)}, u32[]{:S(2)}) %collective-permute-start.7) | collective-permute-done | bytes 221216 | tf_op jit(solution)/shard_map/ppermute | solution.py:449
  43.6 1.0 %shard_map.157 = (bf16[144,768]{1,0:T(8,128)(2,1)}, bf16[144,768]{1,0:T(8,128)(2,1)}) custom-call(bf16[144,768]{1,0:T(8,128)(2,1)S(1)} %get-tuple-element.50.keep, bf16[144,768]{1,0:T(8,128)(2,1)S(1)} %collective-permute-done.7.received), custom_call_target="tpu_custom_call" | custom-call | flops 1000000000 | bytes 3000000 | tf_op jit(solution)/shard_map/pallas_call | solution.py:350
  (3 shorter events, 0.1 us)
Async XLA Ops:
  0.6 5.8 %copy-start = (bf16[2,12,6336]{2,0,1:T(2,128)(2,1)S(1)}, bf16[2,12,6336]{2,0,1:T(2,128)(2,1)}, u32[]{:S(2)}) copy-start(bf16[2,12,6336]{2,0,1:T(2,128)(2,1)} %param.22) | copy-start | bytes 912388
  3.0 5.1 %copy-start.4 = (bf16[768,768]{1,0:T(8,128)(2,1)S(1)}, bf16[768,768]{1,0:T(8,128)(2,1)}, u32[]{:S(2)}) copy-start(bf16[768,768]{1,0:T(8,128)(2,1)} %weight_proj.7) | copy-start | bytes 3538948
  3.0 5.1 %copy-start.6 = (f32[768]{0:T(1024)S(1)}, f32[768]{0:T(1024)}, u32[]{:S(2)}) copy-start(f32[768]{0:T(1024)} %gain.5) | copy-start | bytes 9220
  3.0 5.1 %copy-start.7 = (bf16[144,768]{1,0:T(8,128)(2,1)S(1)}, bf16[144,768]{1,0:T(8,128)(2,1)}, u32[]{:S(2)}) copy-start(bf16[144,768]{1,0:T(8,128)(2,1)} %get-tuple-element.28.keep) | copy-start | bytes 663556
  3.1 5.0 %collective-permute-start = (bf16[144,768]{1,0:T(8,128)(2,1)}, bf16[144,768]{1,0:T(8,128)(2,1)S(1)}, u32[]{:S(2)}, u32[]{:S(2)}) collective-permute-start(bf16[144,768]{1,0:T(8,128)(2,1)} %get-tuple-element.29), channel_id=1, source_target_pairs={{0,1},{1,0},{2,3},{3,2},{4,5},{5,4},{6,7},{7,6},{8,9},{9,8},{10,11... | collective-permute-start | bytes 663560 | tf_op jit(solution)/shard_map/ppermute | solution.py:416
  6.4 2.0 %copy-start.2 = (bf16[768,2304]{1,0:T(8,128)(2,1)S(1)}, bf16[768,2304]{1,0:T(8,128)(2,1)}, u32[]{:S(2)}) copy-start(bf16[768,2304]{1,0:T(8,128)(2,1)} %weight_qkv.5) | copy-start | bytes 10616836
  8.4 11.4 %copy-start.8 = (bf16[2,12,6336]{2,0,1:T(2,128)(2,1)S(1)}, bf16[2,12,6336]{2,0,1:T(2,128)(2,1)}, u32[]{:S(2)}) copy-start(bf16[2,12,6336]{2,0,1:T(2,128)(2,1)} %param.26) | copy-start | bytes 912388
  10.6 10.6 %copy-start.1 = (bf16[768,2304]{1,0:T(8,128)(2,1)S(1)}, bf16[768,2304]{1,0:T(8,128)(2,1)}, u32[]{:S(2)}) copy-start(bf16[768,2304]{1,0:T(8,128)(2,1)} %weight_qkv.4) | copy-start | bytes 10616836
  10.6 10.6 %copy-start.3 = (bf16[768,768]{1,0:T(8,128)(2,1)S(1)}, bf16[768,768]{1,0:T(8,128)(2,1)}, u32[]{:S(2)}) copy-start(bf16[768,768]{1,0:T(8,128)(2,1)} %weight_proj.6) | copy-start | bytes 3538948
  10.6 12.0 %collective-permute-start.1 = (bf16[72,768]{1,0:T(8,128)(2,1)S(1)}, bf16[72,768]{1,0:T(8,128)(2,1)S(1)}, u32[]{:S(2)}, u32[]{:S(2)}) collective-permute-start(bf16[72,768]{1,0:T(8,128)(2,1)S(1)} %get-tuple-element.32), channel_id=1, source_target_pairs={{0,129},{1,0},{2,131},{3,2},{4,133},{5,4},{6,135},{7,6},{8,137},{9... | collective-permute-start | bytes 331784 | tf_op jit(solution)/shard_map/ppermute | solution.py:382
  11.0 11.5 %collective-permute-start.2 = (bf16[72,768]{1,0:T(8,128)(2,1)S(1)}, bf16[72,768]{1,0:T(8,128)(2,1)S(1)}, u32[]{:S(2)}, u32[]{:S(2)}) collective-permute-start(bf16[72,768]{1,0:T(8,128)(2,1)S(1)} %get-tuple-element.33), channel_id=1, source_target_pairs={{0,2},{1,127},{2,4},{3,1},{4,6},{5,3},{6,8},{7,5},{8,10},{9,7},{10... | collective-permute-start | bytes 331784 | tf_op jit(solution)/shard_map/ppermute | solution.py:382
  19.8 5.1 %collective-permute-start.3 = (bf16[72,768]{1,0:T(8,128)(2,1)S(1)}, bf16[72,768]{1,0:T(8,128)(2,1)S(1)}, u32[]{:S(2)}, u32[]{:S(2)}) collective-permute-start(bf16[72,768]{1,0:T(8,128)(2,1)S(1)} %get-tuple-element.34), channel_id=1, source_target_pairs={{0,255},{1,2},{2,129},{3,4},{4,131},{5,6},{6,133},{7,8},{8,135},{9... | collective-permute-start | bytes 331784 | tf_op jit(solution)/shard_map/ppermute | solution.py:382
  21.2 3.6 %copy-start.5 = (f32[768]{0:T(1024)S(1)}, f32[768]{0:T(1024)}, u32[]{:S(2)}) copy-start(f32[768]{0:T(1024)} %gain.4) | copy-start | bytes 9220
  29.2 7.6 %collective-permute-start.4 = (bf16[72,768]{1,0:T(8,128)(2,1)S(1)}, bf16[72,768]{1,0:T(8,128)(2,1)S(1)}, u32[]{:S(2)}, u32[]{:S(2)}) collective-permute-start(bf16[72,768]{1,0:T(8,128)(2,1)S(1)} %get-tuple-element.41), channel_id=1, source_target_pairs={{255,0},{2,1},{129,2},{4,3},{131,4},{6,5},{133,6},{8,7},{135,8},{1... | collective-permute-start | bytes 331784 | tf_op jit(solution)/shard_map/ppermute | solution.py:382
  29.7 9.6 %collective-permute-start.5 = (bf16[72,768]{1,0:T(8,128)(2,1)S(1)}, bf16[72,768]{1,0:T(8,128)(2,1)S(1)}, u32[]{:S(2)}, u32[]{:S(2)}) collective-permute-start(bf16[72,768]{1,0:T(8,128)(2,1)S(1)} %get-tuple-element.42), channel_id=1, source_target_pairs={{2,0},{127,1},{4,2},{1,3},{6,4},{3,5},{8,6},{5,7},{10,8},{7,9},{12... | collective-permute-start | bytes 331784 | tf_op jit(solution)/shard_map/ppermute | solution.py:382
  29.7 9.6 %collective-permute-start.6 = (bf16[72,768]{1,0:T(8,128)(2,1)S(1)}, bf16[72,768]{1,0:T(8,128)(2,1)S(1)}, u32[]{:S(2)}, u32[]{:S(2)}) collective-permute-start(bf16[72,768]{1,0:T(8,128)(2,1)S(1)} %get-tuple-element.43), channel_id=1, source_target_pairs={{129,0},{0,1},{131,2},{2,3},{133,4},{4,5},{135,6},{6,7},{137,8},{8... | collective-permute-start | bytes 331784 | tf_op jit(solution)/shard_map/ppermute | solution.py:382
  42.0 1.6 %collective-permute-start.7 = (bf16[144,768]{1,0:T(8,128)(2,1)S(1)}, bf16[144,768]{1,0:T(8,128)(2,1)S(1)}, u32[]{:S(2)}, u32[]{:S(2)}) collective-permute-start(bf16[144,768]{1,0:T(8,128)(2,1)S(1)} %get-tuple-element.51), channel_id=1, source_target_pairs={{0,1},{1,0},{2,3},{3,2},{4,5},{5,4},{6,7},{7,6},{8,9},{9,8},{10,11... | collective-permute-start | bytes 663560 | tf_op jit(solution)/shard_map/ppermute | solution.py:449

commit v5 on v4

--- a/solution.py
+++ b/solution.py
@@ -206,18 +206,20 @@
 
 def attend_back(qkv, probs, grad_mixed, grad_qkv):
     masks = four_masks(DEPTH ** (-0.5))
+    ones = four_masks(1.0)
     low = iota((TOKENS, 2 * DEPTH), 1) < DEPTH
     for group in range(HEADS // 4):
         first = group * 4 * DEPTH
         v4 = qkv[:, 2 * D + first : 2 * D + first + 256]
         g4 = grad_mixed[:, first : first + 256]
         all_dp = dot_t(jnp.concatenate([v4 * mask for mask in masks], axis=0), g4)
+        k4 = qkv[:, D + first : D + first + 256]
+        slopes = []
         for half in range(2):
             at = first + 128 * half
             q2 = qkv[:, at : at + 128]
-            k2 = qkv[:, D + at : D + at + 128]
             g2 = grad_mixed[:, at : at + 128]
-            ps, ds, ds_t = [], [], []
+            ps, ds = [], []
             for side in range(2):
                 n = 2 * half + side
                 p = probs[group * 4 + n]
@@ -227,12 +229,16 @@
                 d = (wide * (dp - inner)).astype(bf16)
                 ps.append(p)
                 ds.append(d)
-                ds_t.append(d.T)
-            for block, (lhs, rhs) in enumerate(((ds_t, k2), (ds, q2), (ps, g2))):
+            for block, (lhs, rhs) in enumerate(((ds, q2), (ps, g2))):
                 both = dot(jnp.concatenate(lhs, axis=0), rhs)
-                grad_qkv[:, block * D + at : block * D + at + 128] = jnp.where(
+                grad_qkv[:, (block + 1) * D + at : (block + 1) * D + at + 128] = jnp.where(
                     low, both[:TOKENS], both[TOKENS:]
                 ).astype(bf16)
+            slopes += ds
+        keys = jnp.concatenate([k4 * mask for mask in ones], axis=0)
+        grad_qkv[:, first : first + 256] = dot(
+            jnp.concatenate(slopes, axis=0).T, keys
+        ).astype(bf16)
 
 
 def norm_back(dh, gain, normed, inverse):

time: 44.7 us -> 44.6 us (level)
  no operation moved by 1% of the time
where the time goes in v5:
time: 44.6 us; the launch traced here: 44.5 us
  starting transfers between devices  19.3 us (43%)
  Pallas kernels  17.7 us (40%)
  waiting for transfers between devices  5.89 us (13%)
  between operations  0.85 us (2%)
  local copies, waits for them, and re-layouts  0.72 us (2%)
    pallas_call x9, Pallas kernels, call(): pl.pallas_call(kernel, out_shape=outs, scratch_shapes=scratch, compiler_p...  17.7 us
    ppermute x6, starting transfers between devices, exchanged(): lax.ppermute(value, ('lat', 'lon'), exchange(number, back))  15.5 us
    ppermute x6, waiting for transfers between devices, exchanged(): lax.ppermute(value, ('lat', 'lon'), exchange(number, back))  4.78 us
    ppermute x2, starting transfers between devices, body(): received = lax.ppermute(send, 'lon', swap)  3.86 us
    ppermute x2, waiting for transfers between devices, body(): received = lax.ppermute(send, 'lon', swap)  1.11 us
  transfers between devices with their start and end apart: 8, of which 3 were waited for; matrix products, arithmetic and copies ran while one was open for 1% of the time, Pallas kernels for 12%

profile of v5, /device:TPU:1, one launch (start us, length us, event | category | flops | bytes accessed | tf_op | source)
XLA Modules:
  0.0 44.5 jit_solution(18222137449308240223)
XLA Ops:
  0.6 0.0 copy-start
  0.6 2.4 %shard_map.149 = (bf16[144,768]{1,0:T(8,128)(2,1)}, bf16[144,768]{1,0:T(8,128)(2,1)}) custom-call(bf16[144,768]{1,0:T(8,128)(2,1)} %bitcast.20, s32[3,24]{1,0:T(4,128)} %bitcast.22, s32[3,24]{1,0:T(4,128)} %bitcast.23, f32[768]{0:T(1024)} %vector_at.1, f32[8,768]{1,0:T(8,128)} %table_at.1, bf16[144,768]{1,0:T(8,128)(2,1)} %bitcast.21), custom_call_target="tpu_custom_call" | custom-call | flops 3000000000 | bytes 9000000 | tf_op jit(solution)/shard_map/pallas_call | solution.py:356
  3.0 0.0 copy-start.4
  3.0 0.0 copy-start.6
  3.0 0.0 copy-start.7
  3.1 3.3 %collective-permute-start = (bf16[144,768]{1,0:T(8,128)(2,1)}, bf16[144,768]{1,0:T(8,128)(2,1)S(1)}, u32[]{:S(2)}, u32[]{:S(2)}) collective-permute-start(bf16[144,768]{1,0:T(8,128)(2,1)} %get-tuple-element.29), channel_id=1, source_target_pairs={{0,1},{1,0},{2,3},{3,2},{4,5},{5,4},{6,7},{7,6},{8,9},{9,8},{10,11... | collective-permute-start | bytes 663560 | tf_op jit(solution)/shard_map/ppermute | solution.py:422
  6.4 0.0 copy-done
  6.4 0.0 copy-start.2
  6.4 0.3 constant_dynamic-slice_fusion
  6.8 1.3 %shard_map.150.bias = bf16[12,144,144]{2,1,0:T(8,128)(2,1)S(1)} custom-call(bf16[12,6336]{1,0:T(8,128)(2,1)S(1)} %bitcast.19), custom_call_target="tpu_custom_call" | custom-call | flops 1500000000 | bytes 4500000 | tf_op jit(solution)/shard_map/pallas_call | solution.py:356
  8.1 0.0 collective-permute-done.received
  8.1 0.0 copy-done.4
  8.1 0.0 copy-done.6
  8.1 0.0 copy-done.7
  8.1 0.2 copy-done.2
  8.4 0.0 copy-start.8
  8.4 2.2 %shard_map.151 = (bf16[72,768]{1,0:T(8,128)(2,1)S(1)}, bf16[72,768]{1,0:T(8,128)(2,1)S(1)}, bf16[72,768]{1,0:T(8,128)(2,1)S(1)}, bf16[72,768]{1,0:T(8,128)(2,1)S...) custom-call(bf16[144,768]{1,0:T(8,128)(2,1)S(1)} %copy-done.7, ...), custom_call_target="tpu_custom_call" | custom-call | flops 3000000000 | bytes 9000000 | tf_op jit(solution)/shard_map/pallas_call | solution.py:356
  10.6 0.0 copy-start.1
  10.6 0.0 copy-start.3
  10.6 0.4 collective-permute-start.1
  11.0 8.7 %collective-permute-start.2 = (bf16[72,768]{1,0:T(8,128)(2,1)S(1)}, bf16[72,768]{1,0:T(8,128)(2,1)S(1)}, u32[]{:S(2)}, u32[]{:S(2)}) collective-permute-start(bf16[72,768]{1,0:T(8,128)(2,1)S(1)} %get-tuple-element.33), channel_id=1, source_target_pairs={{0,2},{1,127},{2,4},{3,1},{4,6},{5,3},{6,8},{7,5},{8,10},{9,7},{10... | collective-permute-start | bytes 331784 | tf_op jit(solution)/shard_map/ppermute | solution.py:388
  19.8 0.0 collective-permute-start.3
  19.8 0.0 copy-done.8
  19.9 1.3 %shard_map.153.bias = bf16[12,144,144]{2,1,0:T(8,128)(2,1)S(1)} custom-call(bf16[12,6336]{1,0:T(8,128)(2,1)S(1)} %dynamic-slice_bitcast_fusion.table), custom_call_target="tpu_custom_call" | custom-call | flops 1500000000 | bytes 4500000 | tf_op jit(solution)/shard_map/pallas_call | solution.py:356
  21.2 0.0 copy-done.1
  21.2 0.0 copy-done.3
  21.2 0.0 copy-start.5
  21.2 1.3 %shard_map.152 = (bf16[2304,768]{1,0:T(8,128)(2,1)S(1)}, bf16[768,768]{1,0:T(8,128)(2,1)S(1)}) custom-call(bf16[768,2304]{1,0:T(8,128)(2,1)S(1)} %copy-done.1, bf16[768,768]{1,0:T(8,128)(2,1)S(1)} %copy-done.3), custom_call_target="tpu_custom_call" | custom-call | flops 1500000000 | bytes 4500000 | tf_op jit(solution)/shard_map/pallas_call | solution.py:356
  22.5 0.0 collective-permute-done.1.first
  22.6 0.0 collective-permute-done.2.second
  22.6 2.3 %collective-permute-done.3.third = bf16[72,768]{1,0:T(8,128)(2,1)S(1)} collective-permute-done((bf16[72,768]{1,0:T(8,128)(2,1)S(1)}, bf16[72,768]{1,0:T(8,128)(2,1)S(1)}, u32[]{:S(2)}, u32[]{:S(2)}) %collective-permute-start.3) | collective-permute-done | bytes 110624 | tf_op jit(solution)/shard_map/ppermute | solution.py:388
  24.9 0.0 copy-done.5
  24.9 4.5 %shard_map.154 = (bf16[72,768]{1,0:T(8,128)(2,1)S(1)}, bf16[72,768]{1,0:T(8,128)(2,1)S(1)}, bf16[72,768]{1,0:T(8,128)(2,1)S(1)}, bf16[72,768]{1,0:T(8,128)(2,1)S(1)}) custom-call(bf16[72,768]{1,0:T(8,128)(2,1)S(1)} %get-tuple-element.31.stay, bf16[72,768]{1,0:T(8,128)(2,1)S(1)} %collective-permute-done.1.first, ...), custom_call_target="tpu_custom_call" | custom-call | flops 8000000000 | bytes 24000000 | tf_op jit(solution)/shard_map/pallas_call | solution.py:356
  29.3 0.5 %collective-permute-start.4 = (bf16[72,768]{1,0:T(8,128)(2,1)S(1)}, bf16[72,768]{1,0:T(8,128)(2,1)S(1)}, u32[]{:S(2)}, u32[]{:S(2)}) collective-permute-start(bf16[72,768]{1,0:T(8,128)(2,1)S(1)} %get-tuple-element.41), channel_id=1, source_target_pairs={{255,0},{2,1},{129,2},{4,3},{131,4},{6,5},{133,6},{8,7},{135,8},{1... | collective-permute-start | bytes 331784 | tf_op jit(solution)/shard_map/ppermute | solution.py:388
  29.8 0.0 collective-permute-start.5
  29.8 5.8 %collective-permute-start.6 = (bf16[72,768]{1,0:T(8,128)(2,1)S(1)}, bf16[72,768]{1,0:T(8,128)(2,1)S(1)}, u32[]{:S(2)}, u32[]{:S(2)}) collective-permute-start(bf16[72,768]{1,0:T(8,128)(2,1)S(1)} %get-tuple-element.43), channel_id=1, source_target_pairs={{129,0},{0,1},{131,2},{2,3},{133,4},{4,5},{135,6},{6,7},{137,8},{8... | collective-permute-start | bytes 331784 | tf_op jit(solution)/shard_map/ppermute | solution.py:388
  35.6 1.3 %shard_map.155 = (bf16[2304,768]{1,0:T(8,128)(2,1)S(1)}, bf16[768,768]{1,0:T(8,128)(2,1)S(1)}) custom-call(bf16[768,2304]{1,0:T(8,128)(2,1)S(1)} %copy-done.2, bf16[768,768]{1,0:T(8,128)(2,1)S(1)} %copy-done.4), custom_call_target="tpu_custom_call" | custom-call | flops 1500000000 | bytes 4500000 | tf_op jit(solution)/shard_map/pallas_call | solution.py:356
  36.9 0.0 collective-permute-done.4.first
  36.9 2.5 %collective-permute-done.5.second = bf16[72,768]{1,0:T(8,128)(2,1)S(1)} collective-permute-done((bf16[72,768]{1,0:T(8,128)(2,1)S(1)}, bf16[72,768]{1,0:T(8,128)(2,1)S(1)}, u32[]{:S(2)}, u32[]{:S(2)}) %collective-permute-start.5) | collective-permute-done | bytes 110624 | tf_op jit(solution)/shard_map/ppermute | solution.py:388
  39.4 0.0 collective-permute-done.6.third
  39.4 2.5 %shard_map.156 = (bf16[144,768]{1,0:T(8,128)(2,1)S(1)}, bf16[144,768]{1,0:T(8,128)(2,1)S(1)}) custom-call(bf16[72,768]{1,0:T(8,128)(2,1)S(1)} %get-tuple-element.40.stay, bf16[72,768]{1,0:T(8,128)(2,1)S(1)} %collective-permute-done.4.first, bf16[72,768]{1,0:T(8,128)(2,1)S(1)} %collective-permute-done.5.second, ...), custom_call_target="tpu_custom_call" | custom-call | flops 6000000000 | bytes 18000000 | tf_op jit(solution)/shard_map/pallas_call | solution.py:356
  41.9 0.5 %collective-permute-start.7 = (bf16[144,768]{1,0:T(8,128)(2,1)S(1)}, bf16[144,768]{1,0:T(8,128)(2,1)S(1)}, u32[]{:S(2)}, u32[]{:S(2)}) collective-permute-start(bf16[144,768]{1,0:T(8,128)(2,1)S(1)} %get-tuple-element.51), channel_id=1, source_target_pairs={{0,1},{1,0},{2,3},{3,2},{4,5},{5,4},{6,7},{7,6},{8,9},{9,8},{10,11... | collective-permute-start | bytes 663560 | tf_op jit(solution)/shard_map/ppermute | solution.py:455
  42.4 1.1 %collective-permute-done.7.received = bf16[144,768]{1,0:T(8,128)(2,1)S(1)} collective-permute-done((bf16[144,768]{1,0:T(8,128)(2,1)S(1)}, bf16[144,768]{1,0:T(8,128)(2,1)S(1)}, u32[]{:S(2)}, u32[]{:S(2)}) %collective-permute-start.7) | collective-permute-done | bytes 221216 | tf_op jit(solution)/shard_map/ppermute | solution.py:455
  43.5 1.0 %shard_map.157 = (bf16[144,768]{1,0:T(8,128)(2,1)}, bf16[144,768]{1,0:T(8,128)(2,1)}) custom-call(bf16[144,768]{1,0:T(8,128)(2,1)S(1)} %get-tuple-element.50.keep, bf16[144,768]{1,0:T(8,128)(2,1)S(1)} %collective-permute-done.7.received), custom_call_target="tpu_custom_call" | custom-call | flops 1000000000 | bytes 3000000 | tf_op jit(solution)/shard_map/pallas_call | solution.py:356
  (3 shorter events, 0.1 us)
Async XLA Ops:
  0.6 5.8 %copy-start = (bf16[2,12,6336]{2,0,1:T(2,128)(2,1)S(1)}, bf16[2,12,6336]{2,0,1:T(2,128)(2,1)}, u32[]{:S(2)}) copy-start(bf16[2,12,6336]{2,0,1:T(2,128)(2,1)} %param.22) | copy-start | bytes 912388
  3.0 5.1 %copy-start.4 = (bf16[768,768]{1,0:T(8,128)(2,1)S(1)}, bf16[768,768]{1,0:T(8,128)(2,1)}, u32[]{:S(2)}) copy-start(bf16[768,768]{1,0:T(8,128)(2,1)} %weight_proj.7) | copy-start | bytes 3538948
  3.0 5.1 %copy-start.6 = (f32[768]{0:T(1024)S(1)}, f32[768]{0:T(1024)}, u32[]{:S(2)}) copy-start(f32[768]{0:T(1024)} %gain.5) | copy-start | bytes 9220
  3.0 5.1 %copy-start.7 = (bf16[144,768]{1,0:T(8,128)(2,1)S(1)}, bf16[144,768]{1,0:T(8,128)(2,1)}, u32[]{:S(2)}) copy-start(bf16[144,768]{1,0:T(8,128)(2,1)} %get-tuple-element.28.keep) | copy-start | bytes 663556
  3.1 5.0 %collective-permute-start = (bf16[144,768]{1,0:T(8,128)(2,1)}, bf16[144,768]{1,0:T(8,128)(2,1)S(1)}, u32[]{:S(2)}, u32[]{:S(2)}) collective-permute-start(bf16[144,768]{1,0:T(8,128)(2,1)} %get-tuple-element.29), channel_id=1, source_target_pairs={{0,1},{1,0},{2,3},{3,2},{4,5},{5,4},{6,7},{7,6},{8,9},{9,8},{10,11... | collective-permute-start | bytes 663560 | tf_op jit(solution)/shard_map/ppermute | solution.py:422
  6.4 2.0 %copy-start.2 = (bf16[768,2304]{1,0:T(8,128)(2,1)S(1)}, bf16[768,2304]{1,0:T(8,128)(2,1)}, u32[]{:S(2)}) copy-start(bf16[768,2304]{1,0:T(8,128)(2,1)} %weight_qkv.5) | copy-start | bytes 10616836
  8.4 11.4 %copy-start.8 = (bf16[2,12,6336]{2,0,1:T(2,128)(2,1)S(1)}, bf16[2,12,6336]{2,0,1:T(2,128)(2,1)}, u32[]{:S(2)}) copy-start(bf16[2,12,6336]{2,0,1:T(2,128)(2,1)} %param.26) | copy-start | bytes 912388
  10.6 10.6 %copy-start.1 = (bf16[768,2304]{1,0:T(8,128)(2,1)S(1)}, bf16[768,2304]{1,0:T(8,128)(2,1)}, u32[]{:S(2)}) copy-start(bf16[768,2304]{1,0:T(8,128)(2,1)} %weight_qkv.4) | copy-start | bytes 10616836
  10.6 10.6 %copy-start.3 = (bf16[768,768]{1,0:T(8,128)(2,1)S(1)}, bf16[768,768]{1,0:T(8,128)(2,1)}, u32[]{:S(2)}) copy-start(bf16[768,768]{1,0:T(8,128)(2,1)} %weight_proj.6) | copy-start | bytes 3538948
  10.6 12.0 %collective-permute-start.1 = (bf16[72,768]{1,0:T(8,128)(2,1)S(1)}, bf16[72,768]{1,0:T(8,128)(2,1)S(1)}, u32[]{:S(2)}, u32[]{:S(2)}) collective-permute-start(bf16[72,768]{1,0:T(8,128)(2,1)S(1)} %get-tuple-element.32), channel_id=1, source_target_pairs={{0,129},{1,0},{2,131},{3,2},{4,133},{5,4},{6,135},{7,6},{8,137},{9... | collective-permute-start | bytes 331784 | tf_op jit(solution)/shard_map/ppermute | solution.py:388
  11.0 11.5 %collective-permute-start.2 = (bf16[72,768]{1,0:T(8,128)(2,1)S(1)}, bf16[72,768]{1,0:T(8,128)(2,1)S(1)}, u32[]{:S(2)}, u32[]{:S(2)}) collective-permute-start(bf16[72,768]{1,0:T(8,128)(2,1)S(1)} %get-tuple-element.33), channel_id=1, source_target_pairs={{0,2},{1,127},{2,4},{3,1},{4,6},{5,3},{6,8},{7,5},{8,10},{9,7},{10... | collective-permute-start | bytes 331784 | tf_op jit(solution)/shard_map/ppermute | solution.py:388
  19.8 5.1 %collective-permute-start.3 = (bf16[72,768]{1,0:T(8,128)(2,1)S(1)}, bf16[72,768]{1,0:T(8,128)(2,1)S(1)}, u32[]{:S(2)}, u32[]{:S(2)}) collective-permute-start(bf16[72,768]{1,0:T(8,128)(2,1)S(1)} %get-tuple-element.34), channel_id=1, source_target_pairs={{0,255},{1,2},{2,129},{3,4},{4,131},{5,6},{6,133},{7,8},{8,135},{9... | collective-permute-start | bytes 331784 | tf_op jit(solution)/shard_map/ppermute | solution.py:388
  21.2 3.6 %copy-start.5 = (f32[768]{0:T(1024)S(1)}, f32[768]{0:T(1024)}, u32[]{:S(2)}) copy-start(f32[768]{0:T(1024)} %gain.4) | copy-start | bytes 9220
  29.3 7.6 %collective-permute-start.4 = (bf16[72,768]{1,0:T(8,128)(2,1)S(1)}, bf16[72,768]{1,0:T(8,128)(2,1)S(1)}, u32[]{:S(2)}, u32[]{:S(2)}) collective-permute-start(bf16[72,768]{1,0:T(8,128)(2,1)S(1)} %get-tuple-element.41), channel_id=1, source_target_pairs={{255,0},{2,1},{129,2},{4,3},{131,4},{6,5},{133,6},{8,7},{135,8},{1... | collective-permute-start | bytes 331784 | tf_op jit(solution)/shard_map/ppermute | solution.py:388
  29.8 9.6 %collective-permute-start.5 = (bf16[72,768]{1,0:T(8,128)(2,1)S(1)}, bf16[72,768]{1,0:T(8,128)(2,1)S(1)}, u32[]{:S(2)}, u32[]{:S(2)}) collective-permute-start(bf16[72,768]{1,0:T(8,128)(2,1)S(1)} %get-tuple-element.42), channel_id=1, source_target_pairs={{2,0},{127,1},{4,2},{1,3},{6,4},{3,5},{8,6},{5,7},{10,8},{7,9},{12... | collective-permute-start | bytes 331784 | tf_op jit(solution)/shard_map/ppermute | solution.py:388
  29.8 9.6 %collective-permute-start.6 = (bf16[72,768]{1,0:T(8,128)(2,1)S(1)}, bf16[72,768]{1,0:T(8,128)(2,1)S(1)}, u32[]{:S(2)}, u32[]{:S(2)}) collective-permute-start(bf16[72,768]{1,0:T(8,128)(2,1)S(1)} %get-tuple-element.43), channel_id=1, source_target_pairs={{129,0},{0,1},{131,2},{2,3},{133,4},{4,5},{135,6},{6,7},{137,8},{8... | collective-permute-start | bytes 331784 | tf_op jit(solution)/shard_map/ppermute | solution.py:388
  41.9 1.6 %collective-permute-start.7 = (bf16[144,768]{1,0:T(8,128)(2,1)S(1)}, bf16[144,768]{1,0:T(8,128)(2,1)S(1)}, u32[]{:S(2)}, u32[]{:S(2)}) collective-permute-start(bf16[144,768]{1,0:T(8,128)(2,1)S(1)} %get-tuple-element.51), channel_id=1, source_target_pairs={{0,1},{1,0},{2,3},{3,2},{4,5},{5,4},{6,7},{7,6},{8,9},{9,8},{10,11... | collective-permute-start | bytes 663560 | tf_op jit(solution)/shard_map/ppermute | solution.py:455

commit v6 on v5

--- a/solution.py
+++ b/solution.py
@@ -206,6 +206,37 @@
 
 def attend_back(qkv, probs, grad_mixed, grad_qkv):
     masks = four_masks(DEPTH ** (-0.5))
+    low = iota((TOKENS, 2 * DEPTH), 1) < DEPTH
+    for group in range(HEADS // 4):
+        first = group * 4 * DEPTH
+        v4 = qkv[:, 2 * D + first : 2 * D + first + 256]
+        g4 = grad_mixed[:, first : first + 256]
+        all_dp = dot_t(jnp.concatenate([v4 * mask for mask in masks], axis=0), g4)
+        for half in range(2):
+            at = first + 128 * half
+            q2 = qkv[:, at : at + 128]
+            k2 = qkv[:, D + at : D + at + 128]
+            g2 = grad_mixed[:, at : at + 128]
+            ps, ds, ds_t = [], [], []
+            for side in range(2):
+                n = 2 * half + side
+                p = probs[group * 4 + n]
+                wide = p.astype(f32)
+                dp = all_dp[n * TOKENS : n * TOKENS + TOKENS]
+                inner = jnp.sum(wide * dp, axis=0, keepdims=True)
+                d = (wide * (dp - inner)).astype(bf16)
+                ps.append(p)
+                ds.append(d)
+                ds_t.append(d.T)
+            for block, (lhs, rhs) in enumerate(((ds_t, k2), (ds, q2), (ps, g2))):
+                both = dot(jnp.concatenate(lhs, axis=0), rhs)
+                grad_qkv[:, block * D + at : block * D + at + 128] = jnp.where(
+                    low, both[:TOKENS], both[TOKENS:]
+                ).astype(bf16)
+
+
+def attend_back_stacked(qkv, probs, grad_mixed, grad_qkv):
+    masks = four_masks(DEPTH ** (-0.5))
     ones = four_masks(1.0)
     low = iota((TOKENS, 2 * DEPTH), 1) < DEPTH
     for group in range(HEADS // 4):
@@ -333,7 +364,7 @@
     g, turned = gather(ordered(QUARTERS_ONE, BACK), c, (stay, first, second, third))
     normed, inverse = norm(u[...].astype(f32))
     grad_mixed[...] = dot(g.astype(bf16), weight_proj_t[...]).astype(bf16)
-    attend_back(qkv, probs, grad_mixed, grad_qkv)
+    attend_back_stacked(qkv, probs, grad_mixed, grad_qkv)
     dh = dot(grad_qkv[...], weight_qkv_t[...])
     du = g + norm_back(dh, row(gain), normed, inverse)
     mine = c == 0

time: 44.6 us -> 44.6 us (level)
  no operation moved by 1% of the time
where the time goes in v6:
time: 44.6 us; the launch traced here: 44.4 us
  starting transfers between devices  19.3 us (43%)
  Pallas kernels  17.6 us (39%)
  waiting for transfers between devices  5.89 us (13%)
  between operations  0.85 us (2%)
  local copies, waits for them, and re-layouts  0.72 us (2%)
    pallas_call x9, Pallas kernels, call(): pl.pallas_call(kernel, out_shape=outs, scratch_shapes=scratch, compiler_p...  17.6 us
    ppermute x6, starting transfers between devices, exchanged(): lax.ppermute(value, ('lat', 'lon'), exchange(number, back))  15.5 us
    ppermute x6, waiting for transfers between devices, exchanged(): lax.ppermute(value, ('lat', 'lon'), exchange(number, back))  4.78 us
    ppermute x2, starting transfers between devices, body(): received = lax.ppermute(send, 'lon', swap)  3.86 us
    ppermute x2, waiting for transfers between devices, body(): received = lax.ppermute(send, 'lon', swap)  1.11 us
  transfers between devices with their start and end apart: 8, of which 3 were waited for; matrix products, arithmetic and copies ran while one was open for 1% of the time, Pallas kernels for 12%

profile of v6, /device:TPU:1, one launch (start us, length us, event | category | flops | bytes accessed | tf_op | source)
XLA Modules:
  0.0 44.4 jit_solution(14248559441565002573)
XLA Ops:
  0.6 0.0 copy-start
  0.6 2.4 %shard_map.149 = (bf16[144,768]{1,0:T(8,128)(2,1)}, bf16[144,768]{1,0:T(8,128)(2,1)}) custom-call(bf16[144,768]{1,0:T(8,128)(2,1)} %bitcast.20, s32[3,24]{1,0:T(4,128)} %bitcast.22, s32[3,24]{1,0:T(4,128)} %bitcast.23, f32[768]{0:T(1024)} %vector_at.1, f32[8,768]{1,0:T(8,128)} %table_at.1, bf16[144,768]{1,0:T(8,128)(2,1)} %bitcast.21), custom_call_target="tpu_custom_call" | custom-call | flops 3000000000 | bytes 9000000 | tf_op jit(solution)/shard_map/pallas_call | solution.py:387
  3.0 0.0 copy-start.4
  3.0 0.0 copy-start.6
  3.0 0.0 copy-start.7
  3.1 3.3 %collective-permute-start = (bf16[144,768]{1,0:T(8,128)(2,1)}, bf16[144,768]{1,0:T(8,128)(2,1)S(1)}, u32[]{:S(2)}, u32[]{:S(2)}) collective-permute-start(bf16[144,768]{1,0:T(8,128)(2,1)} %get-tuple-element.29), channel_id=1, source_target_pairs={{0,1},{1,0},{2,3},{3,2},{4,5},{5,4},{6,7},{7,6},{8,9},{9,8},{10,11... | collective-permute-start | bytes 663560 | tf_op jit(solution)/shard_map/ppermute | solution.py:453
  6.4 0.0 copy-done
  6.4 0.0 copy-start.2
  6.4 0.3 constant_dynamic-slice_fusion
  6.8 1.3 %shard_map.150.bias = bf16[12,144,144]{2,1,0:T(8,128)(2,1)S(1)} custom-call(bf16[12,6336]{1,0:T(8,128)(2,1)S(1)} %bitcast.19), custom_call_target="tpu_custom_call" | custom-call | flops 1500000000 | bytes 4500000 | tf_op jit(solution)/shard_map/pallas_call | solution.py:387
  8.1 0.0 collective-permute-done.received
  8.1 0.0 copy-done.4
  8.1 0.0 copy-done.6
  8.1 0.0 copy-done.7
  8.1 0.2 copy-done.2
  8.4 0.0 copy-start.8
  8.4 2.2 %shard_map.151 = (bf16[72,768]{1,0:T(8,128)(2,1)S(1)}, bf16[72,768]{1,0:T(8,128)(2,1)S(1)}, bf16[72,768]{1,0:T(8,128)(2,1)S(1)}, bf16[72,768]{1,0:T(8,128)(2,1)S...) custom-call(bf16[144,768]{1,0:T(8,128)(2,1)S(1)} %copy-done.7, ...), custom_call_target="tpu_custom_call" | custom-call | flops 3000000000 | bytes 9000000 | tf_op jit(solution)/shard_map/pallas_call | solution.py:387
  10.6 0.0 copy-start.1
  10.6 0.0 copy-start.3
  10.6 0.4 collective-permute-start.1
  11.0 8.7 %collective-permute-start.2 = (bf16[72,768]{1,0:T(8,128)(2,1)S(1)}, bf16[72,768]{1,0:T(8,128)(2,1)S(1)}, u32[]{:S(2)}, u32[]{:S(2)}) collective-permute-start(bf16[72,768]{1,0:T(8,128)(2,1)S(1)} %get-tuple-element.33), channel_id=1, source_target_pairs={{0,2},{1,127},{2,4},{3,1},{4,6},{5,3},{6,8},{7,5},{8,10},{9,7},{10... | collective-permute-start | bytes 331784 | tf_op jit(solution)/shard_map/ppermute | solution.py:419
  19.8 0.0 collective-permute-start.3
  19.8 0.0 copy-done.8
  19.9 1.3 %shard_map.153.bias = bf16[12,144,144]{2,1,0:T(8,128)(2,1)S(1)} custom-call(bf16[12,6336]{1,0:T(8,128)(2,1)S(1)} %dynamic-slice_bitcast_fusion.table), custom_call_target="tpu_custom_call" | custom-call | flops 1500000000 | bytes 4500000 | tf_op jit(solution)/shard_map/pallas_call | solution.py:387
  21.2 0.0 copy-done.1
  21.2 0.0 copy-done.3
  21.2 0.0 copy-start.5
  21.2 1.3 %shard_map.152 = (bf16[2304,768]{1,0:T(8,128)(2,1)S(1)}, bf16[768,768]{1,0:T(8,128)(2,1)S(1)}) custom-call(bf16[768,2304]{1,0:T(8,128)(2,1)S(1)} %copy-done.1, bf16[768,768]{1,0:T(8,128)(2,1)S(1)} %copy-done.3), custom_call_target="tpu_custom_call" | custom-call | flops 1500000000 | bytes 4500000 | tf_op jit(solution)/shard_map/pallas_call | solution.py:387
  22.5 0.0 collective-permute-done.1.first
  22.6 0.0 collective-permute-done.2.second
  22.6 2.3 %collective-permute-done.3.third = bf16[72,768]{1,0:T(8,128)(2,1)S(1)} collective-permute-done((bf16[72,768]{1,0:T(8,128)(2,1)S(1)}, bf16[72,768]{1,0:T(8,128)(2,1)S(1)}, u32[]{:S(2)}, u32[]{:S(2)}) %collective-permute-start.3) | collective-permute-done | bytes 110624 | tf_op jit(solution)/shard_map/ppermute | solution.py:419
  24.9 0.0 copy-done.5
  24.9 4.4 %shard_map.154 = (bf16[72,768]{1,0:T(8,128)(2,1)S(1)}, bf16[72,768]{1,0:T(8,128)(2,1)S(1)}, bf16[72,768]{1,0:T(8,128)(2,1)S(1)}, bf16[72,768]{1,0:T(8,128)(2,1)S(1)}) custom-call(bf16[72,768]{1,0:T(8,128)(2,1)S(1)} %get-tuple-element.31.stay, bf16[72,768]{1,0:T(8,128)(2,1)S(1)} %collective-permute-done.1.first, ...), custom_call_target="tpu_custom_call" | custom-call | flops 8000000000 | bytes 24000000 | tf_op jit(solution)/shard_map/pallas_call | solution.py:387
  29.2 0.5 %collective-permute-start.4 = (bf16[72,768]{1,0:T(8,128)(2,1)S(1)}, bf16[72,768]{1,0:T(8,128)(2,1)S(1)}, u32[]{:S(2)}, u32[]{:S(2)}) collective-permute-start(bf16[72,768]{1,0:T(8,128)(2,1)S(1)} %get-tuple-element.41), channel_id=1, source_target_pairs={{255,0},{2,1},{129,2},{4,3},{131,4},{6,5},{133,6},{8,7},{135,8},{1... | collective-permute-start | bytes 331784 | tf_op jit(solution)/shard_map/ppermute | solution.py:419
  29.7 0.0 collective-permute-start.5
  29.7 5.8 %collective-permute-start.6 = (bf16[72,768]{1,0:T(8,128)(2,1)S(1)}, bf16[72,768]{1,0:T(8,128)(2,1)S(1)}, u32[]{:S(2)}, u32[]{:S(2)}) collective-permute-start(bf16[72,768]{1,0:T(8,128)(2,1)S(1)} %get-tuple-element.43), channel_id=1, source_target_pairs={{129,0},{0,1},{131,2},{2,3},{133,4},{4,5},{135,6},{6,7},{137,8},{8... | collective-permute-start | bytes 331784 | tf_op jit(solution)/shard_map/ppermute | solution.py:419
  35.5 1.3 %shard_map.155 = (bf16[2304,768]{1,0:T(8,128)(2,1)S(1)}, bf16[768,768]{1,0:T(8,128)(2,1)S(1)}) custom-call(bf16[768,2304]{1,0:T(8,128)(2,1)S(1)} %copy-done.2, bf16[768,768]{1,0:T(8,128)(2,1)S(1)} %copy-done.4), custom_call_target="tpu_custom_call" | custom-call | flops 1500000000 | bytes 4500000 | tf_op jit(solution)/shard_map/pallas_call | solution.py:387
  36.8 0.0 collective-permute-done.4.first
  36.8 2.5 %collective-permute-done.5.second = bf16[72,768]{1,0:T(8,128)(2,1)S(1)} collective-permute-done((bf16[72,768]{1,0:T(8,128)(2,1)S(1)}, bf16[72,768]{1,0:T(8,128)(2,1)S(1)}, u32[]{:S(2)}, u32[]{:S(2)}) %collective-permute-start.5) | collective-permute-done | bytes 110624 | tf_op jit(solution)/shard_map/ppermute | solution.py:419
  39.3 0.0 collective-permute-done.6.third
  39.3 2.5 %shard_map.156 = (bf16[144,768]{1,0:T(8,128)(2,1)S(1)}, bf16[144,768]{1,0:T(8,128)(2,1)S(1)}) custom-call(bf16[72,768]{1,0:T(8,128)(2,1)S(1)} %get-tuple-element.40.stay, bf16[72,768]{1,0:T(8,128)(2,1)S(1)} %collective-permute-done.4.first, bf16[72,768]{1,0:T(8,128)(2,1)S(1)} %collective-permute-done.5.second, ...), custom_call_target="tpu_custom_call" | custom-call | flops 6000000000 | bytes 18000000 | tf_op jit(solution)/shard_map/pallas_call | solution.py:387
  41.8 0.5 %collective-permute-start.7 = (bf16[144,768]{1,0:T(8,128)(2,1)S(1)}, bf16[144,768]{1,0:T(8,128)(2,1)S(1)}, u32[]{:S(2)}, u32[]{:S(2)}) collective-permute-start(bf16[144,768]{1,0:T(8,128)(2,1)S(1)} %get-tuple-element.51), channel_id=1, source_target_pairs={{0,1},{1,0},{2,3},{3,2},{4,5},{5,4},{6,7},{7,6},{8,9},{9,8},{10,11... | collective-permute-start | bytes 663560 | tf_op jit(solution)/shard_map/ppermute | solution.py:486
  42.3 1.1 %collective-permute-done.7.received = bf16[144,768]{1,0:T(8,128)(2,1)S(1)} collective-permute-done((bf16[144,768]{1,0:T(8,128)(2,1)S(1)}, bf16[144,768]{1,0:T(8,128)(2,1)S(1)}, u32[]{:S(2)}, u32[]{:S(2)}) %collective-permute-start.7) | collective-permute-done | bytes 221216 | tf_op jit(solution)/shard_map/ppermute | solution.py:486
  43.4 1.0 %shard_map.157 = (bf16[144,768]{1,0:T(8,128)(2,1)}, bf16[144,768]{1,0:T(8,128)(2,1)}) custom-call(bf16[144,768]{1,0:T(8,128)(2,1)S(1)} %get-tuple-element.50.keep, bf16[144,768]{1,0:T(8,128)(2,1)S(1)} %collective-permute-done.7.received), custom_call_target="tpu_custom_call" | custom-call | flops 1000000000 | bytes 3000000 | tf_op jit(solution)/shard_map/pallas_call | solution.py:387
  (3 shorter events, 0.1 us)
Async XLA Ops:
  0.6 5.8 %copy-start = (bf16[2,12,6336]{2,0,1:T(2,128)(2,1)S(1)}, bf16[2,12,6336]{2,0,1:T(2,128)(2,1)}, u32[]{:S(2)}) copy-start(bf16[2,12,6336]{2,0,1:T(2,128)(2,1)} %param.22) | copy-start | bytes 912388
  3.0 5.1 %copy-start.4 = (bf16[768,768]{1,0:T(8,128)(2,1)S(1)}, bf16[768,768]{1,0:T(8,128)(2,1)}, u32[]{:S(2)}) copy-start(bf16[768,768]{1,0:T(8,128)(2,1)} %weight_proj.7) | copy-start | bytes 3538948
  3.0 5.1 %copy-start.6 = (f32[768]{0:T(1024)S(1)}, f32[768]{0:T(1024)}, u32[]{:S(2)}) copy-start(f32[768]{0:T(1024)} %gain.5) | copy-start | bytes 9220
  3.0 5.1 %copy-start.7 = (bf16[144,768]{1,0:T(8,128)(2,1)S(1)}, bf16[144,768]{1,0:T(8,128)(2,1)}, u32[]{:S(2)}) copy-start(bf16[144,768]{1,0:T(8,128)(2,1)} %get-tuple-element.28.keep) | copy-start | bytes 663556
  3.1 5.0 %collective-permute-start = (bf16[144,768]{1,0:T(8,128)(2,1)}, bf16[144,768]{1,0:T(8,128)(2,1)S(1)}, u32[]{:S(2)}, u32[]{:S(2)}) collective-permute-start(bf16[144,768]{1,0:T(8,128)(2,1)} %get-tuple-element.29), channel_id=1, source_target_pairs={{0,1},{1,0},{2,3},{3,2},{4,5},{5,4},{6,7},{7,6},{8,9},{9,8},{10,11... | collective-permute-start | bytes 663560 | tf_op jit(solution)/shard_map/ppermute | solution.py:453
  6.4 2.0 %copy-start.2 = (bf16[768,2304]{1,0:T(8,128)(2,1)S(1)}, bf16[768,2304]{1,0:T(8,128)(2,1)}, u32[]{:S(2)}) copy-start(bf16[768,2304]{1,0:T(8,128)(2,1)} %weight_qkv.5) | copy-start | bytes 10616836
  8.4 11.4 %copy-start.8 = (bf16[2,12,6336]{2,0,1:T(2,128)(2,1)S(1)}, bf16[2,12,6336]{2,0,1:T(2,128)(2,1)}, u32[]{:S(2)}) copy-start(bf16[2,12,6336]{2,0,1:T(2,128)(2,1)} %param.26) | copy-start | bytes 912388
  10.6 10.6 %copy-start.1 = (bf16[768,2304]{1,0:T(8,128)(2,1)S(1)}, bf16[768,2304]{1,0:T(8,128)(2,1)}, u32[]{:S(2)}) copy-start(bf16[768,2304]{1,0:T(8,128)(2,1)} %weight_qkv.4) | copy-start | bytes 10616836
  10.6 10.6 %copy-start.3 = (bf16[768,768]{1,0:T(8,128)(2,1)S(1)}, bf16[768,768]{1,0:T(8,128)(2,1)}, u32[]{:S(2)}) copy-start(bf16[768,768]{1,0:T(8,128)(2,1)} %weight_proj.6) | copy-start | bytes 3538948
  10.6 12.0 %collective-permute-start.1 = (bf16[72,768]{1,0:T(8,128)(2,1)S(1)}, bf16[72,768]{1,0:T(8,128)(2,1)S(1)}, u32[]{:S(2)}, u32[]{:S(2)}) collective-permute-start(bf16[72,768]{1,0:T(8,128)(2,1)S(1)} %get-tuple-element.32), channel_id=1, source_target_pairs={{0,129},{1,0},{2,131},{3,2},{4,133},{5,4},{6,135},{7,6},{8,137},{9... | collective-permute-start | bytes 331784 | tf_op jit(solution)/shard_map/ppermute | solution.py:419
  11.0 11.5 %collective-permute-start.2 = (bf16[72,768]{1,0:T(8,128)(2,1)S(1)}, bf16[72,768]{1,0:T(8,128)(2,1)S(1)}, u32[]{:S(2)}, u32[]{:S(2)}) collective-permute-start(bf16[72,768]{1,0:T(8,128)(2,1)S(1)} %get-tuple-element.33), channel_id=1, source_target_pairs={{0,2},{1,127},{2,4},{3,1},{4,6},{5,3},{6,8},{7,5},{8,10},{9,7},{10... | collective-permute-start | bytes 331784 | tf_op jit(solution)/shard_map/ppermute | solution.py:419
  19.8 5.1 %collective-permute-start.3 = (bf16[72,768]{1,0:T(8,128)(2,1)S(1)}, bf16[72,768]{1,0:T(8,128)(2,1)S(1)}, u32[]{:S(2)}, u32[]{:S(2)}) collective-permute-start(bf16[72,768]{1,0:T(8,128)(2,1)S(1)} %get-tuple-element.34), channel_id=1, source_target_pairs={{0,255},{1,2},{2,129},{3,4},{4,131},{5,6},{6,133},{7,8},{8,135},{9... | collective-permute-start | bytes 331784 | tf_op jit(solution)/shard_map/ppermute | solution.py:419
  21.2 3.6 %copy-start.5 = (f32[768]{0:T(1024)S(1)}, f32[768]{0:T(1024)}, u32[]{:S(2)}) copy-start(f32[768]{0:T(1024)} %gain.4) | copy-start | bytes 9220
  29.2 7.6 %collective-permute-start.4 = (bf16[72,768]{1,0:T(8,128)(2,1)S(1)}, bf16[72,768]{1,0:T(8,128)(2,1)S(1)}, u32[]{:S(2)}, u32[]{:S(2)}) collective-permute-start(bf16[72,768]{1,0:T(8,128)(2,1)S(1)} %get-tuple-element.41), channel_id=1, source_target_pairs={{255,0},{2,1},{129,2},{4,3},{131,4},{6,5},{133,6},{8,7},{135,8},{1... | collective-permute-start | bytes 331784 | tf_op jit(solution)/shard_map/ppermute | solution.py:419
  29.7 9.6 %collective-permute-start.5 = (bf16[72,768]{1,0:T(8,128)(2,1)S(1)}, bf16[72,768]{1,0:T(8,128)(2,1)S(1)}, u32[]{:S(2)}, u32[]{:S(2)}) collective-permute-start(bf16[72,768]{1,0:T(8,128)(2,1)S(1)} %get-tuple-element.42), channel_id=1, source_target_pairs={{2,0},{127,1},{4,2},{1,3},{6,4},{3,5},{8,6},{5,7},{10,8},{7,9},{12... | collective-permute-start | bytes 331784 | tf_op jit(solution)/shard_map/ppermute | solution.py:419
  29.7 9.6 %collective-permute-start.6 = (bf16[72,768]{1,0:T(8,128)(2,1)S(1)}, bf16[72,768]{1,0:T(8,128)(2,1)S(1)}, u32[]{:S(2)}, u32[]{:S(2)}) collective-permute-start(bf16[72,768]{1,0:T(8,128)(2,1)S(1)} %get-tuple-element.43), channel_id=1, source_target_pairs={{129,0},{0,1},{131,2},{2,3},{133,4},{4,5},{135,6},{6,7},{137,8},{8... | collective-permute-start | bytes 331784 | tf_op jit(solution)/shard_map/ppermute | solution.py:419
  41.8 1.6 %collective-permute-start.7 = (bf16[144,768]{1,0:T(8,128)(2,1)S(1)}, bf16[144,768]{1,0:T(8,128)(2,1)S(1)}, u32[]{:S(2)}, u32[]{:S(2)}) collective-permute-start(bf16[144,768]{1,0:T(8,128)(2,1)S(1)} %get-tuple-element.51), channel_id=1, source_target_pairs={{0,1},{1,0},{2,3},{3,2},{4,5},{5,4},{6,7},{7,6},{8,9},{9,8},{10,11... | collective-permute-start | bytes 663560 | tf_op jit(solution)/shard_map/ppermute | solution.py:486
